TPU v7x, 1024 devices: a whole 4x4x32 slice. The times are simulated.
1024 devices in a mesh: row: 64 (over x_hi, z), col: 16 (over y, x_lo, core).
Axes of the slice: x: 4 (x_hi: 2, x_lo: 2; x = x_hi * 2 + x_lo), y: 4, z: 32, core: 2. Of those that a mesh axis runs over, the one named last changes fastest.
Arguments:
- features: bfloat16 [131072, 128], P('col'), may hold values from -6 to 6
- source_degree: int32 [131072], P('col'), may hold values from 1 to 31
- tile_coords: int32 [64, 16, 2, 96], P('row', 'col'), may hold values from 0 to 127, as said below
- tile_counts: int32 [64, 16, 96], P('row', 'col'), may hold values from 0 to 96, as said below
- tile_values: bfloat16 [64, 16, 96, 4096], P('row', 'col'), may hold values from 0 to 1.5, as said below
- weight: bfloat16 [128, 128], replicated, may hold values from -0.5 to 0.5
- node_order: int32 [1024, 128], P(('row', 'col')), may hold values from 0 to 127, each once within a row
- cotangent: bfloat16 [131072, 128], P(('row', 'col')), may hold values from -24 to 24
Outputs:
- activations: bfloat16 [131072, 128], P(('row', 'col'))
- weight_grad: float32 [128, 128], replicated
Inputs may be any that keep to these rules, and one draw needn't show every extreme that they name: `tile_coords`: tile rows lie below 32, tile columns below 128; some slot reaches each end. `tile_counts`: within each group of 24 slots of one offset the nonempty slots come first; every group has at least one nonempty and one empty slot. `tile_values`: each tile has exactly as many nonzero entries as its slot's count, each between 0.5 and 1.5.
All inputs are finite; a program needn't handle non-finite values.
Results may differ from a plain program's by a relative error of at most 0.0057.
Values may be sent and summed in bfloat16 or wider, within the bound.
No kernel may reach another device: no remote copies, remote signals or barrier semaphores. Data moves between devices by JAX's collectives and lax.ppermute only.
A program may use at most 64 MiB of HBM per device.

v0:
```python
import jax
import jax.numpy as jnp
from jax import lax
from jax.sharding import PartitionSpec as P

TB = 64


def passed_along(value, axis, steps):
    count = lax.axis_size(axis)
    pairs = [(source, (source + steps) % count) for source in range(count)]
    return lax.ppermute(value, axis, pairs)


def per_device(
    features, source_degree, tile_coords, tile_counts, tile_values, weight, node_order, cotangent
):
    columns = lax.axis_size("col")
    row_count = lax.axis_size("row")
    step_total = min(4, columns)
    coords = tile_coords.reshape(2, -1)
    counts = tile_counts.reshape(-1)
    tile_total = counts.shape[0]
    per_step = tile_total // step_total
    tile_size = TB
    values = tile_values.reshape(tile_total, tile_size, tile_size)
    panel_rows, feat_dim = features.shape
    out_rows = node_order.shape[-1]
    row_panel = out_rows * columns
    row_tiles = row_panel // tile_size
    occupied = (counts > 0).astype(jnp.float32)
    targets = (coords[0][None, :] == jnp.arange(row_tiles)[:, None]).astype(jnp.float32) * occupied[
        None, :
    ]
    scaled = (
        features.astype(jnp.float32) * lax.rsqrt(1.0 + source_degree.astype(jnp.float32))[:, None]
    ).astype(jnp.bfloat16)

    def one_step(offset, current):
        start_slot = offset * per_step
        blocks = current.reshape(-1, tile_size, feat_dim)[
            coords[1, start_slot : start_slot + per_step]
        ]
        products = jnp.einsum(
            "tij,tjf->tif",
            values[start_slot : start_slot + per_step],
            blocks,
            preferred_element_type=jnp.float32,
        )
        return jnp.einsum(
            "rt,tif->rif",
            targets[:, start_slot : start_slot + per_step],
            products,
            precision=lax.Precision.HIGHEST,
        )

    current = scaled
    total = one_step(0, current)
    for offset in range(1, step_total):
        current = passed_along(current, "col", 1)
        total = total + one_step(offset, current)
    row_index = lax.axis_index("row")
    owner = row_index * columns // row_count
    self_start = row_index * row_panel % panel_rows
    self_rows = lax.dynamic_slice_in_dim(scaled, self_start, row_panel, 0).astype(jnp.float32)
    holder = (lax.axis_index("col") == owner).astype(jnp.float32)
    partial_value = total.reshape(row_panel, feat_dim) + holder * self_rows
    row_weights = jnp.sum(values, axis=-1, dtype=jnp.float32)
    degree_tiles = jnp.dot(targets, row_weights, precision=lax.Precision.HIGHEST)
    degree_rows = degree_tiles.reshape(-1)
    sums, degrees = (
        lax.psum_scatter(partial_value, "col", scatter_dimension=0, tiled=True),
        lax.psum_scatter(degree_rows, "col", scatter_dimension=0, tiled=True),
    )
    normed = (sums * lax.rsqrt(1.0 + degrees)[:, None]).astype(jnp.bfloat16)
    act = jnp.maximum(jnp.dot(normed, weight, preferred_element_type=jnp.float32), 0.0).astype(
        jnp.bfloat16
    )
    order = node_order.reshape(-1)
    activations = act[order]
    node_total = out_rows * row_count * columns
    local_grad = jnp.dot(
        normed[order].T, cotangent, preferred_element_type=jnp.float32
    ) * node_total ** (-0.5)
    weight_grad = lax.psum(local_grad, ("row", "col"))
    return (activations, weight_grad)


def solution(mesh):
    in_specs = (
        P("col", None),
        P("col"),
        P("row", "col", None, None),
        P("row", "col", None),
        P("row", "col", None, None),
        P(),
        P(("row", "col"), None),
        P(("row", "col"), None),
    )
    out_specs = (P(("row", "col"), None), P())
    return jax.shard_map(
        per_device, mesh=mesh, in_specs=in_specs, out_specs=out_specs, check_vma=False
    )
```

profile of v0, /device:TPU:1, one launch (start us, length us, event | category | flops | bytes accessed | tf_op | source)
XLA Modules:
  0.0 1050.8 jit_solution(4477511897040043104)
XLA Ops:
  8.0 2.5 multiply_convert_fusion
  10.6 4.5 collective-permute-start
  15.1 23.0 %collective-permute-done = bf16[8192,128]{1,0:T(8,128)(2,1)} collective-permute-done((bf16[8192,128]{1,0:T(8,128)(2,1)S(1)}, bf16[8192,128]{1,0:T(8,128)(2,1)}, u32[]{:S(2)}, u32[]{:S(2)}) %collective-permute-start) | collective-permute-done | bytes 2097184 | tf_op jit(solution)/shard_map/ppermute | solution.py:12
  38.1 4.5 collective-permute-start.1
  43.3 1.3 slice.56
  48.8 17.0 %collective-permute-done.1 = bf16[8192,128]{1,0:T(8,128)(2,1)} collective-permute-done((bf16[8192,128]{1,0:T(8,128)(2,1)}, bf16[8192,128]{1,0:T(8,128)(2,1)}, u32[]{:S(2)}, u32[]{:S(2)}) %collective-permute-start.1) | collective-permute-done | bytes 2097184 | tf_op jit(solution)/shard_map/ppermute | solution.py:12
  65.8 4.4 collective-permute-start.2
  70.6 1.4 fusion.4
  72.0 2.9 gather_fusion.1
  74.9 1.4 convolution_bitcast_fusion.2
  76.3 2.4 convolution_add_fusion.2
  78.7 2.2 gather_fusion.2
  80.9 1.3 convolution_bitcast_fusion.1
  82.3 1.4 convolution_add_fusion.1
  83.7 9.7 collective-permute-done.2
  93.5 2.9 gather_fusion.3
  96.4 1.4 convolution_bitcast_fusion
  97.8 1.4 convolution_add_fusion
  102.6 1.3 dynamic-slice
  104.5 47.4 %all-reduce = f32[2048]{0:T(1024)S(1)} all-reduce(f32[2048]{0:T(1024)S(1)} %reshape.196), channel_id=3, replica_groups=mesh['row'=64,'col'=16] {'col'}, use_global_device_ids=true, to_apply=%region_2.3.clone | all-reduce | flops 2048 | bytes 16384
  152.0 39.4 %reduce-scatter.2.cloned.1.call-done = f32[128,128]{1,0:T(8,128)} async-done(((f32[2048,128]{1,0:T(8,128)}), f32[128,128]{1,0:T(8,128)}) %reduce-scatter.2.cloned.1.call-update) | async-done | bytes 65552 | tf_op jit(solution)/shard_map/reduce_scatter | solution.py:72
  194.0 1.3 gather_fusion.4
  195.4 847.2 %all-reduce.3.cloned.1.call-done = f32[128,128]{1,0:T(8,128)} async-done(((f32[128,128]{1,0:T(8,128)}), f32[128,128]{1,0:T(8,128)}) %all-reduce.3.cloned.1.call-update) | async-done | bytes 65552 | tf_op jit(solution)/shard_map/psum | solution.py:85
  1042.5 1.5 copy.27
  (48 shorter events, 12.0 us)
Async XLA Ops:
  7.2 185.9 %copy-start = (bf16[128,128]{1,0:T(8,128)(2,1)S(1)}, bf16[128,128]{1,0:T(8,128)(2,1)}, u32[]{:S(2)}) copy-start(bf16[128,128]{1,0:T(8,128)(2,1)} %param.15) | copy-start | bytes 98308
  7.2 184.2 %reduce-scatter.2.cloned.1.call-start = ((), (), s32[]{:S(2)}) async-start(), calls=%async_computation.1 | async-start | bytes 1114112 | tf_op jit(solution)/shard_map/reduce_scatter | solution.py:72
  8.0 34.6 %copy-start.2 = (bf16[1,1,96,4096]{3,2,1,0:T(8,128)(2,1)S(1)}, bf16[1,1,96,4096]{3,2,1,0:T(8,128)(2,1)}, u32[]{:S(2)}) copy-start(bf16[1,1,96,4096]{3,2,1,0:T(8,128)(2,1)} %param.12) | copy-start | bytes 2359300
  10.6 37.5 %copy-start.5 = (s32[1,1,2,96]{3,2,1,0:T(2,128)S(1)}, s32[1,1,2,96]{3,2,1,0:T(2,128)}, u32[]{:S(2)}) copy-start(s32[1,1,2,96]{3,2,1,0:T(2,128)} %param.10) | copy-start | bytes 2308
  10.6 27.5 %collective-permute-start = (bf16[8192,128]{1,0:T(8,128)(2,1)S(1)}, bf16[8192,128]{1,0:T(8,128)(2,1)}, u32[]{:S(2)}, u32[]{:S(2)}) collective-permute-start(bf16[8192,128]{1,0:T(8,128)(2,1)S(1)} %multiply_convert_fusion), channel_id=1, source_target_pairs={{0,1},{1,2},{2,3},{3,4},{4,5},{5,6},{6,7},{7,8},{8,9},{9,10},{10,1... | collective-permute-start | bytes 6291464 | tf_op jit(solution)/shard_map/ppermute | solution.py:12
  38.1 27.8 %collective-permute-start.1 = (bf16[8192,128]{1,0:T(8,128)(2,1)}, bf16[8192,128]{1,0:T(8,128)(2,1)}, u32[]{:S(2)}, u32[]{:S(2)}) collective-permute-start(bf16[8192,128]{1,0:T(8,128)(2,1)} %collective-permute-done), channel_id=1, source_target_pairs={{0,1},{1,2},{2,3},{3,4},{4,5},{5,6},{6,7},{7,8},{8,9},{9,10},{10,1... | collective-permute-start | bytes 6291464 | tf_op jit(solution)/shard_map/ppermute | solution.py:12
  42.6 27.6 %copy-start.6 = (s32[1,1,96]{2,1,0:T(1,128)S(1)}, s32[1,1,96]{2,1,0:T(1,128)}, u32[]{:S(2)}) copy-start(s32[1,1,96]{2,1,0:T(1,128)} %param.11) | copy-start | bytes 1156
  65.8 27.7 %collective-permute-start.2 = (bf16[8192,128]{1,0:T(8,128)(2,1)}, bf16[8192,128]{1,0:T(8,128)(2,1)}, u32[]{:S(2)}, u32[]{:S(2)}) collective-permute-start(bf16[8192,128]{1,0:T(8,128)(2,1)} %collective-permute-done.1), channel_id=1, source_target_pairs={{0,1},{1,2},{2,3},{3,4},{4,5},{5,6},{6,7},{7,8},{8,9},{9,10},{10,1... | collective-permute-start | bytes 6291464 | tf_op jit(solution)/shard_map/ppermute | solution.py:12
  80.9 1.3 copy-start.1
  99.8 1.4 copy-start.3
  100.9 51.1 %copy-start.7 = (s32[1,128]{1,0:T(1,128)S(1)}, s32[1,128]{1,0:T(1,128)}, u32[]{:S(2)}) copy-start(s32[1,128]{1,0:T(1,128)} %param.14) | copy-start | bytes 1540
  101.0 92.9 %copy-start.4 = (bf16[128,128]{1,0:T(8,128)(2,1)S(1)}, bf16[128,128]{1,0:T(8,128)(2,1)}, u32[]{:S(2)}) copy-start(bf16[128,128]{1,0:T(8,128)(2,1)} %param.13) | copy-start | bytes 98308
  101.0 941.5 %all-reduce.3.cloned.1.call-start = ((), (), s32[]{:S(2)}) async-start(), calls=%async_computation.2 | async-start | bytes 131072 | tf_op jit(solution)/shard_map/psum | solution.py:85
Sparse Core Ops, SparseCore 0:
  101.1 90.2 reduce-scatter.1
  198.3 844.1 all-reduce.2
where the time goes:
time: 1050 us
  waiting for transfers between devices  936 us (89%)
  blocking collectives  47.4 us (5%)
  local copies, waits for them, and re-layouts  20.5 us (2%)
  between operations  15 us (1%)
  starting transfers between devices  13.5 us (1%)
  matrix products  12.2 us (1%)
    psum x1, waiting for transfers between devices, per_device(): weight_grad = lax.psum(local_grad, ('row', 'col'))  847 us
    ppermute x3, waiting for transfers between devices, passed_along(): return lax.ppermute(value, axis, pairs)  49.7 us
    unnamed x1, blocking collectives  47.4 us
    reduce_scatter x1, waiting for transfers between devices, per_device(): lax.psum_scatter(partial_value, 'col', scatter_dimension=0, tiled=True)  39.4 us
  transfers between devices with their start and end apart: 5, of which 5 were waited for; matrix products, arithmetic and copies ran while one was open for 2% of the time, Pallas kernels for 0%

commit v1 on v0

v1 whole, which is shorter than its diff:
```python
import jax
import jax.numpy as jnp
from jax import lax
from jax.sharding import PartitionSpec as P

TB = 64
META_ROWS = 16


def passed_along(value, axis, steps):
    count = lax.axis_size(axis)
    pairs = [(source, (source + steps) % count) for source in range(count)]
    return lax.ppermute(value, axis, pairs)


def three_parts(value):
    high = value.astype(jnp.bfloat16)
    rest = value - high.astype(jnp.float32)
    middle = rest.astype(jnp.bfloat16)
    low = (rest - middle.astype(jnp.float32)).astype(jnp.bfloat16)
    return high, middle, low


def exchanged(parts, axis):
    return lax.all_to_all(parts, axis, 0, 0)


def to_all(value, axis):
    count = lax.axis_size(axis)
    copies = jnp.broadcast_to(value[None], (count, *value.shape))
    return exchanged(lax.optimization_barrier(copies), axis)


def per_device(
    features, source_degree, tile_coords, tile_counts, tile_values, weight, node_order, cotangent
):
    columns = lax.axis_size("col")
    row_count = lax.axis_size("row")
    step_total = min(4, columns)
    coords = tile_coords.reshape(2, step_total, -1)
    occupied = (tile_counts.reshape(step_total, -1) > 0).astype(jnp.bfloat16)
    per_step = coords.shape[-1]
    panel_rows, feat_dim = features.shape
    out_rows = node_order.shape[-1]
    row_panel = out_rows * columns
    row_tiles = row_panel // TB

    places = jnp.stack([coords[0].astype(jnp.bfloat16), coords[1].astype(jnp.bfloat16), occupied], axis=1)
    places = jnp.pad(places, ((0, 0), (0, META_ROWS - 3), (0, 128 - per_step)))
    packed = jnp.concatenate([tile_values.reshape(step_total, -1, 128), places], axis=1)
    packed = lax.optimization_barrier(packed)
    moved = [packed[0]] + [passed_along(packed[step], "col", -step) for step in range(1, step_total)]

    scaled = (
        features.astype(jnp.float32) * lax.rsqrt(1.0 + source_degree.astype(jnp.float32))[:, None]
    ).astype(jnp.bfloat16)
    panel_blocks = scaled.reshape(-1, TB, feat_dim)

    def one_step(group):
        place = group[-META_ROWS:, :per_step]
        tile_row, tile_col, filled = place[0], place[1].astype(jnp.int32), place[2]
        tiles = group[:-META_ROWS].reshape(per_step, TB, TB)
        targets = (
            tile_row.astype(jnp.int32)[None, :] == jnp.arange(row_tiles)[:, None]
        ).astype(jnp.float32) * filled.astype(jnp.float32)[None, :]
        products = jnp.einsum(
            "tij,tjf->tif", tiles, panel_blocks[tile_col], preferred_element_type=jnp.float32
        )
        sums = jnp.einsum("rt,tif->rif", targets, products, precision=lax.Precision.HIGHEST)
        weights = jnp.sum(tiles, axis=-1, dtype=jnp.float32)
        return sums, jnp.dot(targets, weights, precision=lax.Precision.HIGHEST)

    total, degree = one_step(moved[0])
    for group in moved[1:]:
        more, more_degree = one_step(group)
        total, degree = total + more, degree + more_degree
    row_index = lax.axis_index("row")
    owner = row_index * columns // row_count
    self_start = row_index * row_panel % panel_rows
    self_rows = lax.dynamic_slice_in_dim(scaled, self_start, row_panel, 0).astype(jnp.float32)
    holder = (lax.axis_index("col") == owner).astype(jnp.float32)
    partial_value = total.reshape(row_panel, feat_dim) + holder * self_rows
    degree_parts = jnp.stack(three_parts(degree.reshape(columns, out_rows)), axis=1)
    outgoing = jnp.concatenate(
        [
            partial_value.astype(jnp.bfloat16).reshape(columns, out_rows, feat_dim),
            jnp.pad(degree_parts, ((0, 0), (0, META_ROWS - 3), (0, 0))),
        ],
        axis=1,
    )
    arrived = exchanged(outgoing, "col").astype(jnp.float32).sum(0)
    sums = arrived[:out_rows]
    degrees = arrived[out_rows] + arrived[out_rows + 1] + arrived[out_rows + 2]
    normed = (sums * lax.rsqrt(1.0 + degrees)[:, None]).astype(jnp.bfloat16)
    order = node_order.reshape(-1)
    ordered = normed[order]
    activations = jnp.maximum(
        jnp.dot(ordered, weight, preferred_element_type=jnp.float32), 0.0
    ).astype(jnp.bfloat16)
    node_total = out_rows * row_count * columns
    local_grad = jnp.dot(ordered.T, cotangent, preferred_element_type=jnp.float32) * node_total ** (
        -0.5
    )
    share = exchanged(local_grad.reshape(columns, -1, feat_dim), "col").sum(0)
    share = to_all(share, "row").sum(0)
    weight_grad = to_all(share, "col").reshape(local_grad.shape)
    return (activations, weight_grad)


def solution(mesh):
    in_specs = (
        P("col", None),
        P("col"),
        P("row", "col", None, None),
        P("row", "col", None),
        P("row", "col", None, None),
        P(),
        P(("row", "col"), None),
        P(("row", "col"), None),
    )
    out_specs = (P(("row", "col"), None), P())
    return jax.shard_map(
        per_device, mesh=mesh, in_specs=in_specs, out_specs=out_specs, check_vma=False
    )
```

time: 1050 us -> 166 us (0.16)
  waiting for transfers between devices: 936 us -> 15.6 us
  blocking collectives: 47.4 us -> 70.2 us
  starting transfers between devices: 13.5 us -> 32.3 us
  between operations: 15 us -> 0.99 us
    psum x1 -> x0, waiting for transfers between devices: 847 us -> none  [per_device(): weight_grad = lax.psum(local_grad, ('row', 'col'))]
    all_to_all x0 -> x2, blocking collectives: none -> 70.2 us  [exchanged(): return lax.all_to_all(parts, axis, 0, 0)]
    ppermute x3, waiting for transfers between devices: 49.7 us -> 0.01 us  [passed_along(): return lax.ppermute(value, axis, pairs)]
    unnamed x1 -> x0, blocking collectives: 47.4 us -> none
    reduce_scatter x1 -> x0, waiting for transfers between devices: 39.4 us -> none  [per_device(): lax.psum_scatter(partial_value, 'col', scatter_dimension=0, tiled=True)]
    all_to_all x0 -> x2, waiting for transfers between devices: none -> 15.6 us  [exchanged(): return lax.all_to_all(parts, axis, 0, 0)]
    all_to_all x0 -> x2, starting transfers between devices: none -> 12.4 us  [exchanged(): return lax.all_to_all(parts, axis, 0, 0)]
  transfers between devices with their start and end apart: 5 -> 5, of which waited for: 5 -> 2; matrix products, arithmetic and copies ran while one was open for 2% -> 9% of each run, Pallas kernels for 0% -> 0%
where the time goes in v1:
time: 166 us; the launch traced here: 165 us
  blocking collectives  70.2 us (42%)
  starting transfers between devices  32.3 us (19%)
  matrix products  16.2 us (10%)
  local copies, waits for them, and re-layouts  15.9 us (10%)
  waiting for transfers between devices  15.6 us (9%)
  other arithmetic  13.6 us (8%)
    all_to_all x2, blocking collectives, exchanged(): return lax.all_to_all(parts, axis, 0, 0)  70.2 us
    ppermute x3, starting transfers between devices, passed_along(): return lax.ppermute(value, axis, pairs)  19.9 us
    all_to_all x2, waiting for transfers between devices, exchanged(): return lax.all_to_all(parts, axis, 0, 0)  15.6 us
    all_to_all x2, starting transfers between devices, exchanged(): return lax.all_to_all(parts, axis, 0, 0)  12.4 us
    dot_general x4, matrix products, one_step(): jnp.einsum('tij,tjf->tif', tiles, panel_blocks[tile_col], preferred_eleme...  7.12 us
    dot_general x4, matrix products, one_step(): jnp.einsum('rt,tif->rif', targets, products, precision=lax.Precision.HIGH...  7.06 us
    gather x4, local copies, waits for them, and re-layouts, one_step(): panel_blocks[tile_col]  4.73 us
    reduce_sum x4, other arithmetic, one_step(): weights = jnp.sum(tiles, axis=-1, dtype=jnp.float32)  4.1 us
  transfers between devices with their start and end apart: 5, of which 2 were waited for; matrix products, arithmetic and copies ran while one was open for 9% of the time, Pallas kernels for 0%

profile of v1, /device:TPU:1, one launch (start us, length us, event | category | flops | bytes accessed | tf_op | source)
XLA Modules:
  0.0 164.8 jit_solution(14416753201430467631)
XLA Ops:
  2.3 1.5 reshape.268
  4.7 16.1 %collective-permute-start = (bf16[784,128]{1,0:T(8,128)(2,1)S(1)}, bf16[784,128]{1,0:T(8,128)(2,1)}, u32[]{:S(2)}, u32[]{:S(2)}) collective-permute-start(bf16[784,128]{1,0:T(8,128)(2,1)S(1)} %get-tuple-element.6), channel_id=1, source_target_pairs={{0,15},{1,0},{2,1},{3,2},{4,3},{5,4},{6,5},{7,6},{8,7},{9,8},{10,9... | collective-permute-start | bytes 602120 | tf_op jit(solution)/shard_map/ppermute | solution.py:13
  20.7 1.9 %collective-permute-start.1 = (bf16[784,128]{1,0:T(8,128)(2,1)}, bf16[784,128]{1,0:T(8,128)(2,1)}, u32[]{:S(2)}, u32[]{:S(2)}) collective-permute-start(bf16[784,128]{1,0:T(8,128)(2,1)} %get-tuple-element.5), channel_id=1, source_target_pairs={{0,14},{1,15},{2,0},{3,1},{4,2},{5,3},{6,4},{7,5},{8,6},{9,7},{10,... | collective-permute-start | bytes 602120 | tf_op jit(solution)/shard_map/ppermute | solution.py:13
  22.7 1.9 %collective-permute-start.2 = (bf16[784,128]{1,0:T(8,128)(2,1)}, bf16[784,128]{1,0:T(8,128)(2,1)}, u32[]{:S(2)}, u32[]{:S(2)}) collective-permute-start(bf16[784,128]{1,0:T(8,128)(2,1)} %get-tuple-element.4), channel_id=1, source_target_pairs={{0,13},{1,14},{2,15},{3,0},{4,1},{5,2},{6,3},{7,4},{8,5},{9,6},{10... | collective-permute-start | bytes 602120 | tf_op jit(solution)/shard_map/ppermute | solution.py:13
  25.2 2.5 %multiply_convert_fusion = bf16[8192,128]{1,0:T(8,128)(2,1)S(1)} fusion(bf16[8192,128]{1,0:T(8,128)(2,1)} %param.8, f32[8192]{0:T(1024)S(1)} %add_rsqrt_fusion), kind=kLoop, calls=%fused_computation.5 | loop fusion | flops 3145728 | bytes 4227072 | tf_op jit(solution)/shard_map/convert_element_type | solution.py:56
  29.4 2.6 %fusion.9 = f32[32,64,128]{2,0,1:T(8,128)S(1)} fusion(f32[24,64,128]{2,1,0:T(8,128)} %fusion.71, f32[24]{0:T(128)S(1)} %get-tuple-element.15, s32[24]{0:T(128)S(1)} %get-tuple-element.14), kind=kOutput, calls=%fused_computation.27 | convolution fusion | flops 75499008 | bytes 1835200 | tf_op jit(solution)/shard_map/rt,tif->rif/dot_general | solution.py:69
  36.1 1.3 convert_reduce_fusion.3
  37.4 1.3 convert_reduce_fusion.2
  40.5 1.3 convert_reduce_fusion.1
  45.7 1.4 gather_fusion.1
  47.1 2.2 %fusion.72 = f32[24,64,128]{2,1,0:T(8,128)} fusion(bf16[24,64,64]{2,1,0:T(8,128)(2,1)} %reshape.271, bf16[24,64,128]{2,1,0:T(8,128)(2,1)} %gather_fusion.1), kind=kOutput, calls=%fused_computation.140 | convolution fusion | flops 25165824 | bytes 1376256 | tf_op jit(solution)/shard_map/tij,tjf->tif/dot_general | solution.py:66
  50.0 1.3 gather_fusion.2
  51.4 2.3 %fusion.73 = f32[24,64,128]{2,1,0:T(8,128)} fusion(bf16[24,64,64]{2,1,0:T(8,128)(2,1)} %reshape.272, bf16[24,64,128]{2,1,0:T(8,128)(2,1)} %gather_fusion.2), kind=kOutput, calls=%fused_computation.141 | convolution fusion | flops 25165824 | bytes 1376256 | tf_op jit(solution)/shard_map/tij,tjf->tif/dot_general | solution.py:66
  54.3 1.4 gather_fusion.3
  55.7 1.5 fusion.74
  57.2 1.5 convolution_add_fusion.2
  58.7 1.5 convolution_add_fusion.1
  60.2 1.5 convolution_add_fusion
  63.3 4.7 %all-to-all-start = ((bf16[16,144,128]{2,1,0:T(8,128)(2,1)}), bf16[16,144,128]{2,1,0:T(8,128)(2,1)S(1)}, u32[]{:S(2)}, u32[]{:S(2)}) async-start(bf16[16,144,128]{2,1,0:T(8,128)(2,1)} %fusion.11), calls=%async_computation | async-start | bytes 1179648 | tf_op jit(solution)/shard_map/all_to_all | solution.py:25
  68.0 10.5 %all-to-all-done = bf16[16,144,128]{2,1,0:T(8,128)(2,1)S(1)} async-done(((bf16[16,144,128]{2,1,0:T(8,128)(2,1)}), bf16[16,144,128]{2,1,0:T(8,128)(2,1)S(1)}, u32[]{:S(2)}, u32[]{:S(2)}) %all-to-all-start) | async-done | bytes 589856 | tf_op jit(solution)/shard_map/all_to_all | solution.py:25
  79.6 9.4 %all_to_all.20 = f32[16,8,128]{2,1,0:T(8,128)S(1)} all-to-all(f32[16,8,128]{2,1,0:T(8,128)S(1)} %fusion.2), channel_id=1, replica_groups=mesh['row'=64,'col'=16] {'col'}, dimensions={0} | all-to-all | bytes 131072 | tf_op jit(solution)/shard_map/all_to_all | solution.py:25
  89.1 60.8 %all_to_all.21 = f32[64,8,128]{2,1,0:T(8,128)S(1)} all-to-all(f32[64,8,128]{2,1,0:T(8,128)S(1)} %broadcast_in_dim.4), channel_id=1, replica_groups=mesh['row'=64,'col'=16] {'row'}, dimensions={0} | all-to-all | bytes 524288 | tf_op jit(solution)/shard_map/all_to_all | solution.py:25
  150.6 7.7 %all-to-all-start.3 = ((f32[16,8,128]{2,1,0:T(8,128)}), f32[16,8,128]{2,1,0:T(8,128)S(1)}, u32[]{:S(2)}, u32[]{:S(2)}) async-start(f32[16,8,128]{2,1,0:T(8,128)} %broadcast_in_dim.5), calls=%async_computation.3 | async-start | bytes 131072 | tf_op jit(solution)/shard_map/all_to_all | solution.py:25
  159.0 5.1 %all-to-all-done.3 = f32[16,8,128]{2,1,0:T(8,128)S(1)} async-done(((f32[16,8,128]{2,1,0:T(8,128)}), f32[16,8,128]{2,1,0:T(8,128)S(1)}, u32[]{:S(2)}, u32[]{:S(2)}) %all-to-all-start.3) | async-done | bytes 65568 | tf_op jit(solution)/shard_map/all_to_all | solution.py:25
  (73 shorter events, 20.8 us)
Async XLA Ops:
  0.6 78.8 %copy-start = (bf16[128,128]{1,0:T(8,128)(2,1)S(1)}, bf16[128,128]{1,0:T(8,128)(2,1)}, u32[]{:S(2)}) copy-start(bf16[128,128]{1,0:T(8,128)(2,1)} %param.15) | copy-start | bytes 98308
  3.8 21.4 %copy-start.4 = (s32[8192]{0:T(1024)S(1)}, s32[8192]{0:T(1024)}, u32[]{:S(2)}) copy-start(s32[8192]{0:T(1024)} %param.9) | copy-start | bytes 98308
  4.7 27.6 %collective-permute-start = (bf16[784,128]{1,0:T(8,128)(2,1)S(1)}, bf16[784,128]{1,0:T(8,128)(2,1)}, u32[]{:S(2)}, u32[]{:S(2)}) collective-permute-start(bf16[784,128]{1,0:T(8,128)(2,1)S(1)} %get-tuple-element.6), channel_id=1, source_target_pairs={{0,15},{1,0},{2,1},{3,2},{4,3},{5,4},{6,5},{7,6},{8,7},{9,8},{10,9... | collective-permute-start | bytes 602120 | tf_op jit(solution)/shard_map/ppermute | solution.py:13
  20.7 13.5 %collective-permute-start.1 = (bf16[784,128]{1,0:T(8,128)(2,1)}, bf16[784,128]{1,0:T(8,128)(2,1)}, u32[]{:S(2)}, u32[]{:S(2)}) collective-permute-start(bf16[784,128]{1,0:T(8,128)(2,1)} %get-tuple-element.5), channel_id=1, source_target_pairs={{0,14},{1,15},{2,0},{3,1},{4,2},{5,3},{6,4},{7,5},{8,6},{9,7},{10,... | collective-permute-start | bytes 602120 | tf_op jit(solution)/shard_map/ppermute | solution.py:13
  22.7 16.0 %collective-permute-start.2 = (bf16[784,128]{1,0:T(8,128)(2,1)}, bf16[784,128]{1,0:T(8,128)(2,1)}, u32[]{:S(2)}, u32[]{:S(2)}) collective-permute-start(bf16[784,128]{1,0:T(8,128)(2,1)} %get-tuple-element.4), channel_id=1, source_target_pairs={{0,13},{1,14},{2,15},{3,0},{4,1},{5,2},{6,3},{7,4},{8,5},{9,6},{10... | collective-permute-start | bytes 602120 | tf_op jit(solution)/shard_map/ppermute | solution.py:13
  55.7 1.5 copy-start.1
  55.7 3.0 %copy-start.2 = (f32[24,64,128]{2,1,0:T(8,128)S(1)}, f32[24,64,128]{2,1,0:T(8,128)}, u32[]{:S(2)}) copy-start(f32[24,64,128]{2,1,0:T(8,128)} %fusion.73) | copy-start | bytes 2359300
  62.3 5.7 %copy-start.5 = (s32[1,128]{1,0:T(1,128)S(1)}, s32[1,128]{1,0:T(1,128)}, u32[]{:S(2)}) copy-start(s32[1,128]{1,0:T(1,128)} %param.14) | copy-start | bytes 1540
  63.3 95.0 %copy-start.3 = (bf16[128,128]{1,0:T(8,128)(2,1)S(1)}, bf16[128,128]{1,0:T(8,128)(2,1)}, u32[]{:S(2)}) copy-start(bf16[128,128]{1,0:T(8,128)(2,1)} %param.13) | copy-start | bytes 98308
  63.3 15.3 %all-to-all-start = ((bf16[16,144,128]{2,1,0:T(8,128)(2,1)}), bf16[16,144,128]{2,1,0:T(8,128)(2,1)S(1)}, u32[]{:S(2)}, u32[]{:S(2)}) async-start(bf16[16,144,128]{2,1,0:T(8,128)(2,1)} %fusion.11), calls=%async_computation | async-start | bytes 1179648 | tf_op jit(solution)/shard_map/all_to_all | solution.py:25
  150.6 13.5 %all-to-all-start.3 = ((f32[16,8,128]{2,1,0:T(8,128)}), f32[16,8,128]{2,1,0:T(8,128)S(1)}, u32[]{:S(2)}, u32[]{:S(2)}) async-start(f32[16,8,128]{2,1,0:T(8,128)} %broadcast_in_dim.5), calls=%async_computation.3 | async-start | bytes 131072 | tf_op jit(solution)/shard_map/all_to_all | solution.py:25

commit v2 on v1

v2 whole, which is shorter than its diff:
```python
import jax
import jax.numpy as jnp
from jax import lax
from jax.experimental import pallas as pl
from jax.experimental.pallas import tpu as pltpu
from jax.sharding import Mesh, PartitionSpec as P

TB = 64
HALF = TB // 2
META_ROWS = 16
UNROLL = 4
ROW = ("x_hi", "z")
PLANE = ("x_hi", "col")


def passed_along(value, axis, steps):
    count = lax.axis_size(axis)
    pairs = [(source, (source + steps) % count) for source in range(count)]
    return lax.ppermute(value, axis, pairs)


def exchanged(parts, axis):
    return lax.all_to_all(parts, axis, 0, 0)


def to_all(value, axis):
    count = lax.psum(1, axis)
    copies = jnp.broadcast_to(value[None], (count, *value.shape))
    return exchanged(lax.optimization_barrier(copies), axis)


def two_parts(value):
    high = value.astype(jnp.bfloat16)
    return high, (value - high.astype(jnp.float32)).astype(jnp.bfloat16)


def side_by_side(block):
    none = jnp.zeros_like(block)
    return jnp.concatenate(
        [jnp.concatenate([block, none], axis=1), jnp.concatenate([none, block], axis=1)], axis=0
    )


def tiles_kernel(place_ref, panel_ref, *refs):
    groups, out_ref, total = refs[:-2], refs[-2], refs[-1]
    tiles = (groups[0].shape[0] - META_ROWS) // HALF
    feat = panel_ref.shape[1]
    flags = len(groups) * 2 * tiles
    self_loop, self_start = place_ref[flags + len(groups)], place_ref[flags + len(groups) + 1]
    row_tiles = total.shape[0] // HALF

    total[...] = jnp.zeros_like(total)

    @pl.when(self_loop > 0)
    def _():
        at = lax.broadcasted_iota(jnp.int32, (HALF, 2 * TB), 1)
        row = lax.broadcasted_iota(jnp.int32, (HALF, 2 * TB), 0)
        same = (at % TB == 2 * row + at // TB).astype(jnp.float32).astype(jnp.bfloat16)

        @pl.loop(0, row_tiles // UNROLL)
        def _(first):
            for one in range(UNROLL):
                tile = first * UNROLL + one
                block = panel_ref[pl.ds(pl.multiple_of((self_start + tile) * TB, TB), TB), :]
                total[pl.ds(pl.multiple_of(tile * HALF, HALF), HALF), : 2 * feat] = jnp.dot(
                    same, side_by_side(block), preferred_element_type=jnp.float32
                )

    for index, group in enumerate(groups):

        @pl.loop(0, place_ref[flags + index])
        def _(first):
            for one in range(UNROLL):
                slot = first * UNROLL + one
                at = index * 2 * tiles + slot
                tile_row, tile_col = place_ref[at], place_ref[at + tiles]
                tile = group[pl.ds(pl.multiple_of(slot * HALF, HALF), HALF), :]
                block = panel_ref[pl.ds(pl.multiple_of(tile_col * TB, TB), TB), :]
                product = jnp.dot(tile, side_by_side(block), preferred_element_type=jnp.float32)
                rows = pl.ds(pl.multiple_of(tile_row * HALF, HALF), HALF)
                total[rows, : 2 * feat] += product
                total[rows, 2 * feat :] += tile.astype(jnp.float32)

    out_rows = total.shape[0] // out_ref.shape[0]
    lane = lax.broadcasted_iota(jnp.int32, (META_ROWS, 2 * TB), 1)
    line = lax.broadcasted_iota(jnp.int32, (META_ROWS, 2 * TB), 0)
    half = (lane // TB == line % 2).astype(jnp.float32).astype(jnp.bfloat16)
    part = lax.broadcasted_iota(jnp.int32, (META_ROWS, out_rows), 0) // 2

    @pl.loop(0, out_ref.shape[0])
    def _(device):
        rows = pl.ds(pl.multiple_of(device * out_rows, out_rows), out_rows)
        out_ref[device, :out_rows, :] = total[rows, : 2 * feat].astype(out_ref.dtype)
        degree = sum(
            lax.dot_general(
                half, piece, (((1,), (1,)), ((), ())), preferred_element_type=jnp.float32
            )
            for piece in two_parts(total[rows, 2 * feat :])
        )
        high, low = (piece.astype(jnp.float32) for piece in two_parts(degree))
        lines = jnp.where(part == 0, high, jnp.where(part == 1, low, 0.0))
        none = jnp.zeros((META_ROWS, out_ref.shape[2] - out_rows), jnp.float32)
        out_ref[device, out_rows:, :] = jnp.concatenate([lines, none], axis=1).astype(out_ref.dtype)


def layer_kernel(node_total, arrived_ref, order_ref, weight_ref, cotangent_ref, act_ref, grad_ref):
    lines = arrived_ref.shape[1] - META_ROWS
    nodes, feat = cotangent_ref.shape
    total = arrived_ref[0].astype(jnp.float32)
    for device in range(1, arrived_ref.shape[0]):
        total += arrived_ref[device].astype(jnp.float32)
    diagonal = lax.broadcasted_iota(jnp.int32, (lines, lines), 0) == lax.broadcasted_iota(
        jnp.int32, (lines, lines), 1
    )
    normed = []
    for half in range(2):
        degrees = total[lines + half : lines + half + 1, :lines]
        degrees += total[lines + half + 2 : lines + half + 3, :lines]
        scale = jnp.where(diagonal, lax.rsqrt(1.0 + degrees), 0.0).sum(axis=1, keepdims=True)
        normed.append(total[:lines, half * feat : (half + 1) * feat] * scale)
    normed = jnp.concatenate(normed, axis=0).astype(jnp.bfloat16)
    line = lax.broadcasted_iota(jnp.int32, (nodes, nodes), 0)
    node = 2 * (line % lines) + line // lines
    chosen = (order_ref[...] == node).astype(jnp.float32).astype(jnp.bfloat16)
    over_rows = (((0,), (0,)), ((), ()))
    ordered = lax.dot_general(
        chosen, normed, over_rows, preferred_element_type=jnp.float32
    ).astype(jnp.bfloat16)
    pre = jnp.dot(ordered, weight_ref[...], preferred_element_type=jnp.float32)
    act_ref[...] = jnp.maximum(pre, 0.0).astype(act_ref.dtype)
    grad_ref[...] = (
        lax.dot_general(
            ordered, cotangent_ref[...], over_rows, preferred_element_type=jnp.float32
        )
        * node_total ** (-0.5)
    )


def per_device(
    features, source_degree, tile_coords, tile_counts, tile_values, weight, node_order, cotangent
):
    columns = lax.axis_size("col")
    row_count = lax.psum(1, ROW)
    step_total = min(4, columns)
    coords = tile_coords.reshape(2, step_total, -1)
    occupied = tile_counts.reshape(step_total, -1) > 0
    per_step = coords.shape[-1]
    panel_rows, feat_dim = features.shape
    out_rows = node_order.shape[-1]
    row_panel = out_rows * columns
    vmem = pl.BlockSpec(memory_space=pltpu.VMEM)
    smem = pl.BlockSpec(memory_space=pltpu.SMEM)
    params = pltpu.CompilerParams(vmem_limit_bytes=32 * 1024 * 1024)

    filled = jnp.broadcast_to(occupied.sum(axis=1, keepdims=True), occupied.shape)
    places = jnp.stack([coords[0], coords[1], filled], axis=1).astype(jnp.bfloat16)
    places = jnp.pad(places, ((0, 0), (0, META_ROWS - 3), (0, 128 - per_step)))
    tiles = jnp.where(occupied[..., None], tile_values.reshape(step_total, per_step, -1), 0)
    packed = jnp.concatenate([tiles.reshape(step_total, -1, 128), places], axis=1)
    packed = lax.optimization_barrier(packed)
    groups = [packed[0]] + [
        passed_along(packed[step], "col", -step) for step in range(1, step_total)
    ]
    scaled = (
        features.astype(jnp.float32) * lax.rsqrt(1.0 + source_degree.astype(jnp.float32))[:, None]
    ).astype(jnp.bfloat16)
    row_index = lax.axis_index(ROW)
    holder = lax.axis_index("col") == row_index * columns // row_count
    self_start = row_index * row_panel % panel_rows // TB
    met = jnp.stack([group[-META_ROWS:] for group in groups]).astype(jnp.int32)
    place = jnp.concatenate(
        [
            met[:, :2, :per_step].reshape(-1),
            (met[:, 2, 0] + UNROLL - 1) // UNROLL,
            jnp.stack([holder.astype(jnp.int32), self_start.astype(jnp.int32)]),
        ]
    )
    lines = out_rows // 2
    outgoing = pl.pallas_call(
        tiles_kernel,
        out_shape=jax.ShapeDtypeStruct((columns, lines + META_ROWS, 2 * feat_dim), jnp.bfloat16),
        in_specs=[smem] + [vmem] * (1 + step_total),
        out_specs=vmem,
        scratch_shapes=[pltpu.VMEM((row_panel // 2, 2 * feat_dim + 2 * TB), jnp.float32)],
        compiler_params=params,
        name="tiles",
    )(place, scaled, *groups)
    arrived = exchanged(outgoing, "col")
    node_total = out_rows * row_count * columns
    activations, local_grad = pl.pallas_call(
        lambda *refs: layer_kernel(node_total, *refs),
        out_shape=(
            jax.ShapeDtypeStruct((out_rows, feat_dim), jnp.bfloat16),
            jax.ShapeDtypeStruct((feat_dim, feat_dim), jnp.float32),
        ),
        in_specs=[vmem] * 4,
        out_specs=(vmem, vmem),
        compiler_params=params,
        name="layer",
    )(arrived, node_order, weight, cotangent)
    share = exchanged(local_grad.reshape(lax.psum(1, PLANE), -1, feat_dim), PLANE).sum(0)
    share = to_all(share, "z").sum(0)
    weight_grad = to_all(share, PLANE).reshape(local_grad.shape)
    return (activations, weight_grad)


def solution(mesh):
    rows, columns = mesh.devices.shape
    apart = Mesh(mesh.devices.reshape(2, rows // 2, columns), (*ROW, "col"))
    both = (*ROW, "col")
    in_specs = (
        P("col", None),
        P("col"),
        P(ROW, "col", None, None),
        P(ROW, "col", None),
        P(ROW, "col", None, None),
        P(),
        P(both, None),
        P(both, None),
    )
    out_specs = (P(both, None), P())
    return jax.shard_map(
        per_device, mesh=apart, in_specs=in_specs, out_specs=out_specs, check_vma=False
    )
```

time: 166 us -> 126 us (0.76)
  matrix products: 16.2 us -> 0 us
  blocking collectives: 70.2 us -> 84.4 us
  waiting for transfers between devices: 15.6 us -> 2.78 us
  starting transfers between devices: 32.3 us -> 19.9 us
  local copies, waits for them, and re-layouts: 15.9 us -> 4.29 us
  Pallas kernels: 0 us -> 7.76 us
  other arithmetic: 13.6 us -> 5.99 us
    dot_general x14 -> x0, matrix products: 16.2 us -> none  [the longest x4 7.12 us: one_step(): jnp.einsum('tij,tjf->tif', tiles, panel_blocks[tile_col], preferred_eleme...]
    all_to_all x2 -> x0, waiting for transfers between devices: 15.6 us -> none  [exchanged(): return lax.all_to_all(parts, axis, 0, 0)]
    all_to_all x2 -> x4, blocking collectives: 70.2 us -> 84.4 us  [exchanged(): return lax.all_to_all(parts, axis, 0, 0)]
    all_to_all x2 -> x0, starting transfers between devices: 12.4 us -> none  [exchanged(): return lax.all_to_all(parts, axis, 0, 0)]
    pallas_call x0 -> x2, Pallas kernels: none -> 7.76 us  [the longest x1 6.78 us: per_device(): pl.pallas_call(tiles_kernel, out_shape=jax.ShapeDtypeStruct((columns, lin...]
    gather x5 -> x0, local copies, waits for them, and re-layouts: 5.44 us -> none  [the longest x4 4.73 us: one_step(): panel_blocks[tile_col]]
    reduce_sum x7 -> x3, other arithmetic: 4.27 us -> 0.21 us  [the longest x1 0.12 us: per_device(): occupied.sum(axis=1, keepdims=True)]
    reshape x6 -> x2, local copies, waits for them, and re-layouts: 4.51 us -> 1.53 us  [the longest x1 1.45 us: per_device(): tile_values.reshape(step_total, per_step, -1)]
  transfers between devices with their start and end apart: 5 -> 3, of which waited for: 2 -> 2; matrix products, arithmetic and copies ran while one was open for 9% -> 3% of each run, Pallas kernels for 0% -> 0%
where the time goes in v2:
time: 126 us
  blocking collectives  84.4 us (67%)
  starting transfers between devices  19.9 us (16%)
  Pallas kernels  7.76 us (6%)
  other arithmetic  5.99 us (5%)
  local copies, waits for them, and re-layouts  4.29 us (3%)
  waiting for transfers between devices  2.78 us (2%)
    all_to_all x4, blocking collectives, exchanged(): return lax.all_to_all(parts, axis, 0, 0)  84.4 us
    ppermute x3, starting transfers between devices, passed_along(): return lax.ppermute(value, axis, pairs)  19.9 us
    pallas_call x1, Pallas kernels, per_device(): pl.pallas_call(tiles_kernel, out_shape=jax.ShapeDtypeStruct((columns, lin...  6.78 us
    convert_element_type x1, other arithmetic, per_device(): scaled = (features.astype(jnp.float32) * lax.rsqrt(1.0 + source_degree.as...  3.48 us
    ppermute x3, waiting for transfers between devices, passed_along(): return lax.ppermute(value, axis, pairs)  2.78 us
  transfers between devices with their start and end apart: 3, of which 2 were waited for; matrix products, arithmetic and copies ran while one was open for 3% of the time, Pallas kernels for 0%

profile of v2, /device:TPU:1, one launch (start us, length us, event | category | flops | bytes accessed | tf_op | source)
XLA Modules:
  0.0 125.9 jit_solution(16481301350945570776)
XLA Ops:
  0.6 0.7 convert.13
  1.3 0.7 compare_reduce_fusion
  2.0 0.1 gt.19
  2.1 0.1 convert_reduce_fusion
  2.2 0.1 stack_squeeze.10
  2.5 0.1 broadcast_in_dim.32
  2.6 1.5 %reshape.39 = bf16[4,768,128]{2,1,0:T(8,128)(2,1)S(1)} reshape(bf16[1,1,96,4096]{3,2,1,0:T(8,128)(2,1)} %param.12) | data formatting | bytes 1572864 | tf_op jit(solution)/shard_map/reshape | solution.py:158
  4.1 0.6 broadcast_select_fusion
  4.9 0.8 copy-done.3
  5.7 6.9 %collective-permute-start.2 = (bf16[784,128]{1,0:T(8,128)(2,1)S(1)}, bf16[784,128]{1,0:T(8,128)(2,1)S(1)}, u32[]{:S(2)}, u32[]{:S(2)}) collective-permute-start(bf16[784,128]{1,0:T(8,128)(2,1)S(1)} %get-tuple-element.9), channel_id=1, source_target_pairs={{0,13},{1,14},{2,15},{3,0},{4,1},{5,2},{6,3},{7,4},{8,5},{9,6},{10... | collective-permute-start | bytes 602120 | tf_op jit(solution)/shard_map/ppermute | solution.py:19
  12.7 2.2 %collective-permute-start.1 = (bf16[784,128]{1,0:T(8,128)(2,1)S(1)}, bf16[784,128]{1,0:T(8,128)(2,1)S(1)}, u32[]{:S(2)}, u32[]{:S(2)}) collective-permute-start(bf16[784,128]{1,0:T(8,128)(2,1)S(1)} %get-tuple-element.10), channel_id=1, source_target_pairs={{0,14},{1,15},{2,0},{3,1},{4,2},{5,3},{6,4},{7,5},{8,6},{9,7},{10,... | collective-permute-start | bytes 602120 | tf_op jit(solution)/shard_map/ppermute | solution.py:19
  14.8 10.8 %collective-permute-start = (bf16[784,128]{1,0:T(8,128)(2,1)S(1)}, bf16[784,128]{1,0:T(8,128)(2,1)S(1)}, u32[]{:S(2)}, u32[]{:S(2)}) collective-permute-start(bf16[784,128]{1,0:T(8,128)(2,1)S(1)} %get-tuple-element.11), channel_id=1, source_target_pairs={{0,15},{1,0},{2,1},{3,2},{4,3},{5,4},{6,5},{7,6},{8,7},{9,8},{10,9... | collective-permute-start | bytes 602120 | tf_op jit(solution)/shard_map/ppermute | solution.py:19
  25.7 3.5 %multiply_convert_fusion.panel_ref = bf16[8192,128]{1,0:T(8,128)(2,1)S(1)} fusion(bf16[8192,128]{1,0:T(8,128)(2,1)S(1)} %copy-done.4, f32[8192]{0:T(1024)S(1)} %add_rsqrt_fusion), kind=kLoop, calls=%fused_computation | loop fusion | flops 3145728 | bytes 4227072 | tf_op jit(solution)/shard_map/convert_element_type | solution.py:166
  29.2 0.7 slice.54
  29.9 0.5 collective-permute-done.1.refs_2_
  30.4 2.3 %collective-permute-done.refs_1_ = bf16[784,128]{1,0:T(8,128)(2,1)S(1)} collective-permute-done((bf16[784,128]{1,0:T(8,128)(2,1)S(1)}, bf16[784,128]{1,0:T(8,128)(2,1)S(1)}, u32[]{:S(2)}, u32[]{:S(2)}) %collective-permute-start) | collective-permute-done | bytes 200736 | tf_op jit(solution)/shard_map/ppermute | solution.py:19
  32.6 0.2 fusion.11
  33.0 6.8 %tiles.1 = bf16[16,80,256]{2,1,0:T(8,128)(2,1)S(1)} custom-call(s32[198]{0:T(256)S(1)} %pad_add_fusion.place_ref, bf16[8192,128]{1,0:T(8,128)(2,1)S(1)} %multiply_convert_fusion.panel_ref, bf16[784,128]{1,0:T(8,128)(2,1)S(1)} %get-tuple-element.8.refs_0_, bf16[784,128]{1,0:T(8,128)(2,1)S(1)} %collective-permute-done.refs_1_, ...), custom_call_target="tpu_custom_call" | custom-call | tf_op jit(solution)/shard_map/tiles/pallas_call | solution.py:179
  39.8 13.6 %all_to_all.20.refs_0_ = bf16[16,80,256]{2,1,0:T(8,128)(2,1)S(1)} all-to-all(bf16[16,80,256]{2,1,0:T(8,128)(2,1)S(1)} %tiles.1), channel_id=1, replica_groups=mesh['x_hi'=2,'z'=32,'col'=16] {'col'}, dimensions={0} | all-to-all | bytes 1310720 | tf_op jit(solution)/shard_map/all_to_all | solution.py:23
  53.4 1.0 layer.1
  54.4 10.6 %all_to_all.21 = f32[32,4,128]{2,1,0:T(4,128)S(1)} all-to-all(f32[32,4,128]{2,1,0:T(4,128)S(1)} %bitcast.20), channel_id=1, replica_groups=mesh['x_hi'=2,'z'=32,'col'=16] {'x_hi','col'}, dimensions={0} | all-to-all | bytes 131072 | tf_op jit(solution)/shard_map/all_to_all | solution.py:23
  65.1 46.8 %all_to_all.22 = f32[32,4,128]{2,1,0:T(4,128)S(1)} all-to-all(f32[32,4,128]{2,1,0:T(4,128)S(1)} %broadcast_in_dim.35), channel_id=1, replica_groups=mesh['x_hi'=2,'z'=32,'col'=16] {'z'}, dimensions={0} | all-to-all | bytes 131072 | tf_op jit(solution)/shard_map/all_to_all | solution.py:23
  111.9 13.4 %all_to_all.23 = f32[32,4,128]{2,1,0:T(4,128)S(1)} all-to-all(f32[32,4,128]{2,1,0:T(4,128)S(1)} %broadcast_in_dim.36), channel_id=1, replica_groups=mesh['x_hi'=2,'z'=32,'col'=16] {'x_hi','col'}, dimensions={0} | all-to-all | bytes 131072 | tf_op jit(solution)/shard_map/all_to_all | solution.py:23
  125.3 0.6 copy.21
  (32 shorter events, 0.7 us)
Async XLA Ops:
  4.0 21.6 %copy-start.5 = (s32[8192]{0:T(1024)S(1)}, s32[8192]{0:T(1024)}, u32[]{:S(2)}) copy-start(s32[8192]{0:T(1024)} %param.9) | copy-start | bytes 98308
  4.1 21.6 %copy-start.4 = (bf16[8192,128]{1,0:T(8,128)(2,1)S(1)}, bf16[8192,128]{1,0:T(8,128)(2,1)}, u32[]{:S(2)}) copy-start(bf16[8192,128]{1,0:T(8,128)(2,1)} %param.8) | copy-start | bytes 6291460
  4.8 0.9 copy-start.3
  5.7 24.2 %collective-permute-start.2 = (bf16[784,128]{1,0:T(8,128)(2,1)S(1)}, bf16[784,128]{1,0:T(8,128)(2,1)S(1)}, u32[]{:S(2)}, u32[]{:S(2)}) collective-permute-start(bf16[784,128]{1,0:T(8,128)(2,1)S(1)} %get-tuple-element.9), channel_id=1, source_target_pairs={{0,13},{1,14},{2,15},{3,0},{4,1},{5,2},{6,3},{7,4},{8,5},{9,6},{10... | collective-permute-start | bytes 602120 | tf_op jit(solution)/shard_map/ppermute | solution.py:19
  12.7 17.7 %collective-permute-start.1 = (bf16[784,128]{1,0:T(8,128)(2,1)S(1)}, bf16[784,128]{1,0:T(8,128)(2,1)S(1)}, u32[]{:S(2)}, u32[]{:S(2)}) collective-permute-start(bf16[784,128]{1,0:T(8,128)(2,1)S(1)} %get-tuple-element.10), channel_id=1, source_target_pairs={{0,14},{1,15},{2,0},{3,1},{4,2},{5,3},{6,4},{7,5},{8,6},{9,7},{10,... | collective-permute-start | bytes 602120 | tf_op jit(solution)/shard_map/ppermute | solution.py:19
  14.8 17.8 %collective-permute-start = (bf16[784,128]{1,0:T(8,128)(2,1)S(1)}, bf16[784,128]{1,0:T(8,128)(2,1)S(1)}, u32[]{:S(2)}, u32[]{:S(2)}) collective-permute-start(bf16[784,128]{1,0:T(8,128)(2,1)S(1)} %get-tuple-element.11), channel_id=1, source_target_pairs={{0,15},{1,0},{2,1},{3,2},{4,3},{5,4},{6,5},{7,6},{8,7},{9,8},{10,9... | collective-permute-start | bytes 602120 | tf_op jit(solution)/shard_map/ppermute | solution.py:19
  33.0 20.4 %copy-start = (bf16[128,128]{1,0:T(8,128)(2,1)S(1)}, bf16[128,128]{1,0:T(8,128)(2,1)}, u32[]{:S(2)}) copy-start(bf16[128,128]{1,0:T(8,128)(2,1)} %refs_2_.1) | copy-start | bytes 98308
  33.0 20.4 %copy-start.1 = (bf16[128,128]{1,0:T(8,128)(2,1)S(1)}, bf16[128,128]{1,0:T(8,128)(2,1)}, u32[]{:S(2)}) copy-start(bf16[128,128]{1,0:T(8,128)(2,1)} %refs_3_.1) | copy-start | bytes 98308
  33.0 20.4 %copy-start.2 = (s32[1,128]{1,0:T(1,128)S(1)}, s32[1,128]{1,0:T(1,128)}, u32[]{:S(2)}) copy-start(s32[1,128]{1,0:T(1,128)} %refs_1_.1) | copy-start | bytes 1540

commit v3 on v2

v3 whole, which is shorter than its diff:
```python
import functools

import jax
import jax.numpy as jnp
from jax import lax
from jax.experimental import pallas as pl
from jax.experimental.pallas import tpu as pltpu
from jax.sharding import Mesh, PartitionSpec as P

TB = 64
HALF = TB // 2
LANES = 2 * TB
META_ROWS = 16
META_USED = 8
UNROLL = 6
SELF_UNROLL = 8
ROW = ("x_hi", "z")
PLANE = ("x_hi", "col")
VMEM = pl.BlockSpec(memory_space=pltpu.VMEM)
SMEM = pl.BlockSpec(memory_space=pltpu.SMEM)
PARAMS = pltpu.CompilerParams(vmem_limit_bytes=32 * 1024 * 1024)


def passed_along(value, axis, steps):
    count = lax.axis_size(axis)
    pairs = [(source, (source + steps) % count) for source in range(count)]
    return lax.ppermute(value, axis, pairs)


def exchanged(parts, axis):
    return lax.all_to_all(parts, axis, 0, 0)


def to_all(value, axis):
    count = lax.psum(1, axis)
    copies = jnp.broadcast_to(value[None], (count, *value.shape))
    return exchanged(lax.optimization_barrier(copies), axis)


def two_parts(value):
    high = value.astype(jnp.bfloat16)
    return high, (value - high.astype(jnp.float32)).astype(jnp.bfloat16)


def side_by_side(block):
    none = jnp.zeros_like(block)
    return jnp.concatenate(
        [jnp.concatenate([block, none], axis=1), jnp.concatenate([none, block], axis=1)], axis=0
    )


def pack_kernel(coords_ref, counts_ref, values_ref, *refs):
    groups, wide, meta = refs[:-2], refs[-2], refs[-1]
    tiles = values_ref.shape[0]
    for chunk in range(HALF):
        piece = values_ref[:, chunk * LANES : (chunk + 1) * LANES].astype(jnp.float32)
        wide[pl.ds(chunk, tiles, stride=HALF), :] = piece
    meta[...] = jnp.zeros_like(meta)
    meta[0:2, :tiles] = coords_ref[...].astype(jnp.float32)
    meta[2:3, :tiles] = counts_ref[...].astype(jnp.float32)
    rows = wide.shape[0] // len(groups)
    for index, group in enumerate(groups):
        group[:rows, :] = wide[index * rows : (index + 1) * rows, :].astype(group.dtype)
        group[rows:, :] = meta[...].astype(group.dtype)


def places(groups, first, per_group, staged, held, sem):
    lane = lax.broadcasted_iota(jnp.int32, (1, LANES), 1)
    for index, group in enumerate(groups):
        meta = group[group.shape[0] - META_ROWS :, :].astype(jnp.float32).astype(jnp.int32)
        start = (first + index) * per_group
        own = (lane >= start) & (lane < start + per_group) & (meta[2:3, :] > 0)
        filled = own.astype(jnp.int32).astype(jnp.float32).sum(axis=1, keepdims=True)
        staged[index] = meta[:META_USED]
        staged[index, 2:3, :] = jnp.broadcast_to(filled, (1, LANES)).astype(jnp.int32)
    copy = pltpu.make_async_copy(staged, held, sem)
    copy.start()
    copy.wait()


def add_tiles(groups, first, per_group, held, panel_ref, total):
    feat = panel_ref.shape[1]
    for index, group in enumerate(groups):
        start = (first + index) * per_group
        filled = held[index, 2, 0]

        @pl.loop(0, (filled + UNROLL - 1) // UNROLL)
        def _(step):
            for one in range(UNROLL):
                slot = step * UNROLL + one
                tile_row, tile_col = held[index, 0, start + slot], held[index, 1, start + slot]
                tile = group[pl.ds(pl.multiple_of(slot * HALF, HALF), HALF), :]
                tile = jnp.where(slot < filled, tile, jnp.zeros_like(tile))
                block = panel_ref[pl.ds(pl.multiple_of(tile_col * TB, TB), TB), :]
                product = jnp.dot(tile, side_by_side(block), preferred_element_type=jnp.float32)
                rows = pl.ds(pl.multiple_of(tile_row * HALF, HALF), HALF)
                total[rows, : 2 * feat] += product
                total[rows, 2 * feat :] += tile.astype(jnp.float32)


def own_kernel(per_group, self_ref, features_ref, degree_ref, group, panel_ref, total, staged, held, sem):
    feat = panel_ref.shape[1]
    places([group], 0, per_group, staged, held, sem)
    scale = lax.rsqrt(1.0 + degree_ref[...].astype(jnp.float32)).T
    for part in range(degree_ref.shape[0]):
        rows = slice(part * LANES, (part + 1) * LANES)
        block = features_ref[rows, :].astype(jnp.float32) * scale[:, part : part + 1]
        panel_ref[rows, :] = block.astype(panel_ref.dtype)
    total[...] = jnp.zeros_like(total)

    @pl.when(self_ref[0] > 0)
    def _():
        at = lax.broadcasted_iota(jnp.int32, (HALF, LANES), 1)
        row = lax.broadcasted_iota(jnp.int32, (HALF, LANES), 0)
        same = (at % TB == 2 * row + at // TB).astype(jnp.float32).astype(jnp.bfloat16)

        @pl.loop(0, total.shape[0] // HALF // SELF_UNROLL)
        def _(first):
            for one in range(SELF_UNROLL):
                tile = first * SELF_UNROLL + one
                block = panel_ref[pl.ds(pl.multiple_of((self_ref[1] + tile) * TB, TB), TB), :]
                total[pl.ds(pl.multiple_of(tile * HALF, HALF), HALF), : 2 * feat] = jnp.dot(
                    same, side_by_side(block), preferred_element_type=jnp.float32
                )

    add_tiles([group], 0, per_group, held, panel_ref, total)


def moved_kernel(per_group, panel_ref, before_ref, *refs):
    groups, (out_ref, total, staged, held, sem) = refs[:-5], refs[-5:]
    feat = panel_ref.shape[1]
    places(groups, 1, per_group, staged, held, sem)
    total[...] = before_ref[...]
    add_tiles(groups, 1, per_group, held, panel_ref, total)
    out_rows = total.shape[0] // out_ref.shape[0]
    lane = lax.broadcasted_iota(jnp.int32, (META_ROWS, LANES), 1)
    line = lax.broadcasted_iota(jnp.int32, (META_ROWS, LANES), 0)
    half = (lane // TB == line % 2).astype(jnp.float32).astype(jnp.bfloat16)
    part = lax.broadcasted_iota(jnp.int32, (META_ROWS, out_rows), 0) // 2
    none = jnp.zeros((META_ROWS, out_ref.shape[2] - out_rows), jnp.float32)
    for device in range(out_ref.shape[0]):
        rows = slice(device * out_rows, (device + 1) * out_rows)
        out_ref[device, :out_rows, :] = total[rows, : 2 * feat].astype(out_ref.dtype)
        degree = sum(
            lax.dot_general(
                half, piece, (((1,), (1,)), ((), ())), preferred_element_type=jnp.float32
            )
            for piece in two_parts(total[rows, 2 * feat :])
        )
        high, low = (piece.astype(jnp.float32) for piece in two_parts(degree))
        lines = jnp.where(part == 0, high, jnp.where(part == 1, low, 0.0))
        out_ref[device, out_rows:, :] = jnp.concatenate([lines, none], axis=1).astype(out_ref.dtype)


def layer_kernel(node_total, arrived_ref, order_ref, weight_ref, cotangent_ref, act_ref, grad_ref):
    lines = arrived_ref.shape[1] - META_ROWS
    nodes, feat = cotangent_ref.shape
    total = arrived_ref[0].astype(jnp.float32)
    for device in range(1, arrived_ref.shape[0]):
        total += arrived_ref[device].astype(jnp.float32)
    diagonal = lax.broadcasted_iota(jnp.int32, (lines, lines), 0) == lax.broadcasted_iota(
        jnp.int32, (lines, lines), 1
    )
    normed = []
    for half in range(2):
        degrees = total[lines + half : lines + half + 1, :lines]
        degrees += total[lines + half + 2 : lines + half + 3, :lines]
        scale = jnp.where(diagonal, lax.rsqrt(1.0 + degrees), 0.0).sum(axis=1, keepdims=True)
        normed.append(total[:lines, half * feat : (half + 1) * feat] * scale)
    normed = jnp.concatenate(normed, axis=0).astype(jnp.bfloat16)
    line = lax.broadcasted_iota(jnp.int32, (nodes, nodes), 0)
    node = 2 * (line % lines) + line // lines
    chosen = (order_ref[...] == node).astype(jnp.float32).astype(jnp.bfloat16)
    over_rows = (((0,), (0,)), ((), ()))
    ordered = lax.dot_general(
        chosen, normed, over_rows, preferred_element_type=jnp.float32
    ).astype(jnp.bfloat16)
    pre = jnp.dot(ordered, weight_ref[...], preferred_element_type=jnp.float32)
    act_ref[...] = jnp.maximum(pre, 0.0).astype(act_ref.dtype)
    grad_ref[...] = (
        lax.dot_general(
            ordered, cotangent_ref[...], over_rows, preferred_element_type=jnp.float32
        )
        * node_total ** (-0.5)
    )


def packed_groups(coords, counts, values, step_total):
    tiles = values.shape[0]
    rows = tiles // step_total * HALF + META_ROWS
    return pl.pallas_call(
        pack_kernel,
        out_shape=[jax.ShapeDtypeStruct((rows, LANES), jnp.bfloat16)] * step_total,
        in_specs=[VMEM] * 3,
        out_specs=[VMEM] * step_total,
        scratch_shapes=[
            pltpu.VMEM((tiles * HALF, LANES), jnp.float32),
            pltpu.VMEM((META_ROWS, LANES), jnp.float32),
        ],
        compiler_params=PARAMS,
        name="pack",
    )(coords, counts, values)


def scratch_places(groups):
    shape = (groups, META_USED, LANES)
    return [pltpu.VMEM(shape, jnp.int32), pltpu.SMEM(shape, jnp.int32), pltpu.SemaphoreType.DMA]


def own_tiles(self_loop, features, source_degree, group, row_panel):
    panel_rows, feat = features.shape
    per_group = (group.shape[0] - META_ROWS) // HALF
    return pl.pallas_call(
        functools.partial(own_kernel, per_group),
        out_shape=[
            jax.ShapeDtypeStruct((panel_rows, feat), jnp.bfloat16),
            jax.ShapeDtypeStruct((row_panel // 2, 2 * feat + LANES), jnp.float32),
        ],
        in_specs=[SMEM] + [VMEM] * 3,
        out_specs=[VMEM] * 2,
        scratch_shapes=scratch_places(1),
        compiler_params=PARAMS,
        cost_estimate=pl.CostEstimate(
            flops=2 * 24 * TB * TB * feat * 8, bytes_accessed=6 * 1024 * 1024, transcendentals=0
        ),
        name="own_tiles",
    )(self_loop, features, source_degree.reshape(-1, LANES), group)


def moved_tiles(panel, before, groups, columns):
    per_group = (groups[0].shape[0] - META_ROWS) // HALF
    feat = panel.shape[1]
    return pl.pallas_call(
        functools.partial(moved_kernel, per_group),
        out_shape=jax.ShapeDtypeStruct(
            (columns, before.shape[0] // columns + META_ROWS, 2 * feat), jnp.bfloat16
        ),
        in_specs=[VMEM] * (2 + len(groups)),
        out_specs=VMEM,
        scratch_shapes=[pltpu.VMEM(before.shape, jnp.float32)] + scratch_places(len(groups)),
        compiler_params=PARAMS,
        name="moved_tiles",
    )(panel, before, *groups)


def layer(arrived, node_order, weight, cotangent, node_total):
    out_rows, feat = cotangent.shape
    return pl.pallas_call(
        functools.partial(layer_kernel, node_total),
        out_shape=(
            jax.ShapeDtypeStruct((out_rows, feat), jnp.bfloat16),
            jax.ShapeDtypeStruct((feat, feat), jnp.float32),
        ),
        in_specs=[VMEM] * 4,
        out_specs=(VMEM, VMEM),
        compiler_params=PARAMS,
        name="layer",
    )(arrived, node_order, weight, cotangent)


def per_device(
    features, source_degree, tile_coords, tile_counts, tile_values, weight, node_order, cotangent
):
    columns = lax.axis_size("col")
    row_count = lax.psum(1, ROW)
    step_total = min(4, columns)
    tiles = tile_counts.shape[-1]
    panel_rows, feat = features.shape
    out_rows = node_order.shape[-1]
    row_panel = out_rows * columns

    packed = packed_groups(
        tile_coords.reshape(2, tiles),
        tile_counts.reshape(1, tiles),
        tile_values.reshape(tiles, -1),
        step_total,
    )
    arriving = [passed_along(packed[step], "col", -step) for step in range(1, step_total)]
    row_index = lax.axis_index(ROW)
    holder = lax.axis_index("col") == row_index * columns // row_count
    self_start = row_index * row_panel % panel_rows // TB
    self_loop = jnp.stack([holder.astype(jnp.int32), self_start.astype(jnp.int32)])
    panel, before = own_tiles(self_loop, features, source_degree, packed[0], row_panel)
    outgoing = moved_tiles(panel, before, arriving, columns)
    arrived = exchanged(outgoing, "col")
    activations, local_grad = layer(
        arrived, node_order, weight, cotangent, out_rows * row_count * columns
    )
    share = exchanged(local_grad.reshape(lax.psum(1, PLANE), -1, feat), PLANE).sum(0)
    share = to_all(share, "z").sum(0)
    weight_grad = to_all(share, PLANE).reshape(local_grad.shape)
    return (activations, weight_grad)


def solution(mesh):
    rows, columns = mesh.devices.shape
    apart = Mesh(mesh.devices.reshape(2, rows // 2, columns), (*ROW, "col"))
    both = (*ROW, "col")
    in_specs = (
        P("col", None),
        P("col"),
        P(ROW, "col", None, None),
        P(ROW, "col", None),
        P(ROW, "col", None, None),
        P(),
        P(both, None),
        P(both, None),
    )
    out_specs = (P(both, None), P())
    return jax.shard_map(
        per_device, mesh=apart, in_specs=in_specs, out_specs=out_specs, check_vma=False
    )
```

time: 126 us -> 123 us (0.976)
  other arithmetic: 5.99 us -> 0.16 us
  blocking collectives: 84.4 us -> 87.2 us
  waiting for transfers between devices: 2.78 us -> 0.01 us
  Pallas kernels: 7.76 us -> 9.33 us
    unnamed x13 -> x17, local copies, waits for them, and re-layouts: 1.47 us -> 5.46 us
    convert_element_type x1 -> x0, other arithmetic: 3.48 us -> none  [per_device(): scaled = (features.astype(jnp.float32) * lax.rsqrt(1.0 + source_degree.as...]
    all_to_all x4, blocking collectives: 84.4 us -> 87.2 us  [exchanged(): return lax.all_to_all(parts, axis, 0, 0)]
    ppermute x3, waiting for transfers between devices: 2.78 us -> 0.01 us  [passed_along(): return lax.ppermute(value, axis, pairs)]
    pallas_call x2 -> x4, Pallas kernels: 7.76 us -> 9.33 us  [the longest x1 3.49 us: moved_tiles(): pl.pallas_call(functools.partial(moved_kernel, per_group), out_shape=jax....]
    reshape x2 -> x0, local copies, waits for them, and re-layouts: 1.53 us -> none  [the longest x1 1.45 us: per_device(): tile_values.reshape(step_total, per_step, -1)]
  transfers between devices with their start and end apart: 3 -> 3, of which waited for: 2 -> 0; matrix products, arithmetic and copies ran while one was open for 3% -> 0% of each run, Pallas kernels for 0% -> 3%
where the time goes in v3:
time: 123 us
  blocking collectives  87.2 us (71%)
  starting transfers between devices  19.9 us (16%)
  Pallas kernels  9.33 us (8%)
  local copies, waits for them, and re-layouts  5.48 us (4%)
    all_to_all x4, blocking collectives, exchanged(): return lax.all_to_all(parts, axis, 0, 0)  87.2 us
    ppermute x3, starting transfers between devices, passed_along(): return lax.ppermute(value, axis, pairs)  19.9 us
    unnamed x17, local copies, waits for them, and re-layouts  5.46 us
    pallas_call x1, Pallas kernels, moved_tiles(): pl.pallas_call(functools.partial(moved_kernel, per_group), out_shape=jax....  3.49 us
    pallas_call x1, Pallas kernels, own_tiles(): pl.pallas_call(functools.partial(own_kernel, per_group), out_shape=[jax.S...  3.21 us
  transfers between devices with their start and end apart: 3, of which 0 were waited for; matrix products, arithmetic and copies ran while one was open for 0% of the time, Pallas kernels for 3%

profile of v3, /device:TPU:1, one launch (start us, length us, event | category | flops | bytes accessed | tf_op | source)
XLA Modules:
  0.0 122.9 jit_solution(13071519217562354079)
XLA Ops:
  0.6 1.1 copy-done.1
  1.8 0.7 copy-done.5
  2.4 0.7 copy-done.7
  3.1 1.6 %pack.1 = (bf16[784,128]{1,0:T(8,128)(2,1)S(1)}, bf16[784,128]{1,0:T(8,128)(2,1)S(1)}, bf16[784,128]{1,0:T(8,128)(2,1)S(1)}, bf16[784,128]{1,0:T(8,128)(2,1)S(1)}) custom-call(s32[2,96]{1,0:T(2,128)S(1)} %bitcast.11, s32[1,96]{1,0:T(1,128)S(1)} %bitcast.12, bf16[96,4096]{1,0:T(8,128)(2,1)S(1)} %bitcast.8), custom_call_target="tpu_custom_call" | custom-call | tf_op jit(solution)/shard_map/pack/pallas_call | solution.py:191
  4.7 16.1 %collective-permute-start = (bf16[784,128]{1,0:T(8,128)(2,1)S(1)}, bf16[784,128]{1,0:T(8,128)(2,1)S(1)}, u32[]{:S(2)}, u32[]{:S(2)}) collective-permute-start(bf16[784,128]{1,0:T(8,128)(2,1)S(1)} %get-tuple-element.13), channel_id=1, source_target_pairs={{0,15},{1,0},{2,1},{3,2},{4,3},{5,4},{6,5},{7,6},{8,7},{9,8},{10,9... | collective-permute-start | bytes 602120 | tf_op jit(solution)/shard_map/ppermute | solution.py:27
  20.8 1.9 %collective-permute-start.1 = (bf16[784,128]{1,0:T(8,128)(2,1)S(1)}, bf16[784,128]{1,0:T(8,128)(2,1)S(1)}, u32[]{:S(2)}, u32[]{:S(2)}) collective-permute-start(bf16[784,128]{1,0:T(8,128)(2,1)S(1)} %get-tuple-element.14), channel_id=1, source_target_pairs={{0,14},{1,15},{2,0},{3,1},{4,2},{5,3},{6,4},{7,5},{8,6},{9,7},{10,... | collective-permute-start | bytes 602120 | tf_op jit(solution)/shard_map/ppermute | solution.py:27
  22.7 1.9 %collective-permute-start.2 = (bf16[784,128]{1,0:T(8,128)(2,1)S(1)}, bf16[784,128]{1,0:T(8,128)(2,1)S(1)}, u32[]{:S(2)}, u32[]{:S(2)}) collective-permute-start(bf16[784,128]{1,0:T(8,128)(2,1)S(1)} %get-tuple-element.15), channel_id=1, source_target_pairs={{0,13},{1,14},{2,15},{3,0},{4,1},{5,2},{6,3},{7,4},{8,5},{9,6},{10... | collective-permute-start | bytes 602120 | tf_op jit(solution)/shard_map/ppermute | solution.py:27
  24.7 0.1 pad_add_fusion.self_ref
  24.8 1.6 %copy-done = bf16[8192,128]{1,0:T(8,128)(2,1)S(1)} copy-done((bf16[8192,128]{1,0:T(8,128)(2,1)S(1)}, bf16[8192,128]{1,0:T(8,128)(2,1)}, u32[]{:S(2)}) %copy-start) | copy-done | bytes 2097176
  26.4 0.8 copy-done.2
  27.2 3.2 %own_tiles.1 = (bf16[8192,128]{1,0:T(8,128)(2,1)S(1)}, f32[1024,384]{1,0:T(8,128)S(1)}) custom-call(s32[2]{0:T(128)S(1)} %pad_add_fusion.self_ref, bf16[8192,128]{1,0:T(8,128)(2,1)S(1)} %copy-done, s32[64,128]{1,0:T(8,128)S(1)} %bitcast.10, bf16[784,128]{1,0:T(8,128)(2,1)S(1)} %get-tuple-element.10.group), custom_call_target="tpu_custom_call" | custom-call | flops 201326592 | bytes 6291456 | tf_op jit(solution)/shard_map/own_tiles/pallas_call | solution.py:213
  30.4 0.0 collective-permute-done.refs_0_
  30.4 0.0 collective-permute-done.1.refs_1_
  30.4 0.0 collective-permute-done.2.refs_2_
  30.4 0.0 copy-start.3
  30.4 0.0 copy-start.4
  30.4 0.0 copy-start.6
  30.4 3.5 %moved_tiles.1 = bf16[16,80,256]{2,1,0:T(8,128)(2,1)S(1)} custom-call(bf16[8192,128]{1,0:T(8,128)(2,1)S(1)} %get-tuple-element.11.panel_ref, f32[1024,384]{1,0:T(8,128)S(1)} %get-tuple-element.12.before_ref, bf16[784,128]{1,0:T(8,128)(2,1)S(1)} %collective-permute-done.refs_0_, bf16[784,128]{1,0:T(8,128)(2,1)S(1)} %collective-permute-done.1.refs_1_, ...), custom_call_target="tpu_custom_call" | custom-call | tf_op jit(solution)/shard_map/moved_tiles/pallas_call | solution.py:233
  33.9 19.1 %all_to_all.20.arrived_ref = bf16[16,80,256]{2,1,0:T(8,128)(2,1)S(1)} all-to-all(bf16[16,80,256]{2,1,0:T(8,128)(2,1)S(1)} %moved_tiles.1), channel_id=1, replica_groups=mesh['x_hi'=2,'z'=32,'col'=16] {'col'}, dimensions={0} | all-to-all | bytes 1310720 | tf_op jit(solution)/shard_map/all_to_all | solution.py:31
  53.0 1.0 layer.1
  54.0 10.6 %all_to_all.21 = f32[32,4,128]{2,1,0:T(4,128)S(1)} all-to-all(f32[32,4,128]{2,1,0:T(4,128)S(1)} %bitcast.9), channel_id=1, replica_groups=mesh['x_hi'=2,'z'=32,'col'=16] {'x_hi','col'}, dimensions={0} | all-to-all | bytes 131072 | tf_op jit(solution)/shard_map/all_to_all | solution.py:31
  64.6 44.2 %all_to_all.22 = f32[32,4,128]{2,1,0:T(4,128)S(1)} all-to-all(f32[32,4,128]{2,1,0:T(4,128)S(1)} %broadcast_in_dim.4), channel_id=1, replica_groups=mesh['x_hi'=2,'z'=32,'col'=16] {'z'}, dimensions={0} | all-to-all | bytes 131072 | tf_op jit(solution)/shard_map/all_to_all | solution.py:31
  108.9 13.4 %all_to_all.23 = f32[32,4,128]{2,1,0:T(4,128)S(1)} all-to-all(f32[32,4,128]{2,1,0:T(4,128)S(1)} %broadcast_in_dim.5), channel_id=1, replica_groups=mesh['x_hi'=2,'z'=32,'col'=16] {'x_hi','col'}, dimensions={0} | all-to-all | bytes 131072 | tf_op jit(solution)/shard_map/all_to_all | solution.py:31
  122.3 0.6 copy.13
  (12 shorter events, 0.1 us)
Async XLA Ops:
  0.6 1.1 copy-start.1
  1.8 0.7 copy-start.5
  2.4 0.7 copy-start.7
  4.7 25.6 %collective-permute-start = (bf16[784,128]{1,0:T(8,128)(2,1)S(1)}, bf16[784,128]{1,0:T(8,128)(2,1)S(1)}, u32[]{:S(2)}, u32[]{:S(2)}) collective-permute-start(bf16[784,128]{1,0:T(8,128)(2,1)S(1)} %get-tuple-element.13), channel_id=1, source_target_pairs={{0,15},{1,0},{2,1},{3,2},{4,3},{5,4},{6,5},{7,6},{8,7},{9,8},{10,9... | collective-permute-start | bytes 602120 | tf_op jit(solution)/shard_map/ppermute | solution.py:27
  20.8 9.6 %collective-permute-start.1 = (bf16[784,128]{1,0:T(8,128)(2,1)S(1)}, bf16[784,128]{1,0:T(8,128)(2,1)S(1)}, u32[]{:S(2)}, u32[]{:S(2)}) collective-permute-start(bf16[784,128]{1,0:T(8,128)(2,1)S(1)} %get-tuple-element.14), channel_id=1, source_target_pairs={{0,14},{1,15},{2,0},{3,1},{4,2},{5,3},{6,4},{7,5},{8,6},{9,7},{10,... | collective-permute-start | bytes 602120 | tf_op jit(solution)/shard_map/ppermute | solution.py:27
  22.7 7.6 %collective-permute-start.2 = (bf16[784,128]{1,0:T(8,128)(2,1)S(1)}, bf16[784,128]{1,0:T(8,128)(2,1)S(1)}, u32[]{:S(2)}, u32[]{:S(2)}) collective-permute-start(bf16[784,128]{1,0:T(8,128)(2,1)S(1)} %get-tuple-element.15), channel_id=1, source_target_pairs={{0,13},{1,14},{2,15},{3,0},{4,1},{5,2},{6,3},{7,4},{8,5},{9,6},{10... | collective-permute-start | bytes 602120 | tf_op jit(solution)/shard_map/ppermute | solution.py:27
  24.8 1.6 %copy-start = (bf16[8192,128]{1,0:T(8,128)(2,1)S(1)}, bf16[8192,128]{1,0:T(8,128)(2,1)}, u32[]{:S(2)}) copy-start(bf16[8192,128]{1,0:T(8,128)(2,1)} %features_ref.1) | copy-start | bytes 6291460
  26.4 0.8 copy-start.2
  30.4 22.6 %copy-start.3 = (bf16[128,128]{1,0:T(8,128)(2,1)S(1)}, bf16[128,128]{1,0:T(8,128)(2,1)}, u32[]{:S(2)}) copy-start(bf16[128,128]{1,0:T(8,128)(2,1)} %weight_ref.1) | copy-start | bytes 98308
  30.4 22.6 %copy-start.4 = (bf16[128,128]{1,0:T(8,128)(2,1)S(1)}, bf16[128,128]{1,0:T(8,128)(2,1)}, u32[]{:S(2)}) copy-start(bf16[128,128]{1,0:T(8,128)(2,1)} %cotangent_ref.1) | copy-start | bytes 98308
  30.4 22.6 %copy-start.6 = (s32[1,128]{1,0:T(1,128)S(1)}, s32[1,128]{1,0:T(1,128)}, u32[]{:S(2)}) copy-start(s32[1,128]{1,0:T(1,128)} %order_ref.1) | copy-start | bytes 1540

commit v4 on v3

--- a/solution.py
+++ b/solution.py
@@ -12,13 +12,19 @@
 LANES = 2 * TB
 META_ROWS = 16
 META_USED = 8
-UNROLL = 6
+UNROLL = 12
 SELF_UNROLL = 8
-ROW = ("x_hi", "z")
+ROW = ("x_hi", "z_hi", "z_lo")
 PLANE = ("x_hi", "col")
 VMEM = pl.BlockSpec(memory_space=pltpu.VMEM)
+HBM = pl.BlockSpec(memory_space=pltpu.HBM)
 SMEM = pl.BlockSpec(memory_space=pltpu.SMEM)
 PARAMS = pltpu.CompilerParams(vmem_limit_bytes=32 * 1024 * 1024)
+PACK_MIB = 62
+
+
+def limit(mib):
+    return pltpu.CompilerParams(vmem_limit_bytes=mib * 1024 * 1024)
 
 
 def passed_along(value, axis, steps):
@@ -37,6 +43,31 @@
     return exchanged(lax.optimization_barrier(copies), axis)
 
 
+def between(value, pairs):
+    return lax.ppermute(value, "z_hi", pairs)
+
+
+def is_group(*groups):
+    here = lax.axis_index("z_hi")
+    return functools.reduce(jnp.logical_or, [here == group for group in groups])
+
+
+def summed_over_z(share):
+    share = to_all(share, "z_lo").sum(0)
+    joined = share + between(share, [(1, 2), (7, 6)])
+    arrived = [between(joined, [(2, 0)]), between(joined, [(6, 0)])]
+    arrived += [between(share, [(group, 0)]) for group in (3, 5, 4)]
+    return sum(arrived, joined)
+
+
+def spread_over_z(total):
+    second, first, last = (between(total, [(0, group)]) for group in (2, 1, 7))
+    total = jnp.where(is_group(2), second, total)
+    total = jnp.where(is_group(1), first, jnp.where(is_group(7), last, total))
+    total = jnp.where(is_group(3, 6), between(total, [(2, 3), (7, 6)]), total)
+    return jnp.where(is_group(4, 5), between(total, [(3, 4), (6, 5)]), total)
+
+
 def two_parts(value):
     high = value.astype(jnp.bfloat16)
     return high, (value - high.astype(jnp.float32)).astype(jnp.bfloat16)
@@ -49,18 +80,39 @@
     )
 
 
-def pack_kernel(coords_ref, counts_ref, values_ref, *refs):
-    groups, wide, meta = refs[:-2], refs[-2], refs[-1]
+def spread(values_ref, wide, first):
     tiles = values_ref.shape[0]
     for chunk in range(HALF):
         piece = values_ref[:, chunk * LANES : (chunk + 1) * LANES].astype(jnp.float32)
-        wide[pl.ds(chunk, tiles, stride=HALF), :] = piece
+        wide[pl.ds(first + chunk, tiles, stride=HALF), :] = piece
+
+
+def pack_kernel(coords_hbm, counts_hbm, values_hbm, *refs):
+    groups, (coords_ref, counts_ref, values_ref, wide, meta, sems) = refs[:-6], refs[-6:]
+    count = len(groups)
+    tiles = values_hbm.shape[0] // count
+    rows = tiles * HALF
+    copies = [
+        pltpu.make_async_copy(
+            values_hbm.at[pl.ds(index * tiles, tiles)], values_ref.at[index], sems.at[index]
+        )
+        for index in range(count)
+    ]
+    copies.append(pltpu.make_async_copy(coords_hbm, coords_ref, sems.at[count]))
+    copies.append(pltpu.make_async_copy(counts_hbm, counts_ref, sems.at[count + 1]))
+    for copy in copies:
+        copy.start()
     meta[...] = jnp.zeros_like(meta)
-    meta[0:2, :tiles] = coords_ref[...].astype(jnp.float32)
-    meta[2:3, :tiles] = counts_ref[...].astype(jnp.float32)
-    rows = wide.shape[0] // len(groups)
     for index, group in enumerate(groups):
+        copies[index].wait()
+        spread(values_ref.at[index], wide, index * rows)
         group[:rows, :] = wide[index * rows : (index + 1) * rows, :].astype(group.dtype)
+    copies[count].wait()
+    copies[count + 1].wait()
+    slots = counts_ref.shape[1]
+    meta[0:2, :slots] = coords_ref[...].astype(jnp.float32)
+    meta[2:3, :slots] = counts_ref[...].astype(jnp.float32)
+    for group in groups:
         group[rows:, :] = meta[...].astype(group.dtype)
 
 
@@ -186,18 +238,22 @@
 
 
 def packed_groups(coords, counts, values, step_total):
-    tiles = values.shape[0]
-    rows = tiles // step_total * HALF + META_ROWS
+    per_group = values.shape[0] // step_total
+    rows = per_group * HALF
     return pl.pallas_call(
         pack_kernel,
-        out_shape=[jax.ShapeDtypeStruct((rows, LANES), jnp.bfloat16)] * step_total,
-        in_specs=[VMEM] * 3,
+        out_shape=[jax.ShapeDtypeStruct((rows + META_ROWS, LANES), jnp.bfloat16)] * step_total,
+        in_specs=[HBM] * 3,
         out_specs=[VMEM] * step_total,
         scratch_shapes=[
-            pltpu.VMEM((tiles * HALF, LANES), jnp.float32),
+            pltpu.VMEM(coords.shape, jnp.int32),
+            pltpu.VMEM(counts.shape, jnp.int32),
+            pltpu.VMEM((step_total, per_group, values.shape[1]), jnp.bfloat16),
+            pltpu.VMEM((step_total * rows, LANES), jnp.float32),
             pltpu.VMEM((META_ROWS, LANES), jnp.float32),
+            pltpu.SemaphoreType.DMA((step_total + 2,)),
         ],
-        compiler_params=PARAMS,
+        compiler_params=limit(PACK_MIB),
         name="pack",
     )(coords, counts, values)
 
@@ -287,14 +343,14 @@
         arrived, node_order, weight, cotangent, out_rows * row_count * columns
     )
     share = exchanged(local_grad.reshape(lax.psum(1, PLANE), -1, feat), PLANE).sum(0)
-    share = to_all(share, "z").sum(0)
+    share = spread_over_z(summed_over_z(share))
     weight_grad = to_all(share, PLANE).reshape(local_grad.shape)
     return (activations, weight_grad)
 
 
 def solution(mesh):
     rows, columns = mesh.devices.shape
-    apart = Mesh(mesh.devices.reshape(2, rows // 2, columns), (*ROW, "col"))
+    apart = Mesh(mesh.devices.reshape(2, 8, rows // 16, columns), (*ROW, "col"))
     both = (*ROW, "col")
     in_specs = (
         P("col", None),

time: 123 us -> 117 us (0.951)
  blocking collectives: 87.2 us -> 49.6 us
  waiting for transfers between devices: 0.01 us -> 19.4 us
  starting transfers between devices: 19.9 us -> 32.2 us
  local copies, waits for them, and re-layouts: 5.48 us -> 3.94 us
    all_to_all x4, blocking collectives: 87.2 us -> 49.6 us  [exchanged(): return lax.all_to_all(parts, axis, 0, 0)]
    ppermute x0 -> x11, waiting for transfers between devices: none -> 19.4 us  [between(): return lax.ppermute(value, 'z_hi', pairs)]
    ppermute x0 -> x11, starting transfers between devices: none -> 12.3 us  [between(): return lax.ppermute(value, 'z_hi', pairs)]
    pallas_call x1, Pallas kernels: 1.64 us -> 3.39 us  [packed_groups(): pl.pallas_call(pack_kernel, out_shape=[jax.ShapeDtypeStruct((rows + META_...]
    unnamed x17 -> x13, local copies, waits for them, and re-layouts: 5.46 us -> 3.92 us
  transfers between devices with their start and end apart: 3 -> 14, of which waited for: 0 -> 4; matrix products, arithmetic and copies ran while one was open for 0% -> 0% of each run, Pallas kernels for 3% -> 3%
where the time goes in v4:
time: 117 us
  blocking collectives  49.6 us (42%)
  starting transfers between devices  32.2 us (28%)
  waiting for transfers between devices  19.4 us (17%)
  Pallas kernels  10.3 us (9%)
  local copies, waits for them, and re-layouts  3.94 us (3%)
    all_to_all x4, blocking collectives, exchanged(): return lax.all_to_all(parts, axis, 0, 0)  49.6 us
    ppermute x3, starting transfers between devices, passed_along(): return lax.ppermute(value, axis, pairs)  19.9 us
    ppermute x11, waiting for transfers between devices, between(): return lax.ppermute(value, 'z_hi', pairs)  19.4 us
    ppermute x11, starting transfers between devices, between(): return lax.ppermute(value, 'z_hi', pairs)  12.3 us
    unnamed x13, local copies, waits for them, and re-layouts  3.92 us
    pallas_call x1, Pallas kernels, packed_groups(): pl.pallas_call(pack_kernel, out_shape=[jax.ShapeDtypeStruct((rows + META_...  3.39 us
    pallas_call x1, Pallas kernels, own_tiles(): pl.pallas_call(functools.partial(own_kernel, per_group), out_shape=[jax.S...  3.12 us
    pallas_call x1, Pallas kernels, moved_tiles(): pl.pallas_call(functools.partial(moved_kernel, per_group), out_shape=jax....  2.85 us
  transfers between devices with their start and end apart: 14, of which 4 were waited for; matrix products, arithmetic and copies ran while one was open for 0% of the time, Pallas kernels for 3%

profile of v4, /device:TPU:1, one launch (start us, length us, event | category | flops | bytes accessed | tf_op | source)
XLA Modules:
  0.0 116.7 jit_solution(11001132857952920721)
XLA Ops:
  0.6 3.4 %pack.1 = (bf16[784,128]{1,0:T(8,128)(2,1)}, bf16[784,128]{1,0:T(8,128)(2,1)}, bf16[784,128]{1,0:T(8,128)(2,1)}, bf16[784,128]{1,0:T(8,128)(2,1)}) custom-call(s32[2,96]{1,0:T(2,128)} %bitcast.12, s32[1,96]{1,0:T(1,128)} %bitcast.13, bf16[96,4096]{1,0:T(8,128)(2,1)} %bitcast.10), custom_call_target="tpu_custom_call" | custom-call | tf_op jit(solution)/shard_map/pack/pallas_call | solution.py:243
  4.0 16.1 %collective-permute-start = (bf16[784,128]{1,0:T(8,128)(2,1)}, bf16[784,128]{1,0:T(8,128)(2,1)S(1)}, u32[]{:S(2)}, u32[]{:S(2)}) collective-permute-start(bf16[784,128]{1,0:T(8,128)(2,1)} %get-tuple-element.13), channel_id=1, source_target_pairs={{0,15},{1,0},{2,1},{3,2},{4,3},{5,4},{6,5},{7,6},{8,7},{9,8},{10,9... | collective-permute-start | bytes 602120 | tf_op jit(solution)/shard_map/ppermute | solution.py:33
  20.1 1.9 %collective-permute-start.1 = (bf16[784,128]{1,0:T(8,128)(2,1)}, bf16[784,128]{1,0:T(8,128)(2,1)S(1)}, u32[]{:S(2)}, u32[]{:S(2)}) collective-permute-start(bf16[784,128]{1,0:T(8,128)(2,1)} %get-tuple-element.14), channel_id=1, source_target_pairs={{0,14},{1,15},{2,0},{3,1},{4,2},{5,3},{6,4},{7,5},{8,6},{9,7},{10,... | collective-permute-start | bytes 602120 | tf_op jit(solution)/shard_map/ppermute | solution.py:33
  22.0 1.9 %collective-permute-start.2 = (bf16[784,128]{1,0:T(8,128)(2,1)}, bf16[784,128]{1,0:T(8,128)(2,1)S(1)}, u32[]{:S(2)}, u32[]{:S(2)}) collective-permute-start(bf16[784,128]{1,0:T(8,128)(2,1)} %get-tuple-element.15), channel_id=1, source_target_pairs={{0,13},{1,14},{2,15},{3,0},{4,1},{5,2},{6,3},{7,4},{8,5},{9,6},{10... | collective-permute-start | bytes 602120 | tf_op jit(solution)/shard_map/ppermute | solution.py:33
  24.1 1.6 %copy-done = bf16[8192,128]{1,0:T(8,128)(2,1)S(1)} copy-done((bf16[8192,128]{1,0:T(8,128)(2,1)S(1)}, bf16[8192,128]{1,0:T(8,128)(2,1)}, u32[]{:S(2)}) %copy-start) | copy-done | bytes 2097176
  25.7 0.9 copy-done.1
  27.4 3.1 %own_tiles.1 = (bf16[8192,128]{1,0:T(8,128)(2,1)S(1)}, f32[1024,384]{1,0:T(8,128)S(1)}) custom-call(s32[2]{0:T(128)S(1)} %pad_add_fusion.self_ref, bf16[8192,128]{1,0:T(8,128)(2,1)S(1)} %copy-done, s32[64,128]{1,0:T(8,128)S(1)} %bitcast.9, bf16[784,128]{1,0:T(8,128)(2,1)S(1)} %copy-done.1), custom_call_target="tpu_custom_call" | custom-call | flops 201326592 | bytes 6291456 | tf_op jit(solution)/shard_map/own_tiles/pallas_call | solution.py:269
  30.6 2.8 %moved_tiles.1 = bf16[16,80,256]{2,1,0:T(8,128)(2,1)S(1)} custom-call(bf16[8192,128]{1,0:T(8,128)(2,1)S(1)} %get-tuple-element.11.panel_ref, f32[1024,384]{1,0:T(8,128)S(1)} %get-tuple-element.12.before_ref, bf16[784,128]{1,0:T(8,128)(2,1)S(1)} %collective-permute-done.refs_0_, bf16[784,128]{1,0:T(8,128)(2,1)S(1)} %collective-permute-done.1.refs_1_, ...), custom_call_target="tpu_custom_call" | custom-call | tf_op jit(solution)/shard_map/moved_tiles/pallas_call | solution.py:289
  33.4 18.4 %all_to_all.20.arrived_ref = bf16[16,80,256]{2,1,0:T(8,128)(2,1)S(1)} all-to-all(bf16[16,80,256]{2,1,0:T(8,128)(2,1)S(1)} %moved_tiles.1), channel_id=1, replica_groups=mesh['x_hi'=2,'z_hi'=8,'z_lo'=4,'col'=16] {'col'}, dimensions={0} | all-to-all | bytes 1310720 | tf_op jit(solution)/shard_map/all_to_all | solution.py:37
  51.9 1.0 layer.1
  52.9 10.6 %all_to_all.21 = f32[32,4,128]{2,1,0:T(4,128)S(1)} all-to-all(f32[32,4,128]{2,1,0:T(4,128)S(1)} %bitcast.8), channel_id=1, replica_groups=mesh['x_hi'=2,'z_hi'=8,'z_lo'=4,'col'=16] {'x_hi','col'}, dimensions={0} | all-to-all | bytes 131072 | tf_op jit(solution)/shard_map/all_to_all | solution.py:37
  63.5 6.8 %all_to_all.22 = f32[4,4,128]{2,1,0:T(4,128)S(1)} all-to-all(f32[4,4,128]{2,1,0:T(4,128)S(1)} %broadcast_in_dim.4), channel_id=1, replica_groups=mesh['x_hi'=2,'z_hi'=8,'z_lo'=4,'col'=16] {'z_lo'}, dimensions={0} | all-to-all | bytes 16384 | tf_op jit(solution)/shard_map/all_to_all | solution.py:37
  70.9 1.3 %collective-permute-start.6 = (f32[4,128]{1,0:T(4,128)S(1)}, f32[4,128]{1,0:T(4,128)S(1)}, u32[]{:S(2)}, u32[]{:S(2)}) collective-permute-start(f32[4,128]{1,0:T(4,128)S(1)} %reduce_sum.19), channel_id=1, source_target_pairs={{192,0},{193,1},{194,2},{195,3},{196,4},{197,5},{198,6},{199,7},{2... | collective-permute-start | bytes 6152 | tf_op jit(solution)/shard_map/ppermute | solution.py:47
  72.2 1.3 %collective-permute-start.7 = (f32[4,128]{1,0:T(4,128)S(1)}, f32[4,128]{1,0:T(4,128)S(1)}, u32[]{:S(2)}, u32[]{:S(2)}) collective-permute-start(f32[4,128]{1,0:T(4,128)S(1)} %reduce_sum.19), channel_id=1, source_target_pairs={{320,0},{321,1},{322,2},{323,3},{324,4},{325,5},{326,6},{327,7},{3... | collective-permute-start | bytes 6152 | tf_op jit(solution)/shard_map/ppermute | solution.py:47
  73.5 1.3 %collective-permute-start.8 = (f32[4,128]{1,0:T(4,128)S(1)}, f32[4,128]{1,0:T(4,128)S(1)}, u32[]{:S(2)}, u32[]{:S(2)}) collective-permute-start(f32[4,128]{1,0:T(4,128)S(1)} %reduce_sum.19), channel_id=1, source_target_pairs={{256,0},{257,1},{258,2},{259,3},{260,4},{261,5},{262,6},{263,7},{2... | collective-permute-start | bytes 6152 | tf_op jit(solution)/shard_map/ppermute | solution.py:47
  74.8 1.3 %collective-permute-start.4 = (f32[4,128]{1,0:T(4,128)S(1)}, f32[4,128]{1,0:T(4,128)S(1)}, u32[]{:S(2)}, u32[]{:S(2)}) collective-permute-start(f32[4,128]{1,0:T(4,128)S(1)} %add.33), channel_id=1, source_target_pairs={{128,0},{129,1},{130,2},{131,3},{132,4},{133,5},{134,6},{135,7},{1... | collective-permute-start | bytes 6152 | tf_op jit(solution)/shard_map/ppermute | solution.py:47
  76.1 1.3 %collective-permute-start.5 = (f32[4,128]{1,0:T(4,128)S(1)}, f32[4,128]{1,0:T(4,128)S(1)}, u32[]{:S(2)}, u32[]{:S(2)}) collective-permute-start(f32[4,128]{1,0:T(4,128)S(1)} %add.33), channel_id=1, source_target_pairs={{384,0},{385,1},{386,2},{387,3},{388,4},{389,5},{390,6},{391,7},{3... | collective-permute-start | bytes 6152 | tf_op jit(solution)/shard_map/ppermute | solution.py:47
  77.4 11.3 %collective-permute-done.6 = f32[4,128]{1,0:T(4,128)S(1)} collective-permute-done((f32[4,128]{1,0:T(4,128)S(1)}, f32[4,128]{1,0:T(4,128)S(1)}, u32[]{:S(2)}, u32[]{:S(2)}) %collective-permute-start.6) | collective-permute-done | bytes 2080 | tf_op jit(solution)/shard_map/ppermute | solution.py:47
  88.8 1.5 %collective-permute-done.7 = f32[4,128]{1,0:T(4,128)S(1)} collective-permute-done((f32[4,128]{1,0:T(4,128)S(1)}, f32[4,128]{1,0:T(4,128)S(1)}, u32[]{:S(2)}, u32[]{:S(2)}) %collective-permute-start.7) | collective-permute-done | bytes 2080 | tf_op jit(solution)/shard_map/ppermute | solution.py:47
  90.2 5.9 %collective-permute-done.8 = f32[4,128]{1,0:T(4,128)S(1)} collective-permute-done((f32[4,128]{1,0:T(4,128)S(1)}, f32[4,128]{1,0:T(4,128)S(1)}, u32[]{:S(2)}, u32[]{:S(2)}) %collective-permute-start.8) | collective-permute-done | bytes 2080 | tf_op jit(solution)/shard_map/ppermute | solution.py:47
  96.2 1.3 %collective-permute-start.10 = (f32[4,128]{1,0:T(4,128)S(1)}, f32[4,128]{1,0:T(4,128)S(1)}, u32[]{:S(2)}, u32[]{:S(2)}) collective-permute-start(f32[4,128]{1,0:T(4,128)S(1)} %add_add_fusion), channel_id=1, source_target_pairs={{0,448},{1,449},{2,450},{3,451},{4,452},{5,453},{6,454},{7,455},{8... | collective-permute-start | bytes 6152 | tf_op jit(solution)/shard_map/ppermute | solution.py:47
  97.5 1.3 %collective-permute-start.11 = (f32[4,128]{1,0:T(4,128)S(1)}, f32[4,128]{1,0:T(4,128)S(1)}, u32[]{:S(2)}, u32[]{:S(2)}) collective-permute-start(f32[4,128]{1,0:T(4,128)S(1)} %add_add_fusion), channel_id=1, source_target_pairs={{0,128},{1,129},{2,130},{3,131},{4,132},{5,133},{6,134},{7,135},{8... | collective-permute-start | bytes 6152 | tf_op jit(solution)/shard_map/ppermute | solution.py:47
  98.8 1.3 %collective-permute-start.9 = (f32[4,128]{1,0:T(4,128)S(1)}, f32[4,128]{1,0:T(4,128)S(1)}, u32[]{:S(2)}, u32[]{:S(2)}) collective-permute-start(f32[4,128]{1,0:T(4,128)S(1)} %add_add_fusion), channel_id=1, source_target_pairs={{0,64},{1,65},{2,66},{3,67},{4,68},{5,69},{6,70},{7,71},{8,72},{9,... | collective-permute-start | bytes 6152 | tf_op jit(solution)/shard_map/ppermute | solution.py:47
  102.2 13.8 %all_to_all.23 = f32[32,4,128]{2,1,0:T(4,128)S(1)} all-to-all(f32[32,4,128]{2,1,0:T(4,128)S(1)} %broadcast_in_dim.5), channel_id=1, replica_groups=mesh['x_hi'=2,'z_hi'=8,'z_lo'=4,'col'=16] {'x_hi','col'}, dimensions={0} | all-to-all | bytes 131072 | tf_op jit(solution)/shard_map/all_to_all | solution.py:37
  (35 shorter events, 4.3 us)
Async XLA Ops:
  4.0 26.5 %collective-permute-start = (bf16[784,128]{1,0:T(8,128)(2,1)}, bf16[784,128]{1,0:T(8,128)(2,1)S(1)}, u32[]{:S(2)}, u32[]{:S(2)}) collective-permute-start(bf16[784,128]{1,0:T(8,128)(2,1)} %get-tuple-element.13), channel_id=1, source_target_pairs={{0,15},{1,0},{2,1},{3,2},{4,3},{5,4},{6,5},{7,6},{8,7},{9,8},{10,9... | collective-permute-start | bytes 602120 | tf_op jit(solution)/shard_map/ppermute | solution.py:33
  20.1 10.4 %collective-permute-start.1 = (bf16[784,128]{1,0:T(8,128)(2,1)}, bf16[784,128]{1,0:T(8,128)(2,1)S(1)}, u32[]{:S(2)}, u32[]{:S(2)}) collective-permute-start(bf16[784,128]{1,0:T(8,128)(2,1)} %get-tuple-element.14), channel_id=1, source_target_pairs={{0,14},{1,15},{2,0},{3,1},{4,2},{5,3},{6,4},{7,5},{8,6},{9,7},{10,... | collective-permute-start | bytes 602120 | tf_op jit(solution)/shard_map/ppermute | solution.py:33
  22.0 8.5 %collective-permute-start.2 = (bf16[784,128]{1,0:T(8,128)(2,1)}, bf16[784,128]{1,0:T(8,128)(2,1)S(1)}, u32[]{:S(2)}, u32[]{:S(2)}) collective-permute-start(bf16[784,128]{1,0:T(8,128)(2,1)} %get-tuple-element.15), channel_id=1, source_target_pairs={{0,13},{1,14},{2,15},{3,0},{4,1},{5,2},{6,3},{7,4},{8,5},{9,6},{10... | collective-permute-start | bytes 602120 | tf_op jit(solution)/shard_map/ppermute | solution.py:33
  24.1 1.6 %copy-start = (bf16[8192,128]{1,0:T(8,128)(2,1)S(1)}, bf16[8192,128]{1,0:T(8,128)(2,1)}, u32[]{:S(2)}) copy-start(bf16[8192,128]{1,0:T(8,128)(2,1)} %features_ref.1) | copy-start | bytes 6291460
  25.7 0.9 copy-start.1
  26.6 0.8 copy-start.2
  30.5 21.3 %copy-start.3 = (bf16[128,128]{1,0:T(8,128)(2,1)S(1)}, bf16[128,128]{1,0:T(8,128)(2,1)}, u32[]{:S(2)}) copy-start(bf16[128,128]{1,0:T(8,128)(2,1)} %weight_ref.1) | copy-start | bytes 98308
  30.5 21.3 %copy-start.4 = (bf16[128,128]{1,0:T(8,128)(2,1)S(1)}, bf16[128,128]{1,0:T(8,128)(2,1)}, u32[]{:S(2)}) copy-start(bf16[128,128]{1,0:T(8,128)(2,1)} %cotangent_ref.1) | copy-start | bytes 98308
  30.5 21.3 %copy-start.5 = (s32[1,128]{1,0:T(1,128)S(1)}, s32[1,128]{1,0:T(1,128)}, u32[]{:S(2)}) copy-start(s32[1,128]{1,0:T(1,128)} %order_ref.1) | copy-start | bytes 1540
  70.2 4.6 %collective-permute-start.3 = (f32[4,128]{1,0:T(4,128)S(1)}, f32[4,128]{1,0:T(4,128)S(1)}, u32[]{:S(2)}, u32[]{:S(2)}) collective-permute-start(f32[4,128]{1,0:T(4,128)S(1)} %reduce_sum.19), channel_id=1, source_target_pairs={{64,128},{448,384},{65,129},{449,385},{66,130},{450,386},{67,131},... | collective-permute-start | bytes 6152 | tf_op jit(solution)/shard_map/ppermute | solution.py:47
  70.9 17.8 %collective-permute-start.6 = (f32[4,128]{1,0:T(4,128)S(1)}, f32[4,128]{1,0:T(4,128)S(1)}, u32[]{:S(2)}, u32[]{:S(2)}) collective-permute-start(f32[4,128]{1,0:T(4,128)S(1)} %reduce_sum.19), channel_id=1, source_target_pairs={{192,0},{193,1},{194,2},{195,3},{196,4},{197,5},{198,6},{199,7},{2... | collective-permute-start | bytes 6152 | tf_op jit(solution)/shard_map/ppermute | solution.py:47
  72.2 18.0 %collective-permute-start.7 = (f32[4,128]{1,0:T(4,128)S(1)}, f32[4,128]{1,0:T(4,128)S(1)}, u32[]{:S(2)}, u32[]{:S(2)}) collective-permute-start(f32[4,128]{1,0:T(4,128)S(1)} %reduce_sum.19), channel_id=1, source_target_pairs={{320,0},{321,1},{322,2},{323,3},{324,4},{325,5},{326,6},{327,7},{3... | collective-permute-start | bytes 6152 | tf_op jit(solution)/shard_map/ppermute | solution.py:47
  73.5 22.7 %collective-permute-start.8 = (f32[4,128]{1,0:T(4,128)S(1)}, f32[4,128]{1,0:T(4,128)S(1)}, u32[]{:S(2)}, u32[]{:S(2)}) collective-permute-start(f32[4,128]{1,0:T(4,128)S(1)} %reduce_sum.19), channel_id=1, source_target_pairs={{256,0},{257,1},{258,2},{259,3},{260,4},{261,5},{262,6},{263,7},{2... | collective-permute-start | bytes 6152 | tf_op jit(solution)/shard_map/ppermute | solution.py:47
  74.8 21.3 %collective-permute-start.4 = (f32[4,128]{1,0:T(4,128)S(1)}, f32[4,128]{1,0:T(4,128)S(1)}, u32[]{:S(2)}, u32[]{:S(2)}) collective-permute-start(f32[4,128]{1,0:T(4,128)S(1)} %add.33), channel_id=1, source_target_pairs={{128,0},{129,1},{130,2},{131,3},{132,4},{133,5},{134,6},{135,7},{1... | collective-permute-start | bytes 6152 | tf_op jit(solution)/shard_map/ppermute | solution.py:47
  76.1 20.0 %collective-permute-start.5 = (f32[4,128]{1,0:T(4,128)S(1)}, f32[4,128]{1,0:T(4,128)S(1)}, u32[]{:S(2)}, u32[]{:S(2)}) collective-permute-start(f32[4,128]{1,0:T(4,128)S(1)} %add.33), channel_id=1, source_target_pairs={{384,0},{385,1},{386,2},{387,3},{388,4},{389,5},{390,6},{391,7},{3... | collective-permute-start | bytes 6152 | tf_op jit(solution)/shard_map/ppermute | solution.py:47
  96.2 3.9 %collective-permute-start.10 = (f32[4,128]{1,0:T(4,128)S(1)}, f32[4,128]{1,0:T(4,128)S(1)}, u32[]{:S(2)}, u32[]{:S(2)}) collective-permute-start(f32[4,128]{1,0:T(4,128)S(1)} %add_add_fusion), channel_id=1, source_target_pairs={{0,448},{1,449},{2,450},{3,451},{4,452},{5,453},{6,454},{7,455},{8... | collective-permute-start | bytes 6152 | tf_op jit(solution)/shard_map/ppermute | solution.py:47
  97.5 2.6 %collective-permute-start.11 = (f32[4,128]{1,0:T(4,128)S(1)}, f32[4,128]{1,0:T(4,128)S(1)}, u32[]{:S(2)}, u32[]{:S(2)}) collective-permute-start(f32[4,128]{1,0:T(4,128)S(1)} %add_add_fusion), channel_id=1, source_target_pairs={{0,128},{1,129},{2,130},{3,131},{4,132},{5,133},{6,134},{7,135},{8... | collective-permute-start | bytes 6152 | tf_op jit(solution)/shard_map/ppermute | solution.py:47
  98.8 2.0 %collective-permute-start.9 = (f32[4,128]{1,0:T(4,128)S(1)}, f32[4,128]{1,0:T(4,128)S(1)}, u32[]{:S(2)}, u32[]{:S(2)}) collective-permute-start(f32[4,128]{1,0:T(4,128)S(1)} %add_add_fusion), channel_id=1, source_target_pairs={{0,64},{1,65},{2,66},{3,67},{4,68},{5,69},{6,70},{7,71},{8,72},{9,... | collective-permute-start | bytes 6152 | tf_op jit(solution)/shard_map/ppermute | solution.py:47
  100.8 0.7 collective-permute-start.12
  101.5 0.7 collective-permute-start.13

commit v5 on v4

--- a/solution.py
+++ b/solution.py
@@ -54,16 +54,15 @@
 
 def summed_over_z(share):
     share = to_all(share, "z_lo").sum(0)
-    joined = share + between(share, [(1, 2), (7, 6)])
-    arrived = [between(joined, [(2, 0)]), between(joined, [(6, 0)])]
-    arrived += [between(share, [(group, 0)]) for group in (3, 5, 4)]
+    arrived = [between(share, [(group, 1)]) for group in (5, 4, 0)]
+    joined = share + between(share, [(2, 3), (7, 6)])
+    arrived += [between(joined, [(group, 1)]) for group in (6, 3)]
     return sum(arrived, joined)
 
 
 def spread_over_z(total):
-    second, first, last = (between(total, [(0, group)]) for group in (2, 1, 7))
-    total = jnp.where(is_group(2), second, total)
-    total = jnp.where(is_group(1), first, jnp.where(is_group(7), last, total))
+    to_0, to_2, to_7 = (between(total, [(1, group)]) for group in (0, 2, 7))
+    total = jnp.where(is_group(7), to_7, jnp.where(is_group(0), to_0, jnp.where(is_group(2), to_2, total)))
     total = jnp.where(is_group(3, 6), between(total, [(2, 3), (7, 6)]), total)
     return jnp.where(is_group(4, 5), between(total, [(3, 4), (6, 5)]), total)
 

time: 117 us -> 119 us (1.017)
  blocking collectives: 49.6 us -> 51.1 us
    all_to_all x4, blocking collectives: 49.6 us -> 51.1 us  [exchanged(): return lax.all_to_all(parts, axis, 0, 0)]
  transfers between devices with their start and end apart: 14 -> 14, of which waited for: 4 -> 1; matrix products, arithmetic and copies ran while one was open for 0% -> 0% of each run, Pallas kernels for 3% -> 3%
where the time goes in v5:
time: 119 us
  blocking collectives  51.1 us (43%)
  starting transfers between devices  32.5 us (27%)
  waiting for transfers between devices  19.8 us (17%)
  Pallas kernels  10.3 us (9%)
  local copies, waits for them, and re-layouts  3.94 us (3%)
    all_to_all x4, blocking collectives, exchanged(): return lax.all_to_all(parts, axis, 0, 0)  51.1 us
    ppermute x3, starting transfers between devices, passed_along(): return lax.ppermute(value, axis, pairs)  19.9 us
    ppermute x11, waiting for transfers between devices, between(): return lax.ppermute(value, 'z_hi', pairs)  19.8 us
    ppermute x11, starting transfers between devices, between(): return lax.ppermute(value, 'z_hi', pairs)  12.6 us
    unnamed x13, local copies, waits for them, and re-layouts  3.92 us
    pallas_call x1, Pallas kernels, packed_groups(): pl.pallas_call(pack_kernel, out_shape=[jax.ShapeDtypeStruct((rows + META_...  3.39 us
    pallas_call x1, Pallas kernels, own_tiles(): pl.pallas_call(functools.partial(own_kernel, per_group), out_shape=[jax.S...  3.12 us
    pallas_call x1, Pallas kernels, moved_tiles(): pl.pallas_call(functools.partial(moved_kernel, per_group), out_shape=jax....  2.85 us
  transfers between devices with their start and end apart: 14, of which 1 were waited for; matrix products, arithmetic and copies ran while one was open for 0% of the time, Pallas kernels for 3%

profile of v5, /device:TPU:1, one launch (start us, length us, event | category | flops | bytes accessed | tf_op | source)
XLA Modules:
  0.0 118.8 jit_solution(6396478212486144934)
XLA Ops:
  0.6 3.4 %pack.1 = (bf16[784,128]{1,0:T(8,128)(2,1)}, bf16[784,128]{1,0:T(8,128)(2,1)}, bf16[784,128]{1,0:T(8,128)(2,1)}, bf16[784,128]{1,0:T(8,128)(2,1)}) custom-call(s32[2,96]{1,0:T(2,128)} %bitcast.12, s32[1,96]{1,0:T(1,128)} %bitcast.13, bf16[96,4096]{1,0:T(8,128)(2,1)} %bitcast.10), custom_call_target="tpu_custom_call" | custom-call | tf_op jit(solution)/shard_map/pack/pallas_call | solution.py:242
  4.0 16.1 %collective-permute-start = (bf16[784,128]{1,0:T(8,128)(2,1)}, bf16[784,128]{1,0:T(8,128)(2,1)S(1)}, u32[]{:S(2)}, u32[]{:S(2)}) collective-permute-start(bf16[784,128]{1,0:T(8,128)(2,1)} %get-tuple-element.13), channel_id=1, source_target_pairs={{0,15},{1,0},{2,1},{3,2},{4,3},{5,4},{6,5},{7,6},{8,7},{9,8},{10,9... | collective-permute-start | bytes 602120 | tf_op jit(solution)/shard_map/ppermute | solution.py:33
  20.1 1.9 %collective-permute-start.1 = (bf16[784,128]{1,0:T(8,128)(2,1)}, bf16[784,128]{1,0:T(8,128)(2,1)S(1)}, u32[]{:S(2)}, u32[]{:S(2)}) collective-permute-start(bf16[784,128]{1,0:T(8,128)(2,1)} %get-tuple-element.14), channel_id=1, source_target_pairs={{0,14},{1,15},{2,0},{3,1},{4,2},{5,3},{6,4},{7,5},{8,6},{9,7},{10,... | collective-permute-start | bytes 602120 | tf_op jit(solution)/shard_map/ppermute | solution.py:33
  22.0 1.9 %collective-permute-start.2 = (bf16[784,128]{1,0:T(8,128)(2,1)}, bf16[784,128]{1,0:T(8,128)(2,1)S(1)}, u32[]{:S(2)}, u32[]{:S(2)}) collective-permute-start(bf16[784,128]{1,0:T(8,128)(2,1)} %get-tuple-element.15), channel_id=1, source_target_pairs={{0,13},{1,14},{2,15},{3,0},{4,1},{5,2},{6,3},{7,4},{8,5},{9,6},{10... | collective-permute-start | bytes 602120 | tf_op jit(solution)/shard_map/ppermute | solution.py:33
  24.1 1.6 %copy-done = bf16[8192,128]{1,0:T(8,128)(2,1)S(1)} copy-done((bf16[8192,128]{1,0:T(8,128)(2,1)S(1)}, bf16[8192,128]{1,0:T(8,128)(2,1)}, u32[]{:S(2)}) %copy-start) | copy-done | bytes 2097176
  25.7 0.9 copy-done.1
  26.6 0.8 copy-done.2
  27.4 3.1 %own_tiles.1 = (bf16[8192,128]{1,0:T(8,128)(2,1)S(1)}, f32[1024,384]{1,0:T(8,128)S(1)}) custom-call(s32[2]{0:T(128)S(1)} %pad_add_fusion.self_ref, bf16[8192,128]{1,0:T(8,128)(2,1)S(1)} %copy-done, s32[64,128]{1,0:T(8,128)S(1)} %bitcast.9, bf16[784,128]{1,0:T(8,128)(2,1)S(1)} %copy-done.1), custom_call_target="tpu_custom_call" | custom-call | flops 201326592 | bytes 6291456 | tf_op jit(solution)/shard_map/own_tiles/pallas_call | solution.py:268
  30.6 2.8 %moved_tiles.1 = bf16[16,80,256]{2,1,0:T(8,128)(2,1)S(1)} custom-call(bf16[8192,128]{1,0:T(8,128)(2,1)S(1)} %get-tuple-element.11.panel_ref, f32[1024,384]{1,0:T(8,128)S(1)} %get-tuple-element.12.before_ref, bf16[784,128]{1,0:T(8,128)(2,1)S(1)} %collective-permute-done.refs_0_, bf16[784,128]{1,0:T(8,128)(2,1)S(1)} %collective-permute-done.1.refs_1_, ...), custom_call_target="tpu_custom_call" | custom-call | tf_op jit(solution)/shard_map/moved_tiles/pallas_call | solution.py:288
  33.4 18.4 %all_to_all.20.arrived_ref = bf16[16,80,256]{2,1,0:T(8,128)(2,1)S(1)} all-to-all(bf16[16,80,256]{2,1,0:T(8,128)(2,1)S(1)} %moved_tiles.1), channel_id=1, replica_groups=mesh['x_hi'=2,'z_hi'=8,'z_lo'=4,'col'=16] {'col'}, dimensions={0} | all-to-all | bytes 1310720 | tf_op jit(solution)/shard_map/all_to_all | solution.py:37
  51.9 1.0 layer.1
  52.9 10.6 %all_to_all.21 = f32[32,4,128]{2,1,0:T(4,128)S(1)} all-to-all(f32[32,4,128]{2,1,0:T(4,128)S(1)} %bitcast.8), channel_id=1, replica_groups=mesh['x_hi'=2,'z_hi'=8,'z_lo'=4,'col'=16] {'x_hi','col'}, dimensions={0} | all-to-all | bytes 131072 | tf_op jit(solution)/shard_map/all_to_all | solution.py:37
  63.5 6.8 %all_to_all.22 = f32[4,4,128]{2,1,0:T(4,128)S(1)} all-to-all(f32[4,4,128]{2,1,0:T(4,128)S(1)} %broadcast_in_dim.4), channel_id=1, replica_groups=mesh['x_hi'=2,'z_hi'=8,'z_lo'=4,'col'=16] {'z_lo'}, dimensions={0} | all-to-all | bytes 16384 | tf_op jit(solution)/shard_map/all_to_all | solution.py:37
  70.9 0.7 collective-permute-start.4
  71.6 0.7 collective-permute-start.5
  72.2 5.4 %collective-permute-start.6 = (f32[4,128]{1,0:T(4,128)S(1)}, f32[4,128]{1,0:T(4,128)S(1)}, u32[]{:S(2)}, u32[]{:S(2)}) collective-permute-start(f32[4,128]{1,0:T(4,128)S(1)} %reduce_sum.19), channel_id=1, source_target_pairs={{0,64},{1,65},{2,66},{3,67},{4,68},{5,69},{6,70},{7,71},{8,72},{9,... | collective-permute-start | bytes 6152 | tf_op jit(solution)/shard_map/ppermute | solution.py:47
  78.3 0.7 collective-permute-start.8
  79.0 1.3 %collective-permute-start.10 = (f32[4,128]{1,0:T(4,128)S(1)}, f32[4,128]{1,0:T(4,128)S(1)}, u32[]{:S(2)}, u32[]{:S(2)}) collective-permute-start(f32[4,128]{1,0:T(4,128)S(1)} %add_add_fusion), channel_id=1, source_target_pairs={{64,0},{65,1},{66,2},{67,3},{68,4},{69,5},{70,6},{71,7},{72,8},{73... | collective-permute-start | bytes 6152 | tf_op jit(solution)/shard_map/ppermute | solution.py:47
  80.3 0.7 collective-permute-start.11
  81.0 0.7 collective-permute-start.9
  81.7 19.8 %collective-permute-done.10 = f32[4,128]{1,0:T(4,128)S(1)} collective-permute-done((f32[4,128]{1,0:T(4,128)S(1)}, f32[4,128]{1,0:T(4,128)S(1)}, u32[]{:S(2)}, u32[]{:S(2)}) %collective-permute-start.10) | collective-permute-done | bytes 2080 | tf_op jit(solution)/shard_map/ppermute | solution.py:47
  101.5 0.7 collective-permute-start.12
  102.2 0.7 collective-permute-start.13
  102.9 15.3 %all_to_all.23 = f32[32,4,128]{2,1,0:T(4,128)S(1)} all-to-all(f32[32,4,128]{2,1,0:T(4,128)S(1)} %broadcast_in_dim.5), channel_id=1, replica_groups=mesh['x_hi'=2,'z_hi'=8,'z_lo'=4,'col'=16] {'x_hi','col'}, dimensions={0} | all-to-all | bytes 131072 | tf_op jit(solution)/shard_map/all_to_all | solution.py:37
  (35 shorter events, 2.2 us)
Async XLA Ops:
  4.0 26.5 %collective-permute-start = (bf16[784,128]{1,0:T(8,128)(2,1)}, bf16[784,128]{1,0:T(8,128)(2,1)S(1)}, u32[]{:S(2)}, u32[]{:S(2)}) collective-permute-start(bf16[784,128]{1,0:T(8,128)(2,1)} %get-tuple-element.13), channel_id=1, source_target_pairs={{0,15},{1,0},{2,1},{3,2},{4,3},{5,4},{6,5},{7,6},{8,7},{9,8},{10,9... | collective-permute-start | bytes 602120 | tf_op jit(solution)/shard_map/ppermute | solution.py:33
  20.1 10.4 %collective-permute-start.1 = (bf16[784,128]{1,0:T(8,128)(2,1)}, bf16[784,128]{1,0:T(8,128)(2,1)S(1)}, u32[]{:S(2)}, u32[]{:S(2)}) collective-permute-start(bf16[784,128]{1,0:T(8,128)(2,1)} %get-tuple-element.14), channel_id=1, source_target_pairs={{0,14},{1,15},{2,0},{3,1},{4,2},{5,3},{6,4},{7,5},{8,6},{9,7},{10,... | collective-permute-start | bytes 602120 | tf_op jit(solution)/shard_map/ppermute | solution.py:33
  22.0 8.5 %collective-permute-start.2 = (bf16[784,128]{1,0:T(8,128)(2,1)}, bf16[784,128]{1,0:T(8,128)(2,1)S(1)}, u32[]{:S(2)}, u32[]{:S(2)}) collective-permute-start(bf16[784,128]{1,0:T(8,128)(2,1)} %get-tuple-element.15), channel_id=1, source_target_pairs={{0,13},{1,14},{2,15},{3,0},{4,1},{5,2},{6,3},{7,4},{8,5},{9,6},{10... | collective-permute-start | bytes 602120 | tf_op jit(solution)/shard_map/ppermute | solution.py:33
  24.1 1.6 %copy-start = (bf16[8192,128]{1,0:T(8,128)(2,1)S(1)}, bf16[8192,128]{1,0:T(8,128)(2,1)}, u32[]{:S(2)}) copy-start(bf16[8192,128]{1,0:T(8,128)(2,1)} %features_ref.1) | copy-start | bytes 6291460
  25.7 0.9 copy-start.1
  26.6 0.8 copy-start.2
  30.5 21.3 %copy-start.3 = (bf16[128,128]{1,0:T(8,128)(2,1)S(1)}, bf16[128,128]{1,0:T(8,128)(2,1)}, u32[]{:S(2)}) copy-start(bf16[128,128]{1,0:T(8,128)(2,1)} %weight_ref.1) | copy-start | bytes 98308
  30.5 21.3 %copy-start.4 = (bf16[128,128]{1,0:T(8,128)(2,1)S(1)}, bf16[128,128]{1,0:T(8,128)(2,1)}, u32[]{:S(2)}) copy-start(bf16[128,128]{1,0:T(8,128)(2,1)} %cotangent_ref.1) | copy-start | bytes 98308
  30.5 21.3 %copy-start.5 = (s32[1,128]{1,0:T(1,128)S(1)}, s32[1,128]{1,0:T(1,128)}, u32[]{:S(2)}) copy-start(s32[1,128]{1,0:T(1,128)} %order_ref.1) | copy-start | bytes 1540
  70.2 7.4 %collective-permute-start.3 = (f32[4,128]{1,0:T(4,128)S(1)}, f32[4,128]{1,0:T(4,128)S(1)}, u32[]{:S(2)}, u32[]{:S(2)}) collective-permute-start(f32[4,128]{1,0:T(4,128)S(1)} %reduce_sum.19), channel_id=1, source_target_pairs={{128,192},{448,384},{129,193},{449,385},{130,194},{450,386},{131,1... | collective-permute-start | bytes 6152 | tf_op jit(solution)/shard_map/ppermute | solution.py:47
  70.9 8.1 %collective-permute-start.4 = (f32[4,128]{1,0:T(4,128)S(1)}, f32[4,128]{1,0:T(4,128)S(1)}, u32[]{:S(2)}, u32[]{:S(2)}) collective-permute-start(f32[4,128]{1,0:T(4,128)S(1)} %reduce_sum.19), channel_id=1, source_target_pairs={{320,64},{321,65},{322,66},{323,67},{324,68},{325,69},{326,70},{32... | collective-permute-start | bytes 6152 | tf_op jit(solution)/shard_map/ppermute | solution.py:47
  71.6 7.4 %collective-permute-start.5 = (f32[4,128]{1,0:T(4,128)S(1)}, f32[4,128]{1,0:T(4,128)S(1)}, u32[]{:S(2)}, u32[]{:S(2)}) collective-permute-start(f32[4,128]{1,0:T(4,128)S(1)} %reduce_sum.19), channel_id=1, source_target_pairs={{256,64},{257,65},{258,66},{259,67},{260,68},{261,69},{262,70},{26... | collective-permute-start | bytes 6152 | tf_op jit(solution)/shard_map/ppermute | solution.py:47
  72.2 6.7 %collective-permute-start.6 = (f32[4,128]{1,0:T(4,128)S(1)}, f32[4,128]{1,0:T(4,128)S(1)}, u32[]{:S(2)}, u32[]{:S(2)}) collective-permute-start(f32[4,128]{1,0:T(4,128)S(1)} %reduce_sum.19), channel_id=1, source_target_pairs={{0,64},{1,65},{2,66},{3,67},{4,68},{5,69},{6,70},{7,71},{8,72},{9,... | collective-permute-start | bytes 6152 | tf_op jit(solution)/shard_map/ppermute | solution.py:47
  77.6 1.4 %collective-permute-start.7 = (f32[4,128]{1,0:T(4,128)S(1)}, f32[4,128]{1,0:T(4,128)S(1)}, u32[]{:S(2)}, u32[]{:S(2)}) collective-permute-start(f32[4,128]{1,0:T(4,128)S(1)} %add.33), channel_id=1, source_target_pairs={{384,64},{385,65},{386,66},{387,67},{388,68},{389,69},{390,70},{39... | collective-permute-start | bytes 6152 | tf_op jit(solution)/shard_map/ppermute | solution.py:47
  78.3 0.7 collective-permute-start.8
  79.0 22.4 %collective-permute-start.10 = (f32[4,128]{1,0:T(4,128)S(1)}, f32[4,128]{1,0:T(4,128)S(1)}, u32[]{:S(2)}, u32[]{:S(2)}) collective-permute-start(f32[4,128]{1,0:T(4,128)S(1)} %add_add_fusion), channel_id=1, source_target_pairs={{64,0},{65,1},{66,2},{67,3},{68,4},{69,5},{70,6},{71,7},{72,8},{73... | collective-permute-start | bytes 6152 | tf_op jit(solution)/shard_map/ppermute | solution.py:47
  80.3 21.1 %collective-permute-start.11 = (f32[4,128]{1,0:T(4,128)S(1)}, f32[4,128]{1,0:T(4,128)S(1)}, u32[]{:S(2)}, u32[]{:S(2)}) collective-permute-start(f32[4,128]{1,0:T(4,128)S(1)} %add_add_fusion), channel_id=1, source_target_pairs={{64,128},{65,129},{66,130},{67,131},{68,132},{69,133},{70,134},{71... | collective-permute-start | bytes 6152 | tf_op jit(solution)/shard_map/ppermute | solution.py:47
  81.0 20.5 %collective-permute-start.9 = (f32[4,128]{1,0:T(4,128)S(1)}, f32[4,128]{1,0:T(4,128)S(1)}, u32[]{:S(2)}, u32[]{:S(2)}) collective-permute-start(f32[4,128]{1,0:T(4,128)S(1)} %add_add_fusion), channel_id=1, source_target_pairs={{64,448},{65,449},{66,450},{67,451},{68,452},{69,453},{70,454},{71... | collective-permute-start | bytes 6152 | tf_op jit(solution)/shard_map/ppermute | solution.py:47
  101.5 0.7 collective-permute-start.12
  102.2 0.7 collective-permute-start.13

commit v6 on v4

--- a/solution.py
+++ b/solution.py
@@ -54,16 +54,17 @@
 
 def summed_over_z(share):
     share = to_all(share, "z_lo").sum(0)
+    arrived = [between(share, [(group, 0)]) for group in (4, 5, 3)]
     joined = share + between(share, [(1, 2), (7, 6)])
-    arrived = [between(joined, [(2, 0)]), between(joined, [(6, 0)])]
-    arrived += [between(share, [(group, 0)]) for group in (3, 5, 4)]
+    arrived += [between(joined, [(group, 0)]) for group in (6, 2)]
     return sum(arrived, joined)
 
 
 def spread_over_z(total):
     second, first, last = (between(total, [(0, group)]) for group in (2, 1, 7))
-    total = jnp.where(is_group(2), second, total)
-    total = jnp.where(is_group(1), first, jnp.where(is_group(7), last, total))
+    total = jnp.where(
+        is_group(7), last, jnp.where(is_group(1), first, jnp.where(is_group(2), second, total))
+    )
     total = jnp.where(is_group(3, 6), between(total, [(2, 3), (7, 6)]), total)
     return jnp.where(is_group(4, 5), between(total, [(3, 4), (6, 5)]), total)
 

time: 117 us -> 116 us (level)
  waiting for transfers between devices: 19.4 us -> 17.9 us
    ppermute x11, waiting for transfers between devices: 19.4 us -> 17.9 us  [between(): return lax.ppermute(value, 'z_hi', pairs)]
  transfers between devices with their start and end apart: 14 -> 14, of which waited for: 4 -> 3; matrix products, arithmetic and copies ran while one was open for 0% -> 0% of each run, Pallas kernels for 3% -> 3%
where the time goes in v6:
time: 116 us
  blocking collectives  50.2 us (43%)
  starting transfers between devices  32.2 us (28%)
  waiting for transfers between devices  17.9 us (15%)
  Pallas kernels  10.3 us (9%)
  local copies, waits for them, and re-layouts  3.94 us (3%)
    all_to_all x4, blocking collectives, exchanged(): return lax.all_to_all(parts, axis, 0, 0)  50.2 us
    ppermute x3, starting transfers between devices, passed_along(): return lax.ppermute(value, axis, pairs)  19.9 us
    ppermute x11, waiting for transfers between devices, between(): return lax.ppermute(value, 'z_hi', pairs)  17.9 us
    ppermute x11, starting transfers between devices, between(): return lax.ppermute(value, 'z_hi', pairs)  12.3 us
    unnamed x13, local copies, waits for them, and re-layouts  3.92 us
    pallas_call x1, Pallas kernels, packed_groups(): pl.pallas_call(pack_kernel, out_shape=[jax.ShapeDtypeStruct((rows + META_...  3.39 us
    pallas_call x1, Pallas kernels, own_tiles(): pl.pallas_call(functools.partial(own_kernel, per_group), out_shape=[jax.S...  3.12 us
    pallas_call x1, Pallas kernels, moved_tiles(): pl.pallas_call(functools.partial(moved_kernel, per_group), out_shape=jax....  2.85 us
  transfers between devices with their start and end apart: 14, of which 3 were waited for; matrix products, arithmetic and copies ran while one was open for 0% of the time, Pallas kernels for 3%

profile of v6, /device:TPU:1, one launch (start us, length us, event | category | flops | bytes accessed | tf_op | source)
XLA Modules:
  0.0 115.8 jit_solution(14776554128880905820)
XLA Ops:
  0.6 3.4 %pack.1 = (bf16[784,128]{1,0:T(8,128)(2,1)}, bf16[784,128]{1,0:T(8,128)(2,1)}, bf16[784,128]{1,0:T(8,128)(2,1)}, bf16[784,128]{1,0:T(8,128)(2,1)}) custom-call(s32[2,96]{1,0:T(2,128)} %bitcast.12, s32[1,96]{1,0:T(1,128)} %bitcast.13, bf16[96,4096]{1,0:T(8,128)(2,1)} %bitcast.10), custom_call_target="tpu_custom_call" | custom-call | tf_op jit(solution)/shard_map/pack/pallas_call | solution.py:244
  4.0 16.1 %collective-permute-start = (bf16[784,128]{1,0:T(8,128)(2,1)}, bf16[784,128]{1,0:T(8,128)(2,1)S(1)}, u32[]{:S(2)}, u32[]{:S(2)}) collective-permute-start(bf16[784,128]{1,0:T(8,128)(2,1)} %get-tuple-element.13), channel_id=1, source_target_pairs={{0,15},{1,0},{2,1},{3,2},{4,3},{5,4},{6,5},{7,6},{8,7},{9,8},{10,9... | collective-permute-start | bytes 602120 | tf_op jit(solution)/shard_map/ppermute | solution.py:33
  20.1 1.9 %collective-permute-start.1 = (bf16[784,128]{1,0:T(8,128)(2,1)}, bf16[784,128]{1,0:T(8,128)(2,1)S(1)}, u32[]{:S(2)}, u32[]{:S(2)}) collective-permute-start(bf16[784,128]{1,0:T(8,128)(2,1)} %get-tuple-element.14), channel_id=1, source_target_pairs={{0,14},{1,15},{2,0},{3,1},{4,2},{5,3},{6,4},{7,5},{8,6},{9,7},{10,... | collective-permute-start | bytes 602120 | tf_op jit(solution)/shard_map/ppermute | solution.py:33
  22.0 1.9 %collective-permute-start.2 = (bf16[784,128]{1,0:T(8,128)(2,1)}, bf16[784,128]{1,0:T(8,128)(2,1)S(1)}, u32[]{:S(2)}, u32[]{:S(2)}) collective-permute-start(bf16[784,128]{1,0:T(8,128)(2,1)} %get-tuple-element.15), channel_id=1, source_target_pairs={{0,13},{1,14},{2,15},{3,0},{4,1},{5,2},{6,3},{7,4},{8,5},{9,6},{10... | collective-permute-start | bytes 602120 | tf_op jit(solution)/shard_map/ppermute | solution.py:33
  24.1 1.6 %copy-done = bf16[8192,128]{1,0:T(8,128)(2,1)S(1)} copy-done((bf16[8192,128]{1,0:T(8,128)(2,1)S(1)}, bf16[8192,128]{1,0:T(8,128)(2,1)}, u32[]{:S(2)}) %copy-start) | copy-done | bytes 2097176
  25.7 0.9 copy-done.1
  26.6 0.8 copy-done.2
  27.4 3.1 %own_tiles.1 = (bf16[8192,128]{1,0:T(8,128)(2,1)S(1)}, f32[1024,384]{1,0:T(8,128)S(1)}) custom-call(s32[2]{0:T(128)S(1)} %pad_add_fusion.self_ref, bf16[8192,128]{1,0:T(8,128)(2,1)S(1)} %copy-done, s32[64,128]{1,0:T(8,128)S(1)} %bitcast.9, bf16[784,128]{1,0:T(8,128)(2,1)S(1)} %copy-done.1), custom_call_target="tpu_custom_call" | custom-call | flops 201326592 | bytes 6291456 | tf_op jit(solution)/shard_map/own_tiles/pallas_call | solution.py:270
  30.6 2.8 %moved_tiles.1 = bf16[16,80,256]{2,1,0:T(8,128)(2,1)S(1)} custom-call(bf16[8192,128]{1,0:T(8,128)(2,1)S(1)} %get-tuple-element.11.panel_ref, f32[1024,384]{1,0:T(8,128)S(1)} %get-tuple-element.12.before_ref, bf16[784,128]{1,0:T(8,128)(2,1)S(1)} %collective-permute-done.refs_0_, bf16[784,128]{1,0:T(8,128)(2,1)S(1)} %collective-permute-done.1.refs_1_, ...), custom_call_target="tpu_custom_call" | custom-call | tf_op jit(solution)/shard_map/moved_tiles/pallas_call | solution.py:290
  33.4 18.2 %all_to_all.20.arrived_ref = bf16[16,80,256]{2,1,0:T(8,128)(2,1)S(1)} all-to-all(bf16[16,80,256]{2,1,0:T(8,128)(2,1)S(1)} %moved_tiles.1), channel_id=1, replica_groups=mesh['x_hi'=2,'z_hi'=8,'z_lo'=4,'col'=16] {'col'}, dimensions={0} | all-to-all | bytes 1310720 | tf_op jit(solution)/shard_map/all_to_all | solution.py:37
  51.6 1.0 layer.1
  52.6 10.6 %all_to_all.21 = f32[32,4,128]{2,1,0:T(4,128)S(1)} all-to-all(f32[32,4,128]{2,1,0:T(4,128)S(1)} %bitcast.8), channel_id=1, replica_groups=mesh['x_hi'=2,'z_hi'=8,'z_lo'=4,'col'=16] {'x_hi','col'}, dimensions={0} | all-to-all | bytes 131072 | tf_op jit(solution)/shard_map/all_to_all | solution.py:37
  63.2 6.8 %all_to_all.22 = f32[4,4,128]{2,1,0:T(4,128)S(1)} all-to-all(f32[4,4,128]{2,1,0:T(4,128)S(1)} %broadcast_in_dim.4), channel_id=1, replica_groups=mesh['x_hi'=2,'z_hi'=8,'z_lo'=4,'col'=16] {'z_lo'}, dimensions={0} | all-to-all | bytes 16384 | tf_op jit(solution)/shard_map/all_to_all | solution.py:37
  70.7 1.3 %collective-permute-start.4 = (f32[4,128]{1,0:T(4,128)S(1)}, f32[4,128]{1,0:T(4,128)S(1)}, u32[]{:S(2)}, u32[]{:S(2)}) collective-permute-start(f32[4,128]{1,0:T(4,128)S(1)} %reduce_sum.19), channel_id=1, source_target_pairs={{256,0},{257,1},{258,2},{259,3},{260,4},{261,5},{262,6},{263,7},{2... | collective-permute-start | bytes 6152 | tf_op jit(solution)/shard_map/ppermute | solution.py:47
  72.0 1.3 %collective-permute-start.5 = (f32[4,128]{1,0:T(4,128)S(1)}, f32[4,128]{1,0:T(4,128)S(1)}, u32[]{:S(2)}, u32[]{:S(2)}) collective-permute-start(f32[4,128]{1,0:T(4,128)S(1)} %reduce_sum.19), channel_id=1, source_target_pairs={{320,0},{321,1},{322,2},{323,3},{324,4},{325,5},{326,6},{327,7},{3... | collective-permute-start | bytes 6152 | tf_op jit(solution)/shard_map/ppermute | solution.py:47
  73.3 1.3 %collective-permute-start.6 = (f32[4,128]{1,0:T(4,128)S(1)}, f32[4,128]{1,0:T(4,128)S(1)}, u32[]{:S(2)}, u32[]{:S(2)}) collective-permute-start(f32[4,128]{1,0:T(4,128)S(1)} %reduce_sum.19), channel_id=1, source_target_pairs={{192,0},{193,1},{194,2},{195,3},{196,4},{197,5},{198,6},{199,7},{2... | collective-permute-start | bytes 6152 | tf_op jit(solution)/shard_map/ppermute | solution.py:47
  74.6 1.3 %collective-permute-start.7 = (f32[4,128]{1,0:T(4,128)S(1)}, f32[4,128]{1,0:T(4,128)S(1)}, u32[]{:S(2)}, u32[]{:S(2)}) collective-permute-start(f32[4,128]{1,0:T(4,128)S(1)} %add.33), channel_id=1, source_target_pairs={{384,0},{385,1},{386,2},{387,3},{388,4},{389,5},{390,6},{391,7},{3... | collective-permute-start | bytes 6152 | tf_op jit(solution)/shard_map/ppermute | solution.py:47
  75.9 1.3 %collective-permute-start.8 = (f32[4,128]{1,0:T(4,128)S(1)}, f32[4,128]{1,0:T(4,128)S(1)}, u32[]{:S(2)}, u32[]{:S(2)}) collective-permute-start(f32[4,128]{1,0:T(4,128)S(1)} %add.33), channel_id=1, source_target_pairs={{128,0},{129,1},{130,2},{131,3},{132,4},{133,5},{134,6},{135,7},{1... | collective-permute-start | bytes 6152 | tf_op jit(solution)/shard_map/ppermute | solution.py:47
  77.2 16.1 %collective-permute-done.4 = f32[4,128]{1,0:T(4,128)S(1)} collective-permute-done((f32[4,128]{1,0:T(4,128)S(1)}, f32[4,128]{1,0:T(4,128)S(1)}, u32[]{:S(2)}, u32[]{:S(2)}) %collective-permute-start.4) | collective-permute-done | bytes 2080 | tf_op jit(solution)/shard_map/ppermute | solution.py:47
  93.3 1.1 collective-permute-done.7
  94.4 1.3 %collective-permute-start.10 = (f32[4,128]{1,0:T(4,128)S(1)}, f32[4,128]{1,0:T(4,128)S(1)}, u32[]{:S(2)}, u32[]{:S(2)}) collective-permute-start(f32[4,128]{1,0:T(4,128)S(1)} %add_add_fusion), channel_id=1, source_target_pairs={{0,64},{1,65},{2,66},{3,67},{4,68},{5,69},{6,70},{7,71},{8,72},{9,... | collective-permute-start | bytes 6152 | tf_op jit(solution)/shard_map/ppermute | solution.py:47
  95.7 1.3 %collective-permute-start.11 = (f32[4,128]{1,0:T(4,128)S(1)}, f32[4,128]{1,0:T(4,128)S(1)}, u32[]{:S(2)}, u32[]{:S(2)}) collective-permute-start(f32[4,128]{1,0:T(4,128)S(1)} %add_add_fusion), channel_id=1, source_target_pairs={{0,128},{1,129},{2,130},{3,131},{4,132},{5,133},{6,134},{7,135},{8... | collective-permute-start | bytes 6152 | tf_op jit(solution)/shard_map/ppermute | solution.py:47
  97.0 1.3 %collective-permute-start.9 = (f32[4,128]{1,0:T(4,128)S(1)}, f32[4,128]{1,0:T(4,128)S(1)}, u32[]{:S(2)}, u32[]{:S(2)}) collective-permute-start(f32[4,128]{1,0:T(4,128)S(1)} %add_add_fusion), channel_id=1, source_target_pairs={{0,448},{1,449},{2,450},{3,451},{4,452},{5,453},{6,454},{7,455},{8... | collective-permute-start | bytes 6152 | tf_op jit(solution)/shard_map/ppermute | solution.py:47
  100.4 14.7 %all_to_all.23 = f32[32,4,128]{2,1,0:T(4,128)S(1)} all-to-all(f32[32,4,128]{2,1,0:T(4,128)S(1)} %broadcast_in_dim.5), channel_id=1, replica_groups=mesh['x_hi'=2,'z_hi'=8,'z_lo'=4,'col'=16] {'x_hi','col'}, dimensions={0} | all-to-all | bytes 131072 | tf_op jit(solution)/shard_map/all_to_all | solution.py:37
  (35 shorter events, 3.5 us)
Async XLA Ops:
  4.0 26.5 %collective-permute-start = (bf16[784,128]{1,0:T(8,128)(2,1)}, bf16[784,128]{1,0:T(8,128)(2,1)S(1)}, u32[]{:S(2)}, u32[]{:S(2)}) collective-permute-start(bf16[784,128]{1,0:T(8,128)(2,1)} %get-tuple-element.13), channel_id=1, source_target_pairs={{0,15},{1,0},{2,1},{3,2},{4,3},{5,4},{6,5},{7,6},{8,7},{9,8},{10,9... | collective-permute-start | bytes 602120 | tf_op jit(solution)/shard_map/ppermute | solution.py:33
  20.1 10.4 %collective-permute-start.1 = (bf16[784,128]{1,0:T(8,128)(2,1)}, bf16[784,128]{1,0:T(8,128)(2,1)S(1)}, u32[]{:S(2)}, u32[]{:S(2)}) collective-permute-start(bf16[784,128]{1,0:T(8,128)(2,1)} %get-tuple-element.14), channel_id=1, source_target_pairs={{0,14},{1,15},{2,0},{3,1},{4,2},{5,3},{6,4},{7,5},{8,6},{9,7},{10,... | collective-permute-start | bytes 602120 | tf_op jit(solution)/shard_map/ppermute | solution.py:33
  22.0 8.5 %collective-permute-start.2 = (bf16[784,128]{1,0:T(8,128)(2,1)}, bf16[784,128]{1,0:T(8,128)(2,1)S(1)}, u32[]{:S(2)}, u32[]{:S(2)}) collective-permute-start(bf16[784,128]{1,0:T(8,128)(2,1)} %get-tuple-element.15), channel_id=1, source_target_pairs={{0,13},{1,14},{2,15},{3,0},{4,1},{5,2},{6,3},{7,4},{8,5},{9,6},{10... | collective-permute-start | bytes 602120 | tf_op jit(solution)/shard_map/ppermute | solution.py:33
  24.1 1.6 %copy-start = (bf16[8192,128]{1,0:T(8,128)(2,1)S(1)}, bf16[8192,128]{1,0:T(8,128)(2,1)}, u32[]{:S(2)}) copy-start(bf16[8192,128]{1,0:T(8,128)(2,1)} %features_ref.1) | copy-start | bytes 6291460
  25.7 0.9 copy-start.1
  26.6 0.8 copy-start.2
  30.5 21.1 %copy-start.3 = (bf16[128,128]{1,0:T(8,128)(2,1)S(1)}, bf16[128,128]{1,0:T(8,128)(2,1)}, u32[]{:S(2)}) copy-start(bf16[128,128]{1,0:T(8,128)(2,1)} %weight_ref.1) | copy-start | bytes 98308
  30.5 21.1 %copy-start.4 = (bf16[128,128]{1,0:T(8,128)(2,1)S(1)}, bf16[128,128]{1,0:T(8,128)(2,1)}, u32[]{:S(2)}) copy-start(bf16[128,128]{1,0:T(8,128)(2,1)} %cotangent_ref.1) | copy-start | bytes 98308
  30.5 21.1 %copy-start.5 = (s32[1,128]{1,0:T(1,128)S(1)}, s32[1,128]{1,0:T(1,128)}, u32[]{:S(2)}) copy-start(s32[1,128]{1,0:T(1,128)} %order_ref.1) | copy-start | bytes 1540
  70.0 4.6 %collective-permute-start.3 = (f32[4,128]{1,0:T(4,128)S(1)}, f32[4,128]{1,0:T(4,128)S(1)}, u32[]{:S(2)}, u32[]{:S(2)}) collective-permute-start(f32[4,128]{1,0:T(4,128)S(1)} %reduce_sum.19), channel_id=1, source_target_pairs={{64,128},{448,384},{65,129},{449,385},{66,130},{450,386},{67,131},... | collective-permute-start | bytes 6152 | tf_op jit(solution)/shard_map/ppermute | solution.py:47
  70.7 22.7 %collective-permute-start.4 = (f32[4,128]{1,0:T(4,128)S(1)}, f32[4,128]{1,0:T(4,128)S(1)}, u32[]{:S(2)}, u32[]{:S(2)}) collective-permute-start(f32[4,128]{1,0:T(4,128)S(1)} %reduce_sum.19), channel_id=1, source_target_pairs={{256,0},{257,1},{258,2},{259,3},{260,4},{261,5},{262,6},{263,7},{2... | collective-permute-start | bytes 6152 | tf_op jit(solution)/shard_map/ppermute | solution.py:47
  72.0 21.4 %collective-permute-start.5 = (f32[4,128]{1,0:T(4,128)S(1)}, f32[4,128]{1,0:T(4,128)S(1)}, u32[]{:S(2)}, u32[]{:S(2)}) collective-permute-start(f32[4,128]{1,0:T(4,128)S(1)} %reduce_sum.19), channel_id=1, source_target_pairs={{320,0},{321,1},{322,2},{323,3},{324,4},{325,5},{326,6},{327,7},{3... | collective-permute-start | bytes 6152 | tf_op jit(solution)/shard_map/ppermute | solution.py:47
  73.3 20.1 %collective-permute-start.6 = (f32[4,128]{1,0:T(4,128)S(1)}, f32[4,128]{1,0:T(4,128)S(1)}, u32[]{:S(2)}, u32[]{:S(2)}) collective-permute-start(f32[4,128]{1,0:T(4,128)S(1)} %reduce_sum.19), channel_id=1, source_target_pairs={{192,0},{193,1},{194,2},{195,3},{196,4},{197,5},{198,6},{199,7},{2... | collective-permute-start | bytes 6152 | tf_op jit(solution)/shard_map/ppermute | solution.py:47
  74.6 19.8 %collective-permute-start.7 = (f32[4,128]{1,0:T(4,128)S(1)}, f32[4,128]{1,0:T(4,128)S(1)}, u32[]{:S(2)}, u32[]{:S(2)}) collective-permute-start(f32[4,128]{1,0:T(4,128)S(1)} %add.33), channel_id=1, source_target_pairs={{384,0},{385,1},{386,2},{387,3},{388,4},{389,5},{390,6},{391,7},{3... | collective-permute-start | bytes 6152 | tf_op jit(solution)/shard_map/ppermute | solution.py:47
  75.9 18.5 %collective-permute-start.8 = (f32[4,128]{1,0:T(4,128)S(1)}, f32[4,128]{1,0:T(4,128)S(1)}, u32[]{:S(2)}, u32[]{:S(2)}) collective-permute-start(f32[4,128]{1,0:T(4,128)S(1)} %add.33), channel_id=1, source_target_pairs={{128,0},{129,1},{130,2},{131,3},{132,4},{133,5},{134,6},{135,7},{1... | collective-permute-start | bytes 6152 | tf_op jit(solution)/shard_map/ppermute | solution.py:47
  94.4 3.9 %collective-permute-start.10 = (f32[4,128]{1,0:T(4,128)S(1)}, f32[4,128]{1,0:T(4,128)S(1)}, u32[]{:S(2)}, u32[]{:S(2)}) collective-permute-start(f32[4,128]{1,0:T(4,128)S(1)} %add_add_fusion), channel_id=1, source_target_pairs={{0,64},{1,65},{2,66},{3,67},{4,68},{5,69},{6,70},{7,71},{8,72},{9,... | collective-permute-start | bytes 6152 | tf_op jit(solution)/shard_map/ppermute | solution.py:47
  95.7 2.6 %collective-permute-start.11 = (f32[4,128]{1,0:T(4,128)S(1)}, f32[4,128]{1,0:T(4,128)S(1)}, u32[]{:S(2)}, u32[]{:S(2)}) collective-permute-start(f32[4,128]{1,0:T(4,128)S(1)} %add_add_fusion), channel_id=1, source_target_pairs={{0,128},{1,129},{2,130},{3,131},{4,132},{5,133},{6,134},{7,135},{8... | collective-permute-start | bytes 6152 | tf_op jit(solution)/shard_map/ppermute | solution.py:47
  97.0 2.0 %collective-permute-start.9 = (f32[4,128]{1,0:T(4,128)S(1)}, f32[4,128]{1,0:T(4,128)S(1)}, u32[]{:S(2)}, u32[]{:S(2)}) collective-permute-start(f32[4,128]{1,0:T(4,128)S(1)} %add_add_fusion), channel_id=1, source_target_pairs={{0,448},{1,449},{2,450},{3,451},{4,452},{5,453},{6,454},{7,455},{8... | collective-permute-start | bytes 6152 | tf_op jit(solution)/shard_map/ppermute | solution.py:47
  99.0 0.7 collective-permute-start.12
  99.7 0.7 collective-permute-start.13

commit v7 on v6

--- a/solution.py
+++ b/solution.py
@@ -15,7 +15,7 @@
 UNROLL = 12
 SELF_UNROLL = 8
 ROW = ("x_hi", "z_hi", "z_lo")
-PLANE = ("x_hi", "col")
+NEAR = ("x_hi", "z_lo")
 VMEM = pl.BlockSpec(memory_space=pltpu.VMEM)
 HBM = pl.BlockSpec(memory_space=pltpu.HBM)
 SMEM = pl.BlockSpec(memory_space=pltpu.SMEM)
@@ -53,7 +53,7 @@
 
 
 def summed_over_z(share):
-    share = to_all(share, "z_lo").sum(0)
+    share = to_all(share, NEAR).sum(0)
     arrived = [between(share, [(group, 0)]) for group in (4, 5, 3)]
     joined = share + between(share, [(1, 2), (7, 6)])
     arrived += [between(joined, [(group, 0)]) for group in (6, 2)]
@@ -343,9 +343,9 @@
     activations, local_grad = layer(
         arrived, node_order, weight, cotangent, out_rows * row_count * columns
     )
-    share = exchanged(local_grad.reshape(lax.psum(1, PLANE), -1, feat), PLANE).sum(0)
+    share = exchanged(local_grad.reshape(columns, -1, feat), "col").sum(0)
     share = spread_over_z(summed_over_z(share))
-    weight_grad = to_all(share, PLANE).reshape(local_grad.shape)
+    weight_grad = to_all(share, "col").reshape(local_grad.shape)
     return (activations, weight_grad)
 
 

time: 116 us -> 116 us (level)
  transfers between devices with their start and end apart: 14 -> 14, of which waited for: 3 -> 3; matrix products, arithmetic and copies ran while one was open for 0% -> 0% of each run, Pallas kernels for 3% -> 2%
where the time goes in v7:
time: 116 us; the launch traced here: 115 us
  blocking collectives  49.4 us (43%)
  starting transfers between devices  32.2 us (28%)
  waiting for transfers between devices  18.6 us (16%)
  Pallas kernels  10.1 us (9%)
  local copies, waits for them, and re-layouts  3.94 us (3%)
    all_to_all x4, blocking collectives, exchanged(): return lax.all_to_all(parts, axis, 0, 0)  49.4 us
    ppermute x3, starting transfers between devices, passed_along(): return lax.ppermute(value, axis, pairs)  19.9 us
    ppermute x11, waiting for transfers between devices, between(): return lax.ppermute(value, 'z_hi', pairs)  18.5 us
    ppermute x11, starting transfers between devices, between(): return lax.ppermute(value, 'z_hi', pairs)  12.3 us
    unnamed x13, local copies, waits for them, and re-layouts  3.92 us
    pallas_call x1, Pallas kernels, packed_groups(): pl.pallas_call(pack_kernel, out_shape=[jax.ShapeDtypeStruct((rows + META_...  3.39 us
    pallas_call x1, Pallas kernels, own_tiles(): pl.pallas_call(functools.partial(own_kernel, per_group), out_shape=[jax.S...  2.88 us
    pallas_call x1, Pallas kernels, moved_tiles(): pl.pallas_call(functools.partial(moved_kernel, per_group), out_shape=jax....  2.85 us
  transfers between devices with their start and end apart: 14, of which 3 were waited for; matrix products, arithmetic and copies ran while one was open for 0% of the time, Pallas kernels for 2%

profile of v7, /device:TPU:1, one launch (start us, length us, event | category | flops | bytes accessed | tf_op | source)
XLA Modules:
  0.0 115.3 jit_solution(7065204281457869156)
XLA Ops:
  0.6 3.4 %pack.1 = (bf16[784,128]{1,0:T(8,128)(2,1)}, bf16[784,128]{1,0:T(8,128)(2,1)}, bf16[784,128]{1,0:T(8,128)(2,1)}, bf16[784,128]{1,0:T(8,128)(2,1)}) custom-call(s32[2,96]{1,0:T(2,128)} %bitcast.12, s32[1,96]{1,0:T(1,128)} %bitcast.13, bf16[96,4096]{1,0:T(8,128)(2,1)} %bitcast.10), custom_call_target="tpu_custom_call" | custom-call | tf_op jit(solution)/shard_map/pack/pallas_call | solution.py:244
  4.0 16.1 %collective-permute-start = (bf16[784,128]{1,0:T(8,128)(2,1)}, bf16[784,128]{1,0:T(8,128)(2,1)S(1)}, u32[]{:S(2)}, u32[]{:S(2)}) collective-permute-start(bf16[784,128]{1,0:T(8,128)(2,1)} %get-tuple-element.13), channel_id=1, source_target_pairs={{0,15},{1,0},{2,1},{3,2},{4,3},{5,4},{6,5},{7,6},{8,7},{9,8},{10,9... | collective-permute-start | bytes 602120 | tf_op jit(solution)/shard_map/ppermute | solution.py:33
  20.1 1.9 %collective-permute-start.1 = (bf16[784,128]{1,0:T(8,128)(2,1)}, bf16[784,128]{1,0:T(8,128)(2,1)S(1)}, u32[]{:S(2)}, u32[]{:S(2)}) collective-permute-start(bf16[784,128]{1,0:T(8,128)(2,1)} %get-tuple-element.14), channel_id=1, source_target_pairs={{0,14},{1,15},{2,0},{3,1},{4,2},{5,3},{6,4},{7,5},{8,6},{9,7},{10,... | collective-permute-start | bytes 602120 | tf_op jit(solution)/shard_map/ppermute | solution.py:33
  22.0 1.9 %collective-permute-start.2 = (bf16[784,128]{1,0:T(8,128)(2,1)}, bf16[784,128]{1,0:T(8,128)(2,1)S(1)}, u32[]{:S(2)}, u32[]{:S(2)}) collective-permute-start(bf16[784,128]{1,0:T(8,128)(2,1)} %get-tuple-element.15), channel_id=1, source_target_pairs={{0,13},{1,14},{2,15},{3,0},{4,1},{5,2},{6,3},{7,4},{8,5},{9,6},{10... | collective-permute-start | bytes 602120 | tf_op jit(solution)/shard_map/ppermute | solution.py:33
  24.1 1.6 %copy-done = bf16[8192,128]{1,0:T(8,128)(2,1)S(1)} copy-done((bf16[8192,128]{1,0:T(8,128)(2,1)S(1)}, bf16[8192,128]{1,0:T(8,128)(2,1)}, u32[]{:S(2)}) %copy-start) | copy-done | bytes 2097176
  25.7 0.9 copy-done.1
  26.6 0.8 copy-done.2
  27.4 2.9 %own_tiles.1 = (bf16[8192,128]{1,0:T(8,128)(2,1)S(1)}, f32[1024,384]{1,0:T(8,128)S(1)}) custom-call(s32[2]{0:T(128)S(1)} %pad_add_fusion.self_ref, bf16[8192,128]{1,0:T(8,128)(2,1)S(1)} %copy-done, s32[64,128]{1,0:T(8,128)S(1)} %bitcast.9, bf16[784,128]{1,0:T(8,128)(2,1)S(1)} %copy-done.1), custom_call_target="tpu_custom_call" | custom-call | flops 201326592 | bytes 6291456 | tf_op jit(solution)/shard_map/own_tiles/pallas_call | solution.py:270
  30.3 2.8 %moved_tiles.1 = bf16[16,80,256]{2,1,0:T(8,128)(2,1)S(1)} custom-call(bf16[8192,128]{1,0:T(8,128)(2,1)S(1)} %get-tuple-element.11.panel_ref, f32[1024,384]{1,0:T(8,128)S(1)} %get-tuple-element.12.before_ref, bf16[784,128]{1,0:T(8,128)(2,1)S(1)} %collective-permute-done.refs_0_, bf16[784,128]{1,0:T(8,128)(2,1)S(1)} %collective-permute-done.1.refs_1_, ...), custom_call_target="tpu_custom_call" | custom-call | tf_op jit(solution)/shard_map/moved_tiles/pallas_call | solution.py:290
  33.2 18.4 %all_to_all.20.arrived_ref = bf16[16,80,256]{2,1,0:T(8,128)(2,1)S(1)} all-to-all(bf16[16,80,256]{2,1,0:T(8,128)(2,1)S(1)} %moved_tiles.1), channel_id=1, replica_groups=mesh['x_hi'=2,'z_hi'=8,'z_lo'=4,'col'=16] {'col'}, dimensions={0} | all-to-all | bytes 1310720 | tf_op jit(solution)/shard_map/all_to_all | solution.py:37
  51.6 1.0 layer.1
  52.6 8.9 %all_to_all.21 = f32[16,8,128]{2,1,0:T(8,128)S(1)} all-to-all(f32[16,8,128]{2,1,0:T(8,128)S(1)} %bitcast.8), channel_id=1, replica_groups=mesh['x_hi'=2,'z_hi'=8,'z_lo'=4,'col'=16] {'col'}, dimensions={0} | all-to-all | bytes 131072 | tf_op jit(solution)/shard_map/all_to_all | solution.py:37
  61.6 9.5 %all_to_all.22 = f32[8,8,128]{2,1,0:T(8,128)S(1)} all-to-all(f32[8,8,128]{2,1,0:T(8,128)S(1)} %broadcast_in_dim.4), channel_id=1, replica_groups=mesh['x_hi'=2,'z_hi'=8,'z_lo'=4,'col'=16] {'x_hi','z_lo'}, dimensions={0} | all-to-all | bytes 65536 | tf_op jit(solution)/shard_map/all_to_all | solution.py:37
  71.8 1.3 %collective-permute-start.4 = (f32[8,128]{1,0:T(8,128)S(1)}, f32[8,128]{1,0:T(8,128)S(1)}, u32[]{:S(2)}, u32[]{:S(2)}) collective-permute-start(f32[8,128]{1,0:T(8,128)S(1)} %reduce_sum.19), channel_id=1, source_target_pairs={{256,0},{257,1},{258,2},{259,3},{260,4},{261,5},{262,6},{263,7},{2... | collective-permute-start | bytes 12296 | tf_op jit(solution)/shard_map/ppermute | solution.py:47
  73.1 1.3 %collective-permute-start.5 = (f32[8,128]{1,0:T(8,128)S(1)}, f32[8,128]{1,0:T(8,128)S(1)}, u32[]{:S(2)}, u32[]{:S(2)}) collective-permute-start(f32[8,128]{1,0:T(8,128)S(1)} %reduce_sum.19), channel_id=1, source_target_pairs={{320,0},{321,1},{322,2},{323,3},{324,4},{325,5},{326,6},{327,7},{3... | collective-permute-start | bytes 12296 | tf_op jit(solution)/shard_map/ppermute | solution.py:47
  74.4 1.3 %collective-permute-start.6 = (f32[8,128]{1,0:T(8,128)S(1)}, f32[8,128]{1,0:T(8,128)S(1)}, u32[]{:S(2)}, u32[]{:S(2)}) collective-permute-start(f32[8,128]{1,0:T(8,128)S(1)} %reduce_sum.19), channel_id=1, source_target_pairs={{192,0},{193,1},{194,2},{195,3},{196,4},{197,5},{198,6},{199,7},{2... | collective-permute-start | bytes 12296 | tf_op jit(solution)/shard_map/ppermute | solution.py:47
  75.7 1.3 %collective-permute-start.7 = (f32[8,128]{1,0:T(8,128)S(1)}, f32[8,128]{1,0:T(8,128)S(1)}, u32[]{:S(2)}, u32[]{:S(2)}) collective-permute-start(f32[8,128]{1,0:T(8,128)S(1)} %add.33), channel_id=1, source_target_pairs={{384,0},{385,1},{386,2},{387,3},{388,4},{389,5},{390,6},{391,7},{3... | collective-permute-start | bytes 12296 | tf_op jit(solution)/shard_map/ppermute | solution.py:47
  77.0 1.3 %collective-permute-start.8 = (f32[8,128]{1,0:T(8,128)S(1)}, f32[8,128]{1,0:T(8,128)S(1)}, u32[]{:S(2)}, u32[]{:S(2)}) collective-permute-start(f32[8,128]{1,0:T(8,128)S(1)} %add.33), channel_id=1, source_target_pairs={{128,0},{129,1},{130,2},{131,3},{132,4},{133,5},{134,6},{135,7},{1... | collective-permute-start | bytes 12296 | tf_op jit(solution)/shard_map/ppermute | solution.py:47
  78.3 16.2 %collective-permute-done.4 = f32[8,128]{1,0:T(8,128)S(1)} collective-permute-done((f32[8,128]{1,0:T(8,128)S(1)}, f32[8,128]{1,0:T(8,128)S(1)}, u32[]{:S(2)}, u32[]{:S(2)}) %collective-permute-start.4) | collective-permute-done | bytes 4128 | tf_op jit(solution)/shard_map/ppermute | solution.py:47
  94.5 1.6 %collective-permute-done.7 = f32[8,128]{1,0:T(8,128)S(1)} collective-permute-done((f32[8,128]{1,0:T(8,128)S(1)}, f32[8,128]{1,0:T(8,128)S(1)}, u32[]{:S(2)}, u32[]{:S(2)}) %collective-permute-start.7) | collective-permute-done | bytes 4128 | tf_op jit(solution)/shard_map/ppermute | solution.py:47
  96.1 1.3 %collective-permute-start.10 = (f32[8,128]{1,0:T(8,128)S(1)}, f32[8,128]{1,0:T(8,128)S(1)}, u32[]{:S(2)}, u32[]{:S(2)}) collective-permute-start(f32[8,128]{1,0:T(8,128)S(1)} %add_add_fusion), channel_id=1, source_target_pairs={{0,64},{1,65},{2,66},{3,67},{4,68},{5,69},{6,70},{7,71},{8,72},{9,... | collective-permute-start | bytes 12296 | tf_op jit(solution)/shard_map/ppermute | solution.py:47
  97.4 1.3 %collective-permute-start.11 = (f32[8,128]{1,0:T(8,128)S(1)}, f32[8,128]{1,0:T(8,128)S(1)}, u32[]{:S(2)}, u32[]{:S(2)}) collective-permute-start(f32[8,128]{1,0:T(8,128)S(1)} %add_add_fusion), channel_id=1, source_target_pairs={{0,128},{1,129},{2,130},{3,131},{4,132},{5,133},{6,134},{7,135},{8... | collective-permute-start | bytes 12296 | tf_op jit(solution)/shard_map/ppermute | solution.py:47
  98.7 1.3 %collective-permute-start.9 = (f32[8,128]{1,0:T(8,128)S(1)}, f32[8,128]{1,0:T(8,128)S(1)}, u32[]{:S(2)}, u32[]{:S(2)}) collective-permute-start(f32[8,128]{1,0:T(8,128)S(1)} %add_add_fusion), channel_id=1, source_target_pairs={{0,448},{1,449},{2,450},{3,451},{4,452},{5,453},{6,454},{7,455},{8... | collective-permute-start | bytes 12296 | tf_op jit(solution)/shard_map/ppermute | solution.py:47
  102.2 12.4 %all_to_all.23 = f32[16,8,128]{2,1,0:T(8,128)S(1)} all-to-all(f32[16,8,128]{2,1,0:T(8,128)S(1)} %broadcast_in_dim.5), channel_id=1, replica_groups=mesh['x_hi'=2,'z_hi'=8,'z_lo'=4,'col'=16] {'col'}, dimensions={0} | all-to-all | bytes 131072 | tf_op jit(solution)/shard_map/all_to_all | solution.py:37
  (35 shorter events, 3.5 us)
Async XLA Ops:
  4.0 26.2 %collective-permute-start = (bf16[784,128]{1,0:T(8,128)(2,1)}, bf16[784,128]{1,0:T(8,128)(2,1)S(1)}, u32[]{:S(2)}, u32[]{:S(2)}) collective-permute-start(bf16[784,128]{1,0:T(8,128)(2,1)} %get-tuple-element.13), channel_id=1, source_target_pairs={{0,15},{1,0},{2,1},{3,2},{4,3},{5,4},{6,5},{7,6},{8,7},{9,8},{10,9... | collective-permute-start | bytes 602120 | tf_op jit(solution)/shard_map/ppermute | solution.py:33
  20.1 10.2 %collective-permute-start.1 = (bf16[784,128]{1,0:T(8,128)(2,1)}, bf16[784,128]{1,0:T(8,128)(2,1)S(1)}, u32[]{:S(2)}, u32[]{:S(2)}) collective-permute-start(bf16[784,128]{1,0:T(8,128)(2,1)} %get-tuple-element.14), channel_id=1, source_target_pairs={{0,14},{1,15},{2,0},{3,1},{4,2},{5,3},{6,4},{7,5},{8,6},{9,7},{10,... | collective-permute-start | bytes 602120 | tf_op jit(solution)/shard_map/ppermute | solution.py:33
  22.0 8.2 %collective-permute-start.2 = (bf16[784,128]{1,0:T(8,128)(2,1)}, bf16[784,128]{1,0:T(8,128)(2,1)S(1)}, u32[]{:S(2)}, u32[]{:S(2)}) collective-permute-start(bf16[784,128]{1,0:T(8,128)(2,1)} %get-tuple-element.15), channel_id=1, source_target_pairs={{0,13},{1,14},{2,15},{3,0},{4,1},{5,2},{6,3},{7,4},{8,5},{9,6},{10... | collective-permute-start | bytes 602120 | tf_op jit(solution)/shard_map/ppermute | solution.py:33
  24.1 1.6 %copy-start = (bf16[8192,128]{1,0:T(8,128)(2,1)S(1)}, bf16[8192,128]{1,0:T(8,128)(2,1)}, u32[]{:S(2)}) copy-start(bf16[8192,128]{1,0:T(8,128)(2,1)} %features_ref.1) | copy-start | bytes 6291460
  25.7 0.9 copy-start.1
  26.6 0.8 copy-start.2
  30.3 21.3 %copy-start.3 = (bf16[128,128]{1,0:T(8,128)(2,1)S(1)}, bf16[128,128]{1,0:T(8,128)(2,1)}, u32[]{:S(2)}) copy-start(bf16[128,128]{1,0:T(8,128)(2,1)} %weight_ref.1) | copy-start | bytes 98308
  30.3 21.3 %copy-start.4 = (bf16[128,128]{1,0:T(8,128)(2,1)S(1)}, bf16[128,128]{1,0:T(8,128)(2,1)}, u32[]{:S(2)}) copy-start(bf16[128,128]{1,0:T(8,128)(2,1)} %cotangent_ref.1) | copy-start | bytes 98308
  30.3 21.3 %copy-start.5 = (s32[1,128]{1,0:T(1,128)S(1)}, s32[1,128]{1,0:T(1,128)}, u32[]{:S(2)}) copy-start(s32[1,128]{1,0:T(1,128)} %order_ref.1) | copy-start | bytes 1540
  71.1 4.6 %collective-permute-start.3 = (f32[8,128]{1,0:T(8,128)S(1)}, f32[8,128]{1,0:T(8,128)S(1)}, u32[]{:S(2)}, u32[]{:S(2)}) collective-permute-start(f32[8,128]{1,0:T(8,128)S(1)} %reduce_sum.19), channel_id=1, source_target_pairs={{64,128},{448,384},{65,129},{449,385},{66,130},{450,386},{67,131},... | collective-permute-start | bytes 12296 | tf_op jit(solution)/shard_map/ppermute | solution.py:47
  71.8 22.7 %collective-permute-start.4 = (f32[8,128]{1,0:T(8,128)S(1)}, f32[8,128]{1,0:T(8,128)S(1)}, u32[]{:S(2)}, u32[]{:S(2)}) collective-permute-start(f32[8,128]{1,0:T(8,128)S(1)} %reduce_sum.19), channel_id=1, source_target_pairs={{256,0},{257,1},{258,2},{259,3},{260,4},{261,5},{262,6},{263,7},{2... | collective-permute-start | bytes 12296 | tf_op jit(solution)/shard_map/ppermute | solution.py:47
  73.1 21.4 %collective-permute-start.5 = (f32[8,128]{1,0:T(8,128)S(1)}, f32[8,128]{1,0:T(8,128)S(1)}, u32[]{:S(2)}, u32[]{:S(2)}) collective-permute-start(f32[8,128]{1,0:T(8,128)S(1)} %reduce_sum.19), channel_id=1, source_target_pairs={{320,0},{321,1},{322,2},{323,3},{324,4},{325,5},{326,6},{327,7},{3... | collective-permute-start | bytes 12296 | tf_op jit(solution)/shard_map/ppermute | solution.py:47
  74.4 20.1 %collective-permute-start.6 = (f32[8,128]{1,0:T(8,128)S(1)}, f32[8,128]{1,0:T(8,128)S(1)}, u32[]{:S(2)}, u32[]{:S(2)}) collective-permute-start(f32[8,128]{1,0:T(8,128)S(1)} %reduce_sum.19), channel_id=1, source_target_pairs={{192,0},{193,1},{194,2},{195,3},{196,4},{197,5},{198,6},{199,7},{2... | collective-permute-start | bytes 12296 | tf_op jit(solution)/shard_map/ppermute | solution.py:47
  75.7 20.4 %collective-permute-start.7 = (f32[8,128]{1,0:T(8,128)S(1)}, f32[8,128]{1,0:T(8,128)S(1)}, u32[]{:S(2)}, u32[]{:S(2)}) collective-permute-start(f32[8,128]{1,0:T(8,128)S(1)} %add.33), channel_id=1, source_target_pairs={{384,0},{385,1},{386,2},{387,3},{388,4},{389,5},{390,6},{391,7},{3... | collective-permute-start | bytes 12296 | tf_op jit(solution)/shard_map/ppermute | solution.py:47
  77.0 19.1 %collective-permute-start.8 = (f32[8,128]{1,0:T(8,128)S(1)}, f32[8,128]{1,0:T(8,128)S(1)}, u32[]{:S(2)}, u32[]{:S(2)}) collective-permute-start(f32[8,128]{1,0:T(8,128)S(1)} %add.33), channel_id=1, source_target_pairs={{128,0},{129,1},{130,2},{131,3},{132,4},{133,5},{134,6},{135,7},{1... | collective-permute-start | bytes 12296 | tf_op jit(solution)/shard_map/ppermute | solution.py:47
  96.1 3.9 %collective-permute-start.10 = (f32[8,128]{1,0:T(8,128)S(1)}, f32[8,128]{1,0:T(8,128)S(1)}, u32[]{:S(2)}, u32[]{:S(2)}) collective-permute-start(f32[8,128]{1,0:T(8,128)S(1)} %add_add_fusion), channel_id=1, source_target_pairs={{0,64},{1,65},{2,66},{3,67},{4,68},{5,69},{6,70},{7,71},{8,72},{9,... | collective-permute-start | bytes 12296 | tf_op jit(solution)/shard_map/ppermute | solution.py:47
  97.4 2.6 %collective-permute-start.11 = (f32[8,128]{1,0:T(8,128)S(1)}, f32[8,128]{1,0:T(8,128)S(1)}, u32[]{:S(2)}, u32[]{:S(2)}) collective-permute-start(f32[8,128]{1,0:T(8,128)S(1)} %add_add_fusion), channel_id=1, source_target_pairs={{0,128},{1,129},{2,130},{3,131},{4,132},{5,133},{6,134},{7,135},{8... | collective-permute-start | bytes 12296 | tf_op jit(solution)/shard_map/ppermute | solution.py:47
  98.7 2.0 %collective-permute-start.9 = (f32[8,128]{1,0:T(8,128)S(1)}, f32[8,128]{1,0:T(8,128)S(1)}, u32[]{:S(2)}, u32[]{:S(2)}) collective-permute-start(f32[8,128]{1,0:T(8,128)S(1)} %add_add_fusion), channel_id=1, source_target_pairs={{0,448},{1,449},{2,450},{3,451},{4,452},{5,453},{6,454},{7,455},{8... | collective-permute-start | bytes 12296 | tf_op jit(solution)/shard_map/ppermute | solution.py:47
  100.8 0.7 collective-permute-start.12
  101.5 0.7 collective-permute-start.13

commit v8 on v7

--- a/solution.py
+++ b/solution.py
@@ -53,11 +53,10 @@
 
 
 def summed_over_z(share):
-    share = to_all(share, NEAR).sum(0)
     arrived = [between(share, [(group, 0)]) for group in (4, 5, 3)]
     joined = share + between(share, [(1, 2), (7, 6)])
     arrived += [between(joined, [(group, 0)]) for group in (6, 2)]
-    return sum(arrived, joined)
+    return to_all(sum(arrived, joined), NEAR).sum(0)
 
 
 def spread_over_z(total):

time: 116 us -> 116 us (level)
  waiting for transfers between devices: 18.6 us -> 17 us
  blocking collectives: 49.4 us -> 50.7 us
    ppermute x11, waiting for transfers between devices: 18.5 us -> 17 us  [between(): return lax.ppermute(value, 'z_hi', pairs)]
    all_to_all x4, blocking collectives: 49.4 us -> 50.7 us  [exchanged(): return lax.all_to_all(parts, axis, 0, 0)]
  transfers between devices with their start and end apart: 14 -> 14, of which waited for: 3 -> 2; matrix products, arithmetic and copies ran while one was open for 0% -> 0% of each run, Pallas kernels for 2% -> 3%
where the time goes in v8:
time: 116 us; the launch traced here: 115 us
  blocking collectives  50.7 us (44%)
  starting transfers between devices  32.2 us (28%)
  waiting for transfers between devices  17 us (15%)
  Pallas kernels  10.3 us (9%)
  local copies, waits for them, and re-layouts  3.94 us (3%)
    all_to_all x4, blocking collectives, exchanged(): return lax.all_to_all(parts, axis, 0, 0)  50.7 us
    ppermute x3, starting transfers between devices, passed_along(): return lax.ppermute(value, axis, pairs)  19.9 us
    ppermute x11, waiting for transfers between devices, between(): return lax.ppermute(value, 'z_hi', pairs)  17 us
    ppermute x11, starting transfers between devices, between(): return lax.ppermute(value, 'z_hi', pairs)  12.3 us
    unnamed x13, local copies, waits for them, and re-layouts  3.92 us
    pallas_call x1, Pallas kernels, packed_groups(): pl.pallas_call(pack_kernel, out_shape=[jax.ShapeDtypeStruct((rows + META_...  3.39 us
    pallas_call x1, Pallas kernels, own_tiles(): pl.pallas_call(functools.partial(own_kernel, per_group), out_shape=[jax.S...  3.12 us
    pallas_call x1, Pallas kernels, moved_tiles(): pl.pallas_call(functools.partial(moved_kernel, per_group), out_shape=jax....  2.85 us
  transfers between devices with their start and end apart: 14, of which 2 were waited for; matrix products, arithmetic and copies ran while one was open for 0% of the time, Pallas kernels for 3%

profile of v8, /device:TPU:1, one launch (start us, length us, event | category | flops | bytes accessed | tf_op | source)
XLA Modules:
  0.0 115.3 jit_solution(15126647519574803565)
XLA Ops:
  0.6 3.4 %pack.1 = (bf16[784,128]{1,0:T(8,128)(2,1)}, bf16[784,128]{1,0:T(8,128)(2,1)}, bf16[784,128]{1,0:T(8,128)(2,1)}, bf16[784,128]{1,0:T(8,128)(2,1)}) custom-call(s32[2,96]{1,0:T(2,128)} %bitcast.12, s32[1,96]{1,0:T(1,128)} %bitcast.13, bf16[96,4096]{1,0:T(8,128)(2,1)} %bitcast.10), custom_call_target="tpu_custom_call" | custom-call | tf_op jit(solution)/shard_map/pack/pallas_call | solution.py:243
  4.0 16.1 %collective-permute-start = (bf16[784,128]{1,0:T(8,128)(2,1)}, bf16[784,128]{1,0:T(8,128)(2,1)S(1)}, u32[]{:S(2)}, u32[]{:S(2)}) collective-permute-start(bf16[784,128]{1,0:T(8,128)(2,1)} %get-tuple-element.13), channel_id=1, source_target_pairs={{0,15},{1,0},{2,1},{3,2},{4,3},{5,4},{6,5},{7,6},{8,7},{9,8},{10,9... | collective-permute-start | bytes 602120 | tf_op jit(solution)/shard_map/ppermute | solution.py:33
  20.1 1.9 %collective-permute-start.1 = (bf16[784,128]{1,0:T(8,128)(2,1)}, bf16[784,128]{1,0:T(8,128)(2,1)S(1)}, u32[]{:S(2)}, u32[]{:S(2)}) collective-permute-start(bf16[784,128]{1,0:T(8,128)(2,1)} %get-tuple-element.14), channel_id=1, source_target_pairs={{0,14},{1,15},{2,0},{3,1},{4,2},{5,3},{6,4},{7,5},{8,6},{9,7},{10,... | collective-permute-start | bytes 602120 | tf_op jit(solution)/shard_map/ppermute | solution.py:33
  22.0 1.9 %collective-permute-start.2 = (bf16[784,128]{1,0:T(8,128)(2,1)}, bf16[784,128]{1,0:T(8,128)(2,1)S(1)}, u32[]{:S(2)}, u32[]{:S(2)}) collective-permute-start(bf16[784,128]{1,0:T(8,128)(2,1)} %get-tuple-element.15), channel_id=1, source_target_pairs={{0,13},{1,14},{2,15},{3,0},{4,1},{5,2},{6,3},{7,4},{8,5},{9,6},{10... | collective-permute-start | bytes 602120 | tf_op jit(solution)/shard_map/ppermute | solution.py:33
  24.1 1.6 %copy-done = bf16[8192,128]{1,0:T(8,128)(2,1)S(1)} copy-done((bf16[8192,128]{1,0:T(8,128)(2,1)S(1)}, bf16[8192,128]{1,0:T(8,128)(2,1)}, u32[]{:S(2)}) %copy-start) | copy-done | bytes 2097176
  25.7 0.9 copy-done.1
  26.6 0.8 copy-done.2
  27.4 3.1 %own_tiles.1 = (bf16[8192,128]{1,0:T(8,128)(2,1)S(1)}, f32[1024,384]{1,0:T(8,128)S(1)}) custom-call(s32[2]{0:T(128)S(1)} %pad_add_fusion.self_ref, bf16[8192,128]{1,0:T(8,128)(2,1)S(1)} %copy-done, s32[64,128]{1,0:T(8,128)S(1)} %bitcast.9, bf16[784,128]{1,0:T(8,128)(2,1)S(1)} %copy-done.1), custom_call_target="tpu_custom_call" | custom-call | flops 201326592 | bytes 6291456 | tf_op jit(solution)/shard_map/own_tiles/pallas_call | solution.py:269
  30.6 2.8 %moved_tiles.1 = bf16[16,80,256]{2,1,0:T(8,128)(2,1)S(1)} custom-call(bf16[8192,128]{1,0:T(8,128)(2,1)S(1)} %get-tuple-element.11.panel_ref, f32[1024,384]{1,0:T(8,128)S(1)} %get-tuple-element.12.before_ref, bf16[784,128]{1,0:T(8,128)(2,1)S(1)} %collective-permute-done.refs_0_, bf16[784,128]{1,0:T(8,128)(2,1)S(1)} %collective-permute-done.1.refs_1_, ...), custom_call_target="tpu_custom_call" | custom-call | tf_op jit(solution)/shard_map/moved_tiles/pallas_call | solution.py:289
  33.4 18.4 %all_to_all.20.arrived_ref = bf16[16,80,256]{2,1,0:T(8,128)(2,1)S(1)} all-to-all(bf16[16,80,256]{2,1,0:T(8,128)(2,1)S(1)} %moved_tiles.1), channel_id=1, replica_groups=mesh['x_hi'=2,'z_hi'=8,'z_lo'=4,'col'=16] {'col'}, dimensions={0} | all-to-all | bytes 1310720 | tf_op jit(solution)/shard_map/all_to_all | solution.py:37
  51.9 1.0 layer.1
  52.9 8.9 %all_to_all.21 = f32[16,8,128]{2,1,0:T(8,128)S(1)} all-to-all(f32[16,8,128]{2,1,0:T(8,128)S(1)} %bitcast.8), channel_id=1, replica_groups=mesh['x_hi'=2,'z_hi'=8,'z_lo'=4,'col'=16] {'col'}, dimensions={0} | all-to-all | bytes 131072 | tf_op jit(solution)/shard_map/all_to_all | solution.py:37
  62.5 1.3 %collective-permute-start.4 = (f32[8,128]{1,0:T(8,128)S(1)}, f32[8,128]{1,0:T(8,128)S(1)}, u32[]{:S(2)}, u32[]{:S(2)}) collective-permute-start(f32[8,128]{1,0:T(8,128)S(1)} %reduce_sum.18), channel_id=1, source_target_pairs={{256,0},{257,1},{258,2},{259,3},{260,4},{261,5},{262,6},{263,7},{2... | collective-permute-start | bytes 12296 | tf_op jit(solution)/shard_map/ppermute | solution.py:47
  63.8 1.3 %collective-permute-start.5 = (f32[8,128]{1,0:T(8,128)S(1)}, f32[8,128]{1,0:T(8,128)S(1)}, u32[]{:S(2)}, u32[]{:S(2)}) collective-permute-start(f32[8,128]{1,0:T(8,128)S(1)} %reduce_sum.18), channel_id=1, source_target_pairs={{320,0},{321,1},{322,2},{323,3},{324,4},{325,5},{326,6},{327,7},{3... | collective-permute-start | bytes 12296 | tf_op jit(solution)/shard_map/ppermute | solution.py:47
  65.1 1.3 %collective-permute-start.6 = (f32[8,128]{1,0:T(8,128)S(1)}, f32[8,128]{1,0:T(8,128)S(1)}, u32[]{:S(2)}, u32[]{:S(2)}) collective-permute-start(f32[8,128]{1,0:T(8,128)S(1)} %reduce_sum.18), channel_id=1, source_target_pairs={{192,0},{193,1},{194,2},{195,3},{196,4},{197,5},{198,6},{199,7},{2... | collective-permute-start | bytes 12296 | tf_op jit(solution)/shard_map/ppermute | solution.py:47
  66.4 1.3 %collective-permute-start.7 = (f32[8,128]{1,0:T(8,128)S(1)}, f32[8,128]{1,0:T(8,128)S(1)}, u32[]{:S(2)}, u32[]{:S(2)}) collective-permute-start(f32[8,128]{1,0:T(8,128)S(1)} %add.33), channel_id=1, source_target_pairs={{384,0},{385,1},{386,2},{387,3},{388,4},{389,5},{390,6},{391,7},{3... | collective-permute-start | bytes 12296 | tf_op jit(solution)/shard_map/ppermute | solution.py:47
  67.7 1.3 %collective-permute-start.8 = (f32[8,128]{1,0:T(8,128)S(1)}, f32[8,128]{1,0:T(8,128)S(1)}, u32[]{:S(2)}, u32[]{:S(2)}) collective-permute-start(f32[8,128]{1,0:T(8,128)S(1)} %add.33), channel_id=1, source_target_pairs={{128,0},{129,1},{130,2},{131,3},{132,4},{133,5},{134,6},{135,7},{1... | collective-permute-start | bytes 12296 | tf_op jit(solution)/shard_map/ppermute | solution.py:47
  69.0 16.3 %collective-permute-done.4 = f32[8,128]{1,0:T(8,128)S(1)} collective-permute-done((f32[8,128]{1,0:T(8,128)S(1)}, f32[8,128]{1,0:T(8,128)S(1)}, u32[]{:S(2)}, u32[]{:S(2)}) %collective-permute-start.4) | collective-permute-done | bytes 4128 | tf_op jit(solution)/shard_map/ppermute | solution.py:47
  85.3 10.6 %all_to_all.22 = f32[8,8,128]{2,1,0:T(8,128)S(1)} all-to-all(f32[8,8,128]{2,1,0:T(8,128)S(1)} %broadcast_in_dim.4), channel_id=1, replica_groups=mesh['x_hi'=2,'z_hi'=8,'z_lo'=4,'col'=16] {'x_hi','z_lo'}, dimensions={0} | all-to-all | bytes 65536 | tf_op jit(solution)/shard_map/all_to_all | solution.py:37
  95.9 1.3 %collective-permute-start.10 = (f32[8,128]{1,0:T(8,128)S(1)}, f32[8,128]{1,0:T(8,128)S(1)}, u32[]{:S(2)}, u32[]{:S(2)}) collective-permute-start(f32[8,128]{1,0:T(8,128)S(1)} %reduce_sum.19), channel_id=1, source_target_pairs={{0,64},{1,65},{2,66},{3,67},{4,68},{5,69},{6,70},{7,71},{8,72},{9,... | collective-permute-start | bytes 12296 | tf_op jit(solution)/shard_map/ppermute | solution.py:47
  97.2 1.3 %collective-permute-start.11 = (f32[8,128]{1,0:T(8,128)S(1)}, f32[8,128]{1,0:T(8,128)S(1)}, u32[]{:S(2)}, u32[]{:S(2)}) collective-permute-start(f32[8,128]{1,0:T(8,128)S(1)} %reduce_sum.19), channel_id=1, source_target_pairs={{0,128},{1,129},{2,130},{3,131},{4,132},{5,133},{6,134},{7,135},{8... | collective-permute-start | bytes 12296 | tf_op jit(solution)/shard_map/ppermute | solution.py:47
  98.5 1.3 %collective-permute-start.9 = (f32[8,128]{1,0:T(8,128)S(1)}, f32[8,128]{1,0:T(8,128)S(1)}, u32[]{:S(2)}, u32[]{:S(2)}) collective-permute-start(f32[8,128]{1,0:T(8,128)S(1)} %reduce_sum.19), channel_id=1, source_target_pairs={{0,448},{1,449},{2,450},{3,451},{4,452},{5,453},{6,454},{7,455},{8... | collective-permute-start | bytes 12296 | tf_op jit(solution)/shard_map/ppermute | solution.py:47
  99.8 0.7 collective-permute-done.9
  101.9 12.7 %all_to_all.23 = f32[16,8,128]{2,1,0:T(8,128)S(1)} all-to-all(f32[16,8,128]{2,1,0:T(8,128)S(1)} %broadcast_in_dim.5), channel_id=1, replica_groups=mesh['x_hi'=2,'z_hi'=8,'z_lo'=4,'col'=16] {'col'}, dimensions={0} | all-to-all | bytes 131072 | tf_op jit(solution)/shard_map/all_to_all | solution.py:37
  (35 shorter events, 2.8 us)
Async XLA Ops:
  4.0 26.5 %collective-permute-start = (bf16[784,128]{1,0:T(8,128)(2,1)}, bf16[784,128]{1,0:T(8,128)(2,1)S(1)}, u32[]{:S(2)}, u32[]{:S(2)}) collective-permute-start(bf16[784,128]{1,0:T(8,128)(2,1)} %get-tuple-element.13), channel_id=1, source_target_pairs={{0,15},{1,0},{2,1},{3,2},{4,3},{5,4},{6,5},{7,6},{8,7},{9,8},{10,9... | collective-permute-start | bytes 602120 | tf_op jit(solution)/shard_map/ppermute | solution.py:33
  20.1 10.4 %collective-permute-start.1 = (bf16[784,128]{1,0:T(8,128)(2,1)}, bf16[784,128]{1,0:T(8,128)(2,1)S(1)}, u32[]{:S(2)}, u32[]{:S(2)}) collective-permute-start(bf16[784,128]{1,0:T(8,128)(2,1)} %get-tuple-element.14), channel_id=1, source_target_pairs={{0,14},{1,15},{2,0},{3,1},{4,2},{5,3},{6,4},{7,5},{8,6},{9,7},{10,... | collective-permute-start | bytes 602120 | tf_op jit(solution)/shard_map/ppermute | solution.py:33
  22.0 8.5 %collective-permute-start.2 = (bf16[784,128]{1,0:T(8,128)(2,1)}, bf16[784,128]{1,0:T(8,128)(2,1)S(1)}, u32[]{:S(2)}, u32[]{:S(2)}) collective-permute-start(bf16[784,128]{1,0:T(8,128)(2,1)} %get-tuple-element.15), channel_id=1, source_target_pairs={{0,13},{1,14},{2,15},{3,0},{4,1},{5,2},{6,3},{7,4},{8,5},{9,6},{10... | collective-permute-start | bytes 602120 | tf_op jit(solution)/shard_map/ppermute | solution.py:33
  24.1 1.6 %copy-start = (bf16[8192,128]{1,0:T(8,128)(2,1)S(1)}, bf16[8192,128]{1,0:T(8,128)(2,1)}, u32[]{:S(2)}) copy-start(bf16[8192,128]{1,0:T(8,128)(2,1)} %features_ref.1) | copy-start | bytes 6291460
  25.7 0.9 copy-start.1
  26.6 0.8 copy-start.2
  30.5 21.3 %copy-start.3 = (bf16[128,128]{1,0:T(8,128)(2,1)S(1)}, bf16[128,128]{1,0:T(8,128)(2,1)}, u32[]{:S(2)}) copy-start(bf16[128,128]{1,0:T(8,128)(2,1)} %weight_ref.1) | copy-start | bytes 98308
  30.5 21.3 %copy-start.4 = (bf16[128,128]{1,0:T(8,128)(2,1)S(1)}, bf16[128,128]{1,0:T(8,128)(2,1)}, u32[]{:S(2)}) copy-start(bf16[128,128]{1,0:T(8,128)(2,1)} %cotangent_ref.1) | copy-start | bytes 98308
  30.5 21.3 %copy-start.5 = (s32[1,128]{1,0:T(1,128)S(1)}, s32[1,128]{1,0:T(1,128)}, u32[]{:S(2)}) copy-start(s32[1,128]{1,0:T(1,128)} %order_ref.1) | copy-start | bytes 1540
  61.8 4.6 %collective-permute-start.3 = (f32[8,128]{1,0:T(8,128)S(1)}, f32[8,128]{1,0:T(8,128)S(1)}, u32[]{:S(2)}, u32[]{:S(2)}) collective-permute-start(f32[8,128]{1,0:T(8,128)S(1)} %reduce_sum.18), channel_id=1, source_target_pairs={{64,128},{448,384},{65,129},{449,385},{66,130},{450,386},{67,131},... | collective-permute-start | bytes 12296 | tf_op jit(solution)/shard_map/ppermute | solution.py:47
  62.5 22.8 %collective-permute-start.4 = (f32[8,128]{1,0:T(8,128)S(1)}, f32[8,128]{1,0:T(8,128)S(1)}, u32[]{:S(2)}, u32[]{:S(2)}) collective-permute-start(f32[8,128]{1,0:T(8,128)S(1)} %reduce_sum.18), channel_id=1, source_target_pairs={{256,0},{257,1},{258,2},{259,3},{260,4},{261,5},{262,6},{263,7},{2... | collective-permute-start | bytes 12296 | tf_op jit(solution)/shard_map/ppermute | solution.py:47
  63.8 21.5 %collective-permute-start.5 = (f32[8,128]{1,0:T(8,128)S(1)}, f32[8,128]{1,0:T(8,128)S(1)}, u32[]{:S(2)}, u32[]{:S(2)}) collective-permute-start(f32[8,128]{1,0:T(8,128)S(1)} %reduce_sum.18), channel_id=1, source_target_pairs={{320,0},{321,1},{322,2},{323,3},{324,4},{325,5},{326,6},{327,7},{3... | collective-permute-start | bytes 12296 | tf_op jit(solution)/shard_map/ppermute | solution.py:47
  65.1 20.2 %collective-permute-start.6 = (f32[8,128]{1,0:T(8,128)S(1)}, f32[8,128]{1,0:T(8,128)S(1)}, u32[]{:S(2)}, u32[]{:S(2)}) collective-permute-start(f32[8,128]{1,0:T(8,128)S(1)} %reduce_sum.18), channel_id=1, source_target_pairs={{192,0},{193,1},{194,2},{195,3},{196,4},{197,5},{198,6},{199,7},{2... | collective-permute-start | bytes 12296 | tf_op jit(solution)/shard_map/ppermute | solution.py:47
  66.4 18.9 %collective-permute-start.7 = (f32[8,128]{1,0:T(8,128)S(1)}, f32[8,128]{1,0:T(8,128)S(1)}, u32[]{:S(2)}, u32[]{:S(2)}) collective-permute-start(f32[8,128]{1,0:T(8,128)S(1)} %add.33), channel_id=1, source_target_pairs={{384,0},{385,1},{386,2},{387,3},{388,4},{389,5},{390,6},{391,7},{3... | collective-permute-start | bytes 12296 | tf_op jit(solution)/shard_map/ppermute | solution.py:47
  67.7 17.6 %collective-permute-start.8 = (f32[8,128]{1,0:T(8,128)S(1)}, f32[8,128]{1,0:T(8,128)S(1)}, u32[]{:S(2)}, u32[]{:S(2)}) collective-permute-start(f32[8,128]{1,0:T(8,128)S(1)} %add.33), channel_id=1, source_target_pairs={{128,0},{129,1},{130,2},{131,3},{132,4},{133,5},{134,6},{135,7},{1... | collective-permute-start | bytes 12296 | tf_op jit(solution)/shard_map/ppermute | solution.py:47
  95.9 3.9 %collective-permute-start.10 = (f32[8,128]{1,0:T(8,128)S(1)}, f32[8,128]{1,0:T(8,128)S(1)}, u32[]{:S(2)}, u32[]{:S(2)}) collective-permute-start(f32[8,128]{1,0:T(8,128)S(1)} %reduce_sum.19), channel_id=1, source_target_pairs={{0,64},{1,65},{2,66},{3,67},{4,68},{5,69},{6,70},{7,71},{8,72},{9,... | collective-permute-start | bytes 12296 | tf_op jit(solution)/shard_map/ppermute | solution.py:47
  97.2 2.6 %collective-permute-start.11 = (f32[8,128]{1,0:T(8,128)S(1)}, f32[8,128]{1,0:T(8,128)S(1)}, u32[]{:S(2)}, u32[]{:S(2)}) collective-permute-start(f32[8,128]{1,0:T(8,128)S(1)} %reduce_sum.19), channel_id=1, source_target_pairs={{0,128},{1,129},{2,130},{3,131},{4,132},{5,133},{6,134},{7,135},{8... | collective-permute-start | bytes 12296 | tf_op jit(solution)/shard_map/ppermute | solution.py:47
  98.5 2.0 %collective-permute-start.9 = (f32[8,128]{1,0:T(8,128)S(1)}, f32[8,128]{1,0:T(8,128)S(1)}, u32[]{:S(2)}, u32[]{:S(2)}) collective-permute-start(f32[8,128]{1,0:T(8,128)S(1)} %reduce_sum.19), channel_id=1, source_target_pairs={{0,448},{1,449},{2,450},{3,451},{4,452},{5,453},{6,454},{7,455},{8... | collective-permute-start | bytes 12296 | tf_op jit(solution)/shard_map/ppermute | solution.py:47
  100.5 0.7 collective-permute-start.12
  101.2 0.7 collective-permute-start.13

commit v9 on v8

--- a/solution.py
+++ b/solution.py
@@ -14,8 +14,8 @@
 META_USED = 8
 UNROLL = 12
 SELF_UNROLL = 8
-ROW = ("x_hi", "z_hi", "z_lo")
-NEAR = ("x_hi", "z_lo")
+ROW = ("x_hi", "z")
+GROUPS, PLANES = 8, 4
 VMEM = pl.BlockSpec(memory_space=pltpu.VMEM)
 HBM = pl.BlockSpec(memory_space=pltpu.HBM)
 SMEM = pl.BlockSpec(memory_space=pltpu.SMEM)
@@ -43,26 +43,43 @@
     return exchanged(lax.optimization_barrier(copies), axis)
 
 
+def plane(group, place):
+    return (1 + group * PLANES + place) % (GROUPS * PLANES)
+
+
 def between(value, pairs):
-    return lax.ppermute(value, "z_hi", pairs)
+    pairs = [(plane(a, place), plane(b, place)) for a, b in pairs for place in range(PLANES)]
+    return lax.ppermute(value, "z", pairs)
 
 
 def is_group(*groups):
-    here = lax.axis_index("z_hi")
+    depth = GROUPS * PLANES
+    here = (lax.axis_index("z") + depth - 1) % depth // PLANES
     return functools.reduce(jnp.logical_or, [here == group for group in groups])
+
+
+def summed_in_group(value):
+    depth = GROUPS * PLANES
+    members = [
+        [high * depth + plane(group, place) for high in range(2) for place in range(PLANES)]
+        for group in range(GROUPS)
+    ]
+    copies = jnp.broadcast_to(value[None], (2 * PLANES, *value.shape))
+    copies = lax.optimization_barrier(copies)
+    return lax.all_to_all(copies, ROW, 0, 0, axis_index_groups=members).sum(0)
 
 
 def summed_over_z(share):
     arrived = [between(share, [(group, 0)]) for group in (4, 5, 3)]
     joined = share + between(share, [(1, 2), (7, 6)])
     arrived += [between(joined, [(group, 0)]) for group in (6, 2)]
-    return to_all(sum(arrived, joined), NEAR).sum(0)
+    return summed_in_group(sum(arrived, joined))
 
 
 def spread_over_z(total):
     second, first, last = (between(total, [(0, group)]) for group in (2, 1, 7))
     total = jnp.where(
-        is_group(7), last, jnp.where(is_group(1), first, jnp.where(is_group(2), second, total))
+        is_group(2), second, jnp.where(is_group(7), last, jnp.where(is_group(1), first, total))
     )
     total = jnp.where(is_group(3, 6), between(total, [(2, 3), (7, 6)]), total)
     return jnp.where(is_group(4, 5), between(total, [(3, 4), (6, 5)]), total)
@@ -350,7 +367,7 @@
 
 def solution(mesh):
     rows, columns = mesh.devices.shape
-    apart = Mesh(mesh.devices.reshape(2, 8, rows // 16, columns), (*ROW, "col"))
+    apart = Mesh(mesh.devices.reshape(2, rows // 2, columns), (*ROW, "col"))
     both = (*ROW, "col")
     in_specs = (
         P("col", None),

time: 116 us -> 118 us (1.017)
  waiting for transfers between devices: 17 us -> 10.9 us
  starting transfers between devices: 32.2 us -> 37.9 us
  blocking collectives: 50.7 us -> 52.8 us
    all_to_all x0 -> x1, blocking collectives: none -> 12.2 us  [summed_in_group(): return lax.all_to_all(copies, ROW, 0, 0, axis_index_groups=members).sum(0)]
    all_to_all x4 -> x3, blocking collectives: 50.7 us -> 40.6 us  [exchanged(): return lax.all_to_all(parts, axis, 0, 0)]
    ppermute x11, waiting for transfers between devices: 17 us -> 10.8 us  [between(): return lax.ppermute(value, 'z', pairs)]
    ppermute x11, starting transfers between devices: 12.3 us -> 18 us  [between(): return lax.ppermute(value, 'z', pairs)]
where the time goes in v9:
time: 118 us; the launch traced here: 117 us
  blocking collectives  52.8 us (45%)
  starting transfers between devices  37.9 us (32%)
  waiting for transfers between devices  10.9 us (9%)
  Pallas kernels  10.3 us (9%)
  local copies, waits for them, and re-layouts  3.94 us (3%)
    all_to_all x3, blocking collectives, exchanged(): return lax.all_to_all(parts, axis, 0, 0)  40.6 us
    ppermute x3, starting transfers between devices, passed_along(): return lax.ppermute(value, axis, pairs)  19.9 us
    ppermute x11, starting transfers between devices, between(): return lax.ppermute(value, 'z', pairs)  18 us
    all_to_all x1, blocking collectives, summed_in_group(): return lax.all_to_all(copies, ROW, 0, 0, axis_index_groups=members).sum(0)  12.2 us
    ppermute x11, waiting for transfers between devices, between(): return lax.ppermute(value, 'z', pairs)  10.8 us
    unnamed x13, local copies, waits for them, and re-layouts  3.92 us
    pallas_call x1, Pallas kernels, packed_groups(): pl.pallas_call(pack_kernel, out_shape=[jax.ShapeDtypeStruct((rows + META_...  3.39 us
    pallas_call x1, Pallas kernels, own_tiles(): pl.pallas_call(functools.partial(own_kernel, per_group), out_shape=[jax.S...  3.12 us
  transfers between devices with their start and end apart: 14, of which 2 were waited for; matrix products, arithmetic and copies ran while one was open for 0% of the time, Pallas kernels for 3%

profile of v9, /device:TPU:1, one launch (start us, length us, event | category | flops | bytes accessed | tf_op | source)
XLA Modules:
  0.0 117.0 jit_solution(3438540529936850492)
XLA Ops:
  0.6 3.4 %pack.1 = (bf16[784,128]{1,0:T(8,128)(2,1)}, bf16[784,128]{1,0:T(8,128)(2,1)}, bf16[784,128]{1,0:T(8,128)(2,1)}, bf16[784,128]{1,0:T(8,128)(2,1)}) custom-call(s32[2,96]{1,0:T(2,128)} %bitcast.12, s32[1,96]{1,0:T(1,128)} %bitcast.13, bf16[96,4096]{1,0:T(8,128)(2,1)} %bitcast.10), custom_call_target="tpu_custom_call" | custom-call | tf_op jit(solution)/shard_map/pack/pallas_call | solution.py:260
  4.0 16.1 %collective-permute-start = (bf16[784,128]{1,0:T(8,128)(2,1)}, bf16[784,128]{1,0:T(8,128)(2,1)S(1)}, u32[]{:S(2)}, u32[]{:S(2)}) collective-permute-start(bf16[784,128]{1,0:T(8,128)(2,1)} %get-tuple-element.13), channel_id=1, source_target_pairs={{0,15},{1,0},{2,1},{3,2},{4,3},{5,4},{6,5},{7,6},{8,7},{9,8},{10,9... | collective-permute-start | bytes 602120 | tf_op jit(solution)/shard_map/ppermute | solution.py:33
  20.1 1.9 %collective-permute-start.1 = (bf16[784,128]{1,0:T(8,128)(2,1)}, bf16[784,128]{1,0:T(8,128)(2,1)S(1)}, u32[]{:S(2)}, u32[]{:S(2)}) collective-permute-start(bf16[784,128]{1,0:T(8,128)(2,1)} %get-tuple-element.14), channel_id=1, source_target_pairs={{0,14},{1,15},{2,0},{3,1},{4,2},{5,3},{6,4},{7,5},{8,6},{9,7},{10,... | collective-permute-start | bytes 602120 | tf_op jit(solution)/shard_map/ppermute | solution.py:33
  22.0 1.9 %collective-permute-start.2 = (bf16[784,128]{1,0:T(8,128)(2,1)}, bf16[784,128]{1,0:T(8,128)(2,1)S(1)}, u32[]{:S(2)}, u32[]{:S(2)}) collective-permute-start(bf16[784,128]{1,0:T(8,128)(2,1)} %get-tuple-element.15), channel_id=1, source_target_pairs={{0,13},{1,14},{2,15},{3,0},{4,1},{5,2},{6,3},{7,4},{8,5},{9,6},{10... | collective-permute-start | bytes 602120 | tf_op jit(solution)/shard_map/ppermute | solution.py:33
  24.1 1.6 %copy-done = bf16[8192,128]{1,0:T(8,128)(2,1)S(1)} copy-done((bf16[8192,128]{1,0:T(8,128)(2,1)S(1)}, bf16[8192,128]{1,0:T(8,128)(2,1)}, u32[]{:S(2)}) %copy-start) | copy-done | bytes 2097176
  25.7 0.9 copy-done.1
  26.6 0.8 copy-done.2
  27.4 3.1 %own_tiles.1 = (bf16[8192,128]{1,0:T(8,128)(2,1)S(1)}, f32[1024,384]{1,0:T(8,128)S(1)}) custom-call(s32[2]{0:T(128)S(1)} %pad_add_fusion.self_ref, bf16[8192,128]{1,0:T(8,128)(2,1)S(1)} %copy-done, s32[64,128]{1,0:T(8,128)S(1)} %bitcast.9, bf16[784,128]{1,0:T(8,128)(2,1)S(1)} %copy-done.1), custom_call_target="tpu_custom_call" | custom-call | flops 201326592 | bytes 6291456 | tf_op jit(solution)/shard_map/own_tiles/pallas_call | solution.py:286
  30.6 2.8 %moved_tiles.1 = bf16[16,80,256]{2,1,0:T(8,128)(2,1)S(1)} custom-call(bf16[8192,128]{1,0:T(8,128)(2,1)S(1)} %get-tuple-element.11.panel_ref, f32[1024,384]{1,0:T(8,128)S(1)} %get-tuple-element.12.before_ref, bf16[784,128]{1,0:T(8,128)(2,1)S(1)} %collective-permute-done.refs_0_, bf16[784,128]{1,0:T(8,128)(2,1)S(1)} %collective-permute-done.1.refs_1_, ...), custom_call_target="tpu_custom_call" | custom-call | tf_op jit(solution)/shard_map/moved_tiles/pallas_call | solution.py:306
  33.4 18.4 %all_to_all.20.arrived_ref = bf16[16,80,256]{2,1,0:T(8,128)(2,1)S(1)} all-to-all(bf16[16,80,256]{2,1,0:T(8,128)(2,1)S(1)} %moved_tiles.1), channel_id=1, replica_groups=mesh['x_hi'=2,'z'=32,'col'=16] {'col'}, dimensions={0} | all-to-all | bytes 1310720 | tf_op jit(solution)/shard_map/all_to_all | solution.py:37
  51.9 1.0 layer.1
  52.9 8.9 %all_to_all.21 = f32[16,8,128]{2,1,0:T(8,128)S(1)} all-to-all(f32[16,8,128]{2,1,0:T(8,128)S(1)} %bitcast.8), channel_id=1, replica_groups=mesh['x_hi'=2,'z'=32,'col'=16] {'col'}, dimensions={0} | all-to-all | bytes 131072 | tf_op jit(solution)/shard_map/all_to_all | solution.py:37
  61.8 10.2 %collective-permute-start.3 = (f32[8,128]{1,0:T(8,128)S(1)}, f32[8,128]{1,0:T(8,128)S(1)}, u32[]{:S(2)}, u32[]{:S(2)}) collective-permute-start(f32[8,128]{1,0:T(8,128)S(1)} %reduce_sum.18), channel_id=1, source_target_pairs={{80,144},{96,160},{112,176},{128,192},{464,400},{480,416},{496,432... | collective-permute-start | bytes 12296 | tf_op jit(solution)/shard_map/ppermute | solution.py:52
  72.0 0.7 collective-permute-start.4
  72.7 0.7 collective-permute-start.5
  73.3 0.7 collective-permute-start.6
  74.0 0.7 collective-permute-start.7
  74.7 0.7 collective-permute-start.8
  75.5 12.2 %all_to_all.22 = f32[8,8,128]{2,1,0:T(8,128)S(1)} all-to-all(f32[8,8,128]{2,1,0:T(8,128)S(1)} %broadcast_in_dim.4), channel_id=1, replica_groups={{16,32,48,64,528,544,560,576},{80,96,112,128,592,608,624,640},{144,160,..., dimensions={0} | all-to-all | bytes 65536 | tf_op jit(solution)/shard_map/all_to_all | solution.py:69
  87.7 1.3 %collective-permute-start.10 = (f32[8,128]{1,0:T(8,128)S(1)}, f32[8,128]{1,0:T(8,128)S(1)}, u32[]{:S(2)}, u32[]{:S(2)}) collective-permute-start(f32[8,128]{1,0:T(8,128)S(1)} %reduce_sum.19), channel_id=1, source_target_pairs={{16,464},{32,480},{48,496},{64,0},{17,465},{33,481},{49,497},{65,1... | collective-permute-start | bytes 12296 | tf_op jit(solution)/shard_map/ppermute | solution.py:52
  90.3 10.1 %collective-permute-done.10 = f32[8,128]{1,0:T(8,128)S(1)} collective-permute-done((f32[8,128]{1,0:T(8,128)S(1)}, f32[8,128]{1,0:T(8,128)S(1)}, u32[]{:S(2)}, u32[]{:S(2)}) %collective-permute-start.10) | collective-permute-done | bytes 4128 | tf_op jit(solution)/shard_map/ppermute | solution.py:52
  100.4 1.3 %collective-permute-start.12 = (f32[8,128]{1,0:T(8,128)S(1)}, f32[8,128]{1,0:T(8,128)S(1)}, u32[]{:S(2)}, u32[]{:S(2)}) collective-permute-start(f32[8,128]{1,0:T(8,128)S(1)} %select_select_fusion), channel_id=1, source_target_pairs={{144,208},{160,224},{176,240},{192,256},{464,400},{480,416},{496,4... | collective-permute-start | bytes 12296 | tf_op jit(solution)/shard_map/ppermute | solution.py:52
  101.7 0.7 collective-permute-done.12
  103.2 13.2 %all_to_all.23 = f32[16,8,128]{2,1,0:T(8,128)S(1)} all-to-all(f32[16,8,128]{2,1,0:T(8,128)S(1)} %broadcast_in_dim.5), channel_id=1, replica_groups=mesh['x_hi'=2,'z'=32,'col'=16] {'col'}, dimensions={0} | all-to-all | bytes 131072 | tf_op jit(solution)/shard_map/all_to_all | solution.py:37
  (35 shorter events, 2.8 us)
Async XLA Ops:
  4.0 26.5 %collective-permute-start = (bf16[784,128]{1,0:T(8,128)(2,1)}, bf16[784,128]{1,0:T(8,128)(2,1)S(1)}, u32[]{:S(2)}, u32[]{:S(2)}) collective-permute-start(bf16[784,128]{1,0:T(8,128)(2,1)} %get-tuple-element.13), channel_id=1, source_target_pairs={{0,15},{1,0},{2,1},{3,2},{4,3},{5,4},{6,5},{7,6},{8,7},{9,8},{10,9... | collective-permute-start | bytes 602120 | tf_op jit(solution)/shard_map/ppermute | solution.py:33
  20.1 10.4 %collective-permute-start.1 = (bf16[784,128]{1,0:T(8,128)(2,1)}, bf16[784,128]{1,0:T(8,128)(2,1)S(1)}, u32[]{:S(2)}, u32[]{:S(2)}) collective-permute-start(bf16[784,128]{1,0:T(8,128)(2,1)} %get-tuple-element.14), channel_id=1, source_target_pairs={{0,14},{1,15},{2,0},{3,1},{4,2},{5,3},{6,4},{7,5},{8,6},{9,7},{10,... | collective-permute-start | bytes 602120 | tf_op jit(solution)/shard_map/ppermute | solution.py:33
  22.0 8.5 %collective-permute-start.2 = (bf16[784,128]{1,0:T(8,128)(2,1)}, bf16[784,128]{1,0:T(8,128)(2,1)S(1)}, u32[]{:S(2)}, u32[]{:S(2)}) collective-permute-start(bf16[784,128]{1,0:T(8,128)(2,1)} %get-tuple-element.15), channel_id=1, source_target_pairs={{0,13},{1,14},{2,15},{3,0},{4,1},{5,2},{6,3},{7,4},{8,5},{9,6},{10... | collective-permute-start | bytes 602120 | tf_op jit(solution)/shard_map/ppermute | solution.py:33
  24.1 1.6 %copy-start = (bf16[8192,128]{1,0:T(8,128)(2,1)S(1)}, bf16[8192,128]{1,0:T(8,128)(2,1)}, u32[]{:S(2)}) copy-start(bf16[8192,128]{1,0:T(8,128)(2,1)} %features_ref.1) | copy-start | bytes 6291460
  25.7 0.9 copy-start.1
  26.6 0.8 copy-start.2
  30.5 21.3 %copy-start.3 = (bf16[128,128]{1,0:T(8,128)(2,1)S(1)}, bf16[128,128]{1,0:T(8,128)(2,1)}, u32[]{:S(2)}) copy-start(bf16[128,128]{1,0:T(8,128)(2,1)} %weight_ref.1) | copy-start | bytes 98308
  30.5 21.3 %copy-start.4 = (bf16[128,128]{1,0:T(8,128)(2,1)S(1)}, bf16[128,128]{1,0:T(8,128)(2,1)}, u32[]{:S(2)}) copy-start(bf16[128,128]{1,0:T(8,128)(2,1)} %cotangent_ref.1) | copy-start | bytes 98308
  30.5 21.3 %copy-start.5 = (s32[1,128]{1,0:T(1,128)S(1)}, s32[1,128]{1,0:T(1,128)}, u32[]{:S(2)}) copy-start(s32[1,128]{1,0:T(1,128)} %order_ref.1) | copy-start | bytes 1540
  61.8 12.2 %collective-permute-start.3 = (f32[8,128]{1,0:T(8,128)S(1)}, f32[8,128]{1,0:T(8,128)S(1)}, u32[]{:S(2)}, u32[]{:S(2)}) collective-permute-start(f32[8,128]{1,0:T(8,128)S(1)} %reduce_sum.18), channel_id=1, source_target_pairs={{80,144},{96,160},{112,176},{128,192},{464,400},{480,416},{496,432... | collective-permute-start | bytes 12296 | tf_op jit(solution)/shard_map/ppermute | solution.py:52
  72.0 3.4 %collective-permute-start.4 = (f32[8,128]{1,0:T(8,128)S(1)}, f32[8,128]{1,0:T(8,128)S(1)}, u32[]{:S(2)}, u32[]{:S(2)}) collective-permute-start(f32[8,128]{1,0:T(8,128)S(1)} %reduce_sum.18), channel_id=1, source_target_pairs={{272,16},{288,32},{304,48},{320,64},{273,17},{289,33},{305,49},{32... | collective-permute-start | bytes 12296 | tf_op jit(solution)/shard_map/ppermute | solution.py:52
  72.7 2.7 %collective-permute-start.5 = (f32[8,128]{1,0:T(8,128)S(1)}, f32[8,128]{1,0:T(8,128)S(1)}, u32[]{:S(2)}, u32[]{:S(2)}) collective-permute-start(f32[8,128]{1,0:T(8,128)S(1)} %reduce_sum.18), channel_id=1, source_target_pairs={{336,16},{352,32},{368,48},{384,64},{337,17},{353,33},{369,49},{38... | collective-permute-start | bytes 12296 | tf_op jit(solution)/shard_map/ppermute | solution.py:52
  73.3 2.1 %collective-permute-start.6 = (f32[8,128]{1,0:T(8,128)S(1)}, f32[8,128]{1,0:T(8,128)S(1)}, u32[]{:S(2)}, u32[]{:S(2)}) collective-permute-start(f32[8,128]{1,0:T(8,128)S(1)} %reduce_sum.18), channel_id=1, source_target_pairs={{208,16},{224,32},{240,48},{256,64},{209,17},{225,33},{241,49},{25... | collective-permute-start | bytes 12296 | tf_op jit(solution)/shard_map/ppermute | solution.py:52
  74.0 1.4 %collective-permute-start.7 = (f32[8,128]{1,0:T(8,128)S(1)}, f32[8,128]{1,0:T(8,128)S(1)}, u32[]{:S(2)}, u32[]{:S(2)}) collective-permute-start(f32[8,128]{1,0:T(8,128)S(1)} %add.46), channel_id=1, source_target_pairs={{400,16},{416,32},{432,48},{448,64},{401,17},{417,33},{433,49},{44... | collective-permute-start | bytes 12296 | tf_op jit(solution)/shard_map/ppermute | solution.py:52
  74.7 0.7 collective-permute-start.8
  87.7 12.8 %collective-permute-start.10 = (f32[8,128]{1,0:T(8,128)S(1)}, f32[8,128]{1,0:T(8,128)S(1)}, u32[]{:S(2)}, u32[]{:S(2)}) collective-permute-start(f32[8,128]{1,0:T(8,128)S(1)} %reduce_sum.19), channel_id=1, source_target_pairs={{16,464},{32,480},{48,496},{64,0},{17,465},{33,481},{49,497},{65,1... | collective-permute-start | bytes 12296 | tf_op jit(solution)/shard_map/ppermute | solution.py:52
  89.0 11.5 %collective-permute-start.11 = (f32[8,128]{1,0:T(8,128)S(1)}, f32[8,128]{1,0:T(8,128)S(1)}, u32[]{:S(2)}, u32[]{:S(2)}) collective-permute-start(f32[8,128]{1,0:T(8,128)S(1)} %reduce_sum.19), channel_id=1, source_target_pairs={{16,80},{32,96},{48,112},{64,128},{17,81},{33,97},{49,113},{65,129... | collective-permute-start | bytes 12296 | tf_op jit(solution)/shard_map/ppermute | solution.py:52
  89.6 10.8 %collective-permute-start.9 = (f32[8,128]{1,0:T(8,128)S(1)}, f32[8,128]{1,0:T(8,128)S(1)}, u32[]{:S(2)}, u32[]{:S(2)}) collective-permute-start(f32[8,128]{1,0:T(8,128)S(1)} %reduce_sum.19), channel_id=1, source_target_pairs={{16,144},{32,160},{48,176},{64,192},{17,145},{33,161},{49,177},{65... | collective-permute-start | bytes 12296 | tf_op jit(solution)/shard_map/ppermute | solution.py:52
  100.4 2.0 %collective-permute-start.12 = (f32[8,128]{1,0:T(8,128)S(1)}, f32[8,128]{1,0:T(8,128)S(1)}, u32[]{:S(2)}, u32[]{:S(2)}) collective-permute-start(f32[8,128]{1,0:T(8,128)S(1)} %select_select_fusion), channel_id=1, source_target_pairs={{144,208},{160,224},{176,240},{192,256},{464,400},{480,416},{496,4... | collective-permute-start | bytes 12296 | tf_op jit(solution)/shard_map/ppermute | solution.py:52
  102.5 0.7 collective-permute-start.13

commit v10 on v8

--- a/solution.py
+++ b/solution.py
@@ -60,12 +60,11 @@
 
 
 def spread_over_z(total):
-    second, first, last = (between(total, [(0, group)]) for group in (2, 1, 7))
-    total = jnp.where(
-        is_group(7), last, jnp.where(is_group(1), first, jnp.where(is_group(2), second, total))
-    )
-    total = jnp.where(is_group(3, 6), between(total, [(2, 3), (7, 6)]), total)
-    return jnp.where(is_group(4, 5), between(total, [(3, 4), (6, 5)]), total)
+    first, last = between(total, [(0, 1)]), between(total, [(0, 7)])
+    total = jnp.where(is_group(1), first, jnp.where(is_group(7), last, total))
+    far, near = between(total, [(1, 3), (7, 5)]), between(total, [(1, 2), (7, 6)])
+    total = jnp.where(is_group(3, 5), far, jnp.where(is_group(2, 6), near, total))
+    return jnp.where(is_group(4), between(total, [(3, 4)]), total)
 
 
 def two_parts(value):

time: 116 us -> 116 us (level)
  no operation moved by 1% of the time
where the time goes in v10:
time: 116 us; the launch traced here: 115 us
  blocking collectives  50.9 us (44%)
  starting transfers between devices  31.6 us (27%)
  waiting for transfers between devices  17 us (15%)
  Pallas kernels  10.1 us (9%)
  local copies, waits for them, and re-layouts  3.94 us (3%)
    all_to_all x4, blocking collectives, exchanged(): return lax.all_to_all(parts, axis, 0, 0)  50.9 us
    ppermute x3, starting transfers between devices, passed_along(): return lax.ppermute(value, axis, pairs)  19.9 us
    ppermute x11, waiting for transfers between devices, between(): return lax.ppermute(value, 'z_hi', pairs)  17 us
    ppermute x11, starting transfers between devices, between(): return lax.ppermute(value, 'z_hi', pairs)  11.7 us
    unnamed x13, local copies, waits for them, and re-layouts  3.92 us
    pallas_call x1, Pallas kernels, packed_groups(): pl.pallas_call(pack_kernel, out_shape=[jax.ShapeDtypeStruct((rows + META_...  3.39 us
    pallas_call x1, Pallas kernels, own_tiles(): pl.pallas_call(functools.partial(own_kernel, per_group), out_shape=[jax.S...  2.88 us
    pallas_call x1, Pallas kernels, moved_tiles(): pl.pallas_call(functools.partial(moved_kernel, per_group), out_shape=jax....  2.85 us
  transfers between devices with their start and end apart: 14, of which 2 were waited for; matrix products, arithmetic and copies ran while one was open for 0% of the time, Pallas kernels for 3%

profile of v10, /device:TPU:1, one launch (start us, length us, event | category | flops | bytes accessed | tf_op | source)
XLA Modules:
  0.0 114.6 jit_solution(8778158577249056179)
XLA Ops:
  0.6 3.4 %pack.1 = (bf16[784,128]{1,0:T(8,128)(2,1)}, bf16[784,128]{1,0:T(8,128)(2,1)}, bf16[784,128]{1,0:T(8,128)(2,1)}, bf16[784,128]{1,0:T(8,128)(2,1)}) custom-call(s32[2,96]{1,0:T(2,128)} %bitcast.12, s32[1,96]{1,0:T(1,128)} %bitcast.13, bf16[96,4096]{1,0:T(8,128)(2,1)} %bitcast.10), custom_call_target="tpu_custom_call" | custom-call | tf_op jit(solution)/shard_map/pack/pallas_call | solution.py:242
  4.0 16.1 %collective-permute-start = (bf16[784,128]{1,0:T(8,128)(2,1)}, bf16[784,128]{1,0:T(8,128)(2,1)S(1)}, u32[]{:S(2)}, u32[]{:S(2)}) collective-permute-start(bf16[784,128]{1,0:T(8,128)(2,1)} %get-tuple-element.13), channel_id=1, source_target_pairs={{0,15},{1,0},{2,1},{3,2},{4,3},{5,4},{6,5},{7,6},{8,7},{9,8},{10,9... | collective-permute-start | bytes 602120 | tf_op jit(solution)/shard_map/ppermute | solution.py:33
  20.1 1.9 %collective-permute-start.1 = (bf16[784,128]{1,0:T(8,128)(2,1)}, bf16[784,128]{1,0:T(8,128)(2,1)S(1)}, u32[]{:S(2)}, u32[]{:S(2)}) collective-permute-start(bf16[784,128]{1,0:T(8,128)(2,1)} %get-tuple-element.14), channel_id=1, source_target_pairs={{0,14},{1,15},{2,0},{3,1},{4,2},{5,3},{6,4},{7,5},{8,6},{9,7},{10,... | collective-permute-start | bytes 602120 | tf_op jit(solution)/shard_map/ppermute | solution.py:33
  22.0 1.9 %collective-permute-start.2 = (bf16[784,128]{1,0:T(8,128)(2,1)}, bf16[784,128]{1,0:T(8,128)(2,1)S(1)}, u32[]{:S(2)}, u32[]{:S(2)}) collective-permute-start(bf16[784,128]{1,0:T(8,128)(2,1)} %get-tuple-element.15), channel_id=1, source_target_pairs={{0,13},{1,14},{2,15},{3,0},{4,1},{5,2},{6,3},{7,4},{8,5},{9,6},{10... | collective-permute-start | bytes 602120 | tf_op jit(solution)/shard_map/ppermute | solution.py:33
  24.1 1.6 %copy-done = bf16[8192,128]{1,0:T(8,128)(2,1)S(1)} copy-done((bf16[8192,128]{1,0:T(8,128)(2,1)S(1)}, bf16[8192,128]{1,0:T(8,128)(2,1)}, u32[]{:S(2)}) %copy-start) | copy-done | bytes 2097176
  25.7 0.9 copy-done.1
  26.6 0.8 copy-done.2
  27.4 2.9 %own_tiles.1 = (bf16[8192,128]{1,0:T(8,128)(2,1)S(1)}, f32[1024,384]{1,0:T(8,128)S(1)}) custom-call(s32[2]{0:T(128)S(1)} %pad_add_fusion.self_ref, bf16[8192,128]{1,0:T(8,128)(2,1)S(1)} %copy-done, s32[64,128]{1,0:T(8,128)S(1)} %bitcast.9, bf16[784,128]{1,0:T(8,128)(2,1)S(1)} %copy-done.1), custom_call_target="tpu_custom_call" | custom-call | flops 201326592 | bytes 6291456 | tf_op jit(solution)/shard_map/own_tiles/pallas_call | solution.py:268
  30.3 2.8 %moved_tiles.1 = bf16[16,80,256]{2,1,0:T(8,128)(2,1)S(1)} custom-call(bf16[8192,128]{1,0:T(8,128)(2,1)S(1)} %get-tuple-element.11.panel_ref, f32[1024,384]{1,0:T(8,128)S(1)} %get-tuple-element.12.before_ref, bf16[784,128]{1,0:T(8,128)(2,1)S(1)} %collective-permute-done.refs_0_, bf16[784,128]{1,0:T(8,128)(2,1)S(1)} %collective-permute-done.1.refs_1_, ...), custom_call_target="tpu_custom_call" | custom-call | tf_op jit(solution)/shard_map/moved_tiles/pallas_call | solution.py:288
  33.2 18.7 %all_to_all.20.arrived_ref = bf16[16,80,256]{2,1,0:T(8,128)(2,1)S(1)} all-to-all(bf16[16,80,256]{2,1,0:T(8,128)(2,1)S(1)} %moved_tiles.1), channel_id=1, replica_groups=mesh['x_hi'=2,'z_hi'=8,'z_lo'=4,'col'=16] {'col'}, dimensions={0} | all-to-all | bytes 1310720 | tf_op jit(solution)/shard_map/all_to_all | solution.py:37
  51.9 1.0 layer.1
  52.9 8.9 %all_to_all.21 = f32[16,8,128]{2,1,0:T(8,128)S(1)} all-to-all(f32[16,8,128]{2,1,0:T(8,128)S(1)} %bitcast.8), channel_id=1, replica_groups=mesh['x_hi'=2,'z_hi'=8,'z_lo'=4,'col'=16] {'col'}, dimensions={0} | all-to-all | bytes 131072 | tf_op jit(solution)/shard_map/all_to_all | solution.py:37
  62.5 1.3 %collective-permute-start.4 = (f32[8,128]{1,0:T(8,128)S(1)}, f32[8,128]{1,0:T(8,128)S(1)}, u32[]{:S(2)}, u32[]{:S(2)}) collective-permute-start(f32[8,128]{1,0:T(8,128)S(1)} %reduce_sum.18), channel_id=1, source_target_pairs={{256,0},{257,1},{258,2},{259,3},{260,4},{261,5},{262,6},{263,7},{2... | collective-permute-start | bytes 12296 | tf_op jit(solution)/shard_map/ppermute | solution.py:47
  63.8 1.3 %collective-permute-start.5 = (f32[8,128]{1,0:T(8,128)S(1)}, f32[8,128]{1,0:T(8,128)S(1)}, u32[]{:S(2)}, u32[]{:S(2)}) collective-permute-start(f32[8,128]{1,0:T(8,128)S(1)} %reduce_sum.18), channel_id=1, source_target_pairs={{320,0},{321,1},{322,2},{323,3},{324,4},{325,5},{326,6},{327,7},{3... | collective-permute-start | bytes 12296 | tf_op jit(solution)/shard_map/ppermute | solution.py:47
  65.1 1.3 %collective-permute-start.6 = (f32[8,128]{1,0:T(8,128)S(1)}, f32[8,128]{1,0:T(8,128)S(1)}, u32[]{:S(2)}, u32[]{:S(2)}) collective-permute-start(f32[8,128]{1,0:T(8,128)S(1)} %reduce_sum.18), channel_id=1, source_target_pairs={{192,0},{193,1},{194,2},{195,3},{196,4},{197,5},{198,6},{199,7},{2... | collective-permute-start | bytes 12296 | tf_op jit(solution)/shard_map/ppermute | solution.py:47
  66.4 1.3 %collective-permute-start.7 = (f32[8,128]{1,0:T(8,128)S(1)}, f32[8,128]{1,0:T(8,128)S(1)}, u32[]{:S(2)}, u32[]{:S(2)}) collective-permute-start(f32[8,128]{1,0:T(8,128)S(1)} %add.33), channel_id=1, source_target_pairs={{384,0},{385,1},{386,2},{387,3},{388,4},{389,5},{390,6},{391,7},{3... | collective-permute-start | bytes 12296 | tf_op jit(solution)/shard_map/ppermute | solution.py:47
  67.7 1.3 %collective-permute-start.8 = (f32[8,128]{1,0:T(8,128)S(1)}, f32[8,128]{1,0:T(8,128)S(1)}, u32[]{:S(2)}, u32[]{:S(2)}) collective-permute-start(f32[8,128]{1,0:T(8,128)S(1)} %add.33), channel_id=1, source_target_pairs={{128,0},{129,1},{130,2},{131,3},{132,4},{133,5},{134,6},{135,7},{1... | collective-permute-start | bytes 12296 | tf_op jit(solution)/shard_map/ppermute | solution.py:47
  69.0 16.3 %collective-permute-done.4 = f32[8,128]{1,0:T(8,128)S(1)} collective-permute-done((f32[8,128]{1,0:T(8,128)S(1)}, f32[8,128]{1,0:T(8,128)S(1)}, u32[]{:S(2)}, u32[]{:S(2)}) %collective-permute-start.4) | collective-permute-done | bytes 4128 | tf_op jit(solution)/shard_map/ppermute | solution.py:47
  85.3 10.5 %all_to_all.22 = f32[8,8,128]{2,1,0:T(8,128)S(1)} all-to-all(f32[8,8,128]{2,1,0:T(8,128)S(1)} %broadcast_in_dim.4), channel_id=1, replica_groups=mesh['x_hi'=2,'z_hi'=8,'z_lo'=4,'col'=16] {'x_hi','z_lo'}, dimensions={0} | all-to-all | bytes 65536 | tf_op jit(solution)/shard_map/all_to_all | solution.py:37
  95.9 1.3 %collective-permute-start.10 = (f32[8,128]{1,0:T(8,128)S(1)}, f32[8,128]{1,0:T(8,128)S(1)}, u32[]{:S(2)}, u32[]{:S(2)}) collective-permute-start(f32[8,128]{1,0:T(8,128)S(1)} %reduce_sum.19), channel_id=1, source_target_pairs={{0,448},{1,449},{2,450},{3,451},{4,452},{5,453},{6,454},{7,455},{8... | collective-permute-start | bytes 12296 | tf_op jit(solution)/shard_map/ppermute | solution.py:47
  97.1 1.3 %collective-permute-start.9 = (f32[8,128]{1,0:T(8,128)S(1)}, f32[8,128]{1,0:T(8,128)S(1)}, u32[]{:S(2)}, u32[]{:S(2)}) collective-permute-start(f32[8,128]{1,0:T(8,128)S(1)} %reduce_sum.19), channel_id=1, source_target_pairs={{0,64},{1,65},{2,66},{3,67},{4,68},{5,69},{6,70},{7,71},{8,72},{9,... | collective-permute-start | bytes 12296 | tf_op jit(solution)/shard_map/ppermute | solution.py:47
  98.5 0.7 collective-permute-done.9
  99.8 0.7 collective-permute-start.12
  101.3 12.7 %all_to_all.23 = f32[16,8,128]{2,1,0:T(8,128)S(1)} all-to-all(f32[16,8,128]{2,1,0:T(8,128)S(1)} %broadcast_in_dim.5), channel_id=1, replica_groups=mesh['x_hi'=2,'z_hi'=8,'z_lo'=4,'col'=16] {'col'}, dimensions={0} | all-to-all | bytes 131072 | tf_op jit(solution)/shard_map/all_to_all | solution.py:37
  (35 shorter events, 2.8 us)
Async XLA Ops:
  4.0 26.2 %collective-permute-start = (bf16[784,128]{1,0:T(8,128)(2,1)}, bf16[784,128]{1,0:T(8,128)(2,1)S(1)}, u32[]{:S(2)}, u32[]{:S(2)}) collective-permute-start(bf16[784,128]{1,0:T(8,128)(2,1)} %get-tuple-element.13), channel_id=1, source_target_pairs={{0,15},{1,0},{2,1},{3,2},{4,3},{5,4},{6,5},{7,6},{8,7},{9,8},{10,9... | collective-permute-start | bytes 602120 | tf_op jit(solution)/shard_map/ppermute | solution.py:33
  20.1 10.2 %collective-permute-start.1 = (bf16[784,128]{1,0:T(8,128)(2,1)}, bf16[784,128]{1,0:T(8,128)(2,1)S(1)}, u32[]{:S(2)}, u32[]{:S(2)}) collective-permute-start(bf16[784,128]{1,0:T(8,128)(2,1)} %get-tuple-element.14), channel_id=1, source_target_pairs={{0,14},{1,15},{2,0},{3,1},{4,2},{5,3},{6,4},{7,5},{8,6},{9,7},{10,... | collective-permute-start | bytes 602120 | tf_op jit(solution)/shard_map/ppermute | solution.py:33
  22.0 8.2 %collective-permute-start.2 = (bf16[784,128]{1,0:T(8,128)(2,1)}, bf16[784,128]{1,0:T(8,128)(2,1)S(1)}, u32[]{:S(2)}, u32[]{:S(2)}) collective-permute-start(bf16[784,128]{1,0:T(8,128)(2,1)} %get-tuple-element.15), channel_id=1, source_target_pairs={{0,13},{1,14},{2,15},{3,0},{4,1},{5,2},{6,3},{7,4},{8,5},{9,6},{10... | collective-permute-start | bytes 602120 | tf_op jit(solution)/shard_map/ppermute | solution.py:33
  24.1 1.6 %copy-start = (bf16[8192,128]{1,0:T(8,128)(2,1)S(1)}, bf16[8192,128]{1,0:T(8,128)(2,1)}, u32[]{:S(2)}) copy-start(bf16[8192,128]{1,0:T(8,128)(2,1)} %features_ref.1) | copy-start | bytes 6291460
  25.7 0.9 copy-start.1
  26.6 0.8 copy-start.2
  30.3 21.6 %copy-start.3 = (bf16[128,128]{1,0:T(8,128)(2,1)S(1)}, bf16[128,128]{1,0:T(8,128)(2,1)}, u32[]{:S(2)}) copy-start(bf16[128,128]{1,0:T(8,128)(2,1)} %weight_ref.1) | copy-start | bytes 98308
  30.3 21.6 %copy-start.4 = (bf16[128,128]{1,0:T(8,128)(2,1)S(1)}, bf16[128,128]{1,0:T(8,128)(2,1)}, u32[]{:S(2)}) copy-start(bf16[128,128]{1,0:T(8,128)(2,1)} %cotangent_ref.1) | copy-start | bytes 98308
  30.3 21.6 %copy-start.5 = (s32[1,128]{1,0:T(1,128)S(1)}, s32[1,128]{1,0:T(1,128)}, u32[]{:S(2)}) copy-start(s32[1,128]{1,0:T(1,128)} %order_ref.1) | copy-start | bytes 1540
  61.8 4.6 %collective-permute-start.3 = (f32[8,128]{1,0:T(8,128)S(1)}, f32[8,128]{1,0:T(8,128)S(1)}, u32[]{:S(2)}, u32[]{:S(2)}) collective-permute-start(f32[8,128]{1,0:T(8,128)S(1)} %reduce_sum.18), channel_id=1, source_target_pairs={{64,128},{448,384},{65,129},{449,385},{66,130},{450,386},{67,131},... | collective-permute-start | bytes 12296 | tf_op jit(solution)/shard_map/ppermute | solution.py:47
  62.5 22.8 %collective-permute-start.4 = (f32[8,128]{1,0:T(8,128)S(1)}, f32[8,128]{1,0:T(8,128)S(1)}, u32[]{:S(2)}, u32[]{:S(2)}) collective-permute-start(f32[8,128]{1,0:T(8,128)S(1)} %reduce_sum.18), channel_id=1, source_target_pairs={{256,0},{257,1},{258,2},{259,3},{260,4},{261,5},{262,6},{263,7},{2... | collective-permute-start | bytes 12296 | tf_op jit(solution)/shard_map/ppermute | solution.py:47
  63.8 21.5 %collective-permute-start.5 = (f32[8,128]{1,0:T(8,128)S(1)}, f32[8,128]{1,0:T(8,128)S(1)}, u32[]{:S(2)}, u32[]{:S(2)}) collective-permute-start(f32[8,128]{1,0:T(8,128)S(1)} %reduce_sum.18), channel_id=1, source_target_pairs={{320,0},{321,1},{322,2},{323,3},{324,4},{325,5},{326,6},{327,7},{3... | collective-permute-start | bytes 12296 | tf_op jit(solution)/shard_map/ppermute | solution.py:47
  65.1 20.2 %collective-permute-start.6 = (f32[8,128]{1,0:T(8,128)S(1)}, f32[8,128]{1,0:T(8,128)S(1)}, u32[]{:S(2)}, u32[]{:S(2)}) collective-permute-start(f32[8,128]{1,0:T(8,128)S(1)} %reduce_sum.18), channel_id=1, source_target_pairs={{192,0},{193,1},{194,2},{195,3},{196,4},{197,5},{198,6},{199,7},{2... | collective-permute-start | bytes 12296 | tf_op jit(solution)/shard_map/ppermute | solution.py:47
  66.4 18.9 %collective-permute-start.7 = (f32[8,128]{1,0:T(8,128)S(1)}, f32[8,128]{1,0:T(8,128)S(1)}, u32[]{:S(2)}, u32[]{:S(2)}) collective-permute-start(f32[8,128]{1,0:T(8,128)S(1)} %add.33), channel_id=1, source_target_pairs={{384,0},{385,1},{386,2},{387,3},{388,4},{389,5},{390,6},{391,7},{3... | collective-permute-start | bytes 12296 | tf_op jit(solution)/shard_map/ppermute | solution.py:47
  67.7 17.6 %collective-permute-start.8 = (f32[8,128]{1,0:T(8,128)S(1)}, f32[8,128]{1,0:T(8,128)S(1)}, u32[]{:S(2)}, u32[]{:S(2)}) collective-permute-start(f32[8,128]{1,0:T(8,128)S(1)} %add.33), channel_id=1, source_target_pairs={{128,0},{129,1},{130,2},{131,3},{132,4},{133,5},{134,6},{135,7},{1... | collective-permute-start | bytes 12296 | tf_op jit(solution)/shard_map/ppermute | solution.py:47
  95.9 2.6 %collective-permute-start.10 = (f32[8,128]{1,0:T(8,128)S(1)}, f32[8,128]{1,0:T(8,128)S(1)}, u32[]{:S(2)}, u32[]{:S(2)}) collective-permute-start(f32[8,128]{1,0:T(8,128)S(1)} %reduce_sum.19), channel_id=1, source_target_pairs={{0,448},{1,449},{2,450},{3,451},{4,452},{5,453},{6,454},{7,455},{8... | collective-permute-start | bytes 12296 | tf_op jit(solution)/shard_map/ppermute | solution.py:47
  97.1 2.0 %collective-permute-start.9 = (f32[8,128]{1,0:T(8,128)S(1)}, f32[8,128]{1,0:T(8,128)S(1)}, u32[]{:S(2)}, u32[]{:S(2)}) collective-permute-start(f32[8,128]{1,0:T(8,128)S(1)} %reduce_sum.19), channel_id=1, source_target_pairs={{0,64},{1,65},{2,66},{3,67},{4,68},{5,69},{6,70},{7,71},{8,72},{9,... | collective-permute-start | bytes 12296 | tf_op jit(solution)/shard_map/ppermute | solution.py:47
  99.2 1.3 %collective-permute-start.11 = (f32[8,128]{1,0:T(8,128)S(1)}, f32[8,128]{1,0:T(8,128)S(1)}, u32[]{:S(2)}, u32[]{:S(2)}) collective-permute-start(f32[8,128]{1,0:T(8,128)S(1)} %select_select_fusion.1), channel_id=1, source_target_pairs={{64,192},{448,320},{65,193},{449,321},{66,194},{450,322},{67,195},... | collective-permute-start | bytes 12296 | tf_op jit(solution)/shard_map/ppermute | solution.py:47
  99.8 0.7 collective-permute-start.12
  100.6 0.7 collective-permute-start.13
